TPU v7x, 32 devices: a whole 2x2x4 slice. The times are simulated.
32 devices in a mesh: rows: 8 (over z, y), cols: 4 (over x, core).
Axes of the slice: x: 2, y: 2, z: 4, core: 2. Of those that a mesh axis runs over, the one named last changes fastest.
Arguments:
- patches: bfloat16 [192, 96, 1280], P('rows', 'cols'), may hold values from -6 to 6
- conv_taps: float32 [3, 3, 1280], replicated, may hold values from -1.5 to 1.5
- conv_bias: float32 [1280], replicated, may hold values from -3 to 3
- norm_gain: float32 [1280], replicated, may hold values from 0.1 to 1.9
- norm_bias: float32 [1280], replicated, may hold values from -3 to 3
- qkv_weight: bfloat16 [3, 1280, 1280], P(None, None, 'cols'), may hold values from -0.15625 to 0.15625
- qkv_bias: bfloat16 [3, 1280], P(None, 'cols'), may hold values from -3 to 3
Outputs:
- qkv_heads: bfloat16 [3, 16, 192, 7680], P(None, 'cols', 'rows')
All inputs are finite; a program needn't handle non-finite values.
Results may differ from a plain program's by a relative error of at most 0.0047.
Values may be sent and summed in bfloat16 or wider, within the bound.
No kernel may reach another device: no remote copies, remote signals or barrier semaphores. Data moves between devices by JAX's collectives and lax.ppermute only.
A program may use at most 128 MiB of HBM per device.

v0:
```python
import jax
import jax.numpy as jnp
from jax import lax
from jax.sharding import PartitionSpec as P

HD = 80


def with_halo(cells, sides, width):
    for axis, dim in sides:
        count = lax.axis_size(axis)
        ends = count - 1
        head = lax.slice_in_dim(cells, 0, width, axis=dim)
        tail = lax.slice_in_dim(cells, cells.shape[dim] - width, cells.shape[dim], axis=dim)
        cells = jnp.concatenate(
            [
                lax.ppermute(tail, axis, [(i, (i + 1) % count) for i in range(ends)]),
                cells,
                lax.ppermute(head, axis, [((i + 1) % count, i) for i in range(ends)]),
            ],
            axis=dim,
        )
    return cells


def local(patches, conv_taps, conv_bias, norm_gain, norm_bias, qkv_weight, qkv_bias):
    tile_rows, tile_cols, width = patches.shape
    padded = with_halo(patches, (("rows", 0), ("cols", 1)), 1)
    mixed = patches.astype(jnp.float32) + conv_bias
    for a in range(3):
        for b in range(3):
            mixed = mixed + conv_taps[a, b] * padded[a : a + tile_rows, b : b + tile_cols].astype(
                jnp.float32
            )
    mean = jnp.mean(mixed, axis=-1, keepdims=True)
    var = jnp.mean((mixed - mean) ** 2, axis=-1, keepdims=True)
    normed = ((mixed - mean) / jnp.sqrt(var + 1e-06) * norm_gain + norm_bias).astype(jnp.bfloat16)
    own_heads = qkv_weight.shape[2] // HD
    weight_own = qkv_weight.reshape(3, width, own_heads, HD)
    bias_own = qkv_bias.astype(jnp.float32).reshape(3, own_heads, 1, 1, HD)
    out = jnp.einsum(
        "rcd,tdhe->thrce",
        lax.all_gather(normed, "cols", axis=1, tiled=True),
        weight_own,
        preferred_element_type=jnp.float32,
    )
    result = (out + bias_own).astype(jnp.bfloat16)
    return result.reshape(3, result.shape[1], tile_rows, result.shape[3] * HD)


def solution(mesh):
    placed = (P("rows", "cols", None), P(), P(), P(), P(), P(None, None, "cols"), P(None, "cols"))
    return jax.shard_map(
        local, mesh=mesh, in_specs=placed, out_specs=P(None, "cols", "rows", None), check_vma=False
    )
```

profile of v0, /device:TPU:0, one launch (start us, length us, event | category | flops | bytes accessed | tf_op | source)
XLA Modules:
  0.0 122.3 jit_solution(8353807459525792010)
XLA Ops:
  6.5 0.0 copy-start
  6.5 0.0 copy-start.2
  6.5 0.0 copy-start.3
  6.5 0.0 all-gather.2.cloned.1.call-start
  6.5 0.0 copy-start.1
  6.6 1.0 fusion.21
  7.6 5.0 %collective-permute-start = (bf16[1,24,1280]{2,1,0:T(8,128)(2,1)S(1)}, bf16[1,24,1280]{2,1,0:T(8,128)(2,1)S(1)}, u32[]{:S(2)}, u32[]{:S(2)}) collective-permute-start(bf16[1,24,1280]{2,1,0:T(8,128)(2,1)S(1)} %get-tuple-element.19), channel_id=1, source_target_pairs={{0,4},{4,8},{8,12},{12,16},{16,20},{20,24},{24,28},{1,5},{5,9},{9,... | collective-permute-start | bytes 184328 | tf_op jit(solution)/shard_map/ppermute | solution.py:17
  12.6 1.3 %collective-permute-start.1 = (bf16[1,24,1280]{2,1,0:T(8,128)(2,1)S(1)}, bf16[1,24,1280]{2,1,0:T(8,128)(2,1)S(1)}, u32[]{:S(2)}, u32[]{:S(2)}) collective-permute-start(bf16[1,24,1280]{2,1,0:T(8,128)(2,1)S(1)} %get-tuple-element.18), channel_id=1, source_target_pairs={{4,0},{8,4},{12,8},{16,12},{20,16},{24,20},{28,24},{5,1},{9,5},{13... | collective-permute-start | bytes 184328 | tf_op jit(solution)/shard_map/ppermute | solution.py:19
  13.9 0.5 collective-permute-done
  14.4 1.5 %constant_dynamic-update-slice_fusion.1 = bf16[26,24,1280]{2,1,0:T(8,128)(2,1)S(1)} fusion(bf16[26,24,1280]{2,1,0:T(8,128)(2,1)S(1)} %constant_dynamic-update-slice_fusion.2, bf16[24,24,1280]{2,1,0:T(8,128)(2,1)} %param.7), kind=kLoop, calls=%fused_computation.35 | loop fusion | bytes 2949120
  15.9 2.8 %collective-permute-done.1 = bf16[1,24,1280]{2,1,0:T(8,128)(2,1)S(1)} collective-permute-done((bf16[1,24,1280]{2,1,0:T(8,128)(2,1)S(1)}, bf16[1,24,1280]{2,1,0:T(8,128)(2,1)S(1)}, u32[]{:S(2)}, u32[]{:S(2)}) %collective-permute-start.1) | collective-permute-done | bytes 61472 | tf_op jit(solution)/shard_map/ppermute | solution.py:19
  18.7 0.2 fusion.20
  18.9 1.3 %collective-permute-start.2 = (bf16[26,1,1280]{2,1,0:T(2,128)(2,1)S(1)}, bf16[26,1,1280]{2,1,0:T(2,128)(2,1)S(1)}, u32[]{:S(2)}, u32[]{:S(2)}) collective-permute-start(bf16[26,1,1280]{2,1,0:T(2,128)(2,1)S(1)} %get-tuple-element.16), channel_id=1, source_target_pairs={{0,1},{1,2},{2,3},{4,5},{5,6},{6,7},{8,9},{9,10},{10,11},{12,13},{... | collective-permute-start | bytes 199688 | tf_op jit(solution)/shard_map/ppermute | solution.py:17
  20.2 1.3 %collective-permute-start.3 = (bf16[26,1,1280]{2,1,0:T(2,128)(2,1)S(1)}, bf16[26,1,1280]{2,1,0:T(2,128)(2,1)S(1)}, u32[]{:S(2)}, u32[]{:S(2)}) collective-permute-start(bf16[26,1,1280]{2,1,0:T(2,128)(2,1)S(1)} %get-tuple-element.17), channel_id=1, source_target_pairs={{1,0},{2,1},{3,2},{5,4},{6,5},{7,6},{9,8},{10,9},{11,10},{13,12},{... | collective-permute-start | bytes 199688 | tf_op jit(solution)/shard_map/ppermute | solution.py:19
  21.5 0.0 copy-done.2
  21.5 0.1 slice_reduce_fusion.8
  21.7 0.0 collective-permute-done.2
  21.7 3.5 %collective-permute-done.3 = bf16[26,1,1280]{2,1,0:T(2,128)(2,1)S(1)} collective-permute-done((bf16[26,1,1280]{2,1,0:T(2,128)(2,1)S(1)}, bf16[26,1,1280]{2,1,0:T(2,128)(2,1)S(1)}, u32[]{:S(2)}, u32[]{:S(2)}) %collective-permute-start.3) | collective-permute-done | bytes 66592 | tf_op jit(solution)/shard_map/ppermute | solution.py:19
  25.2 0.0 copy-done.3
  25.2 0.0 copy-done.1
  25.2 5.9 %fusion.18 = (f32[24,24]{1,0:T(8,128)S(1)}, f32[24,24,1280]{2,1,0:T(8,128)S(1)}) fusion(bf16[26,1,1280]{2,1,0:T(2,128)(2,1)S(1)} %collective-permute-done.3, bf16[26,24,1280]{2,1,0:T(8,128)(2,1)S(1)} %constant_dynamic-update-slice_fusion, f32[1280]{0:T(1024)S(1)} %get-tuple-element.12, bf16[1,24,1280]{2,1,0:T(8,128)(2,1)S(1)} %collective-permute-done.1, ...), kind=kLoop, calls=%fused_computation.47 | loop fusion | flops 39075264 | bytes 6330624 | tf_op jit(solution)/shard_map/reduce_sum | solution.py:35
  31.1 0.0 copy-start.4
  31.2 0.0 copy-start.5
  31.2 0.4 multiply_reduce_fusion
  31.6 0.2 copy-done.4
  31.8 0.0 copy-done.5
  31.9 0.0 copy-start.6
  31.9 1.6 %add_convert_fusion.1 = bf16[24,24,1280]{2,1,0:T(8,128)(2,1)} fusion(f32[24,24,1280]{2,1,0:T(8,128)S(1)} %get-tuple-element.15, f32[1280]{0:T(1024)S(1)} %copy-done.4, f32[1280]{0:T(1024)S(1)} %copy-done.5, f32[24,24]{1,0:T(8,128)S(1)} %add_sqrt_fusion, f32[24,24]{1,0:T(8,128)S(1)} %broadcast_multiply_fusion), kind=kLoop, calls=%fused_computation.15 | loop fusion | flops 3686400 | bytes 4438528 | tf_op jit(solution)/shard_map/convert_element_type | solution.py:37
  33.5 0.0 all-gather.2.cloned.1.call-update
  33.5 0.0 copy-done.6
  33.5 0.1 reshape.25
  33.6 47.6 %all-gather.2.cloned.1.call-done = bf16[24,96,1280]{2,1,0:T(8,128)(2,1)} async-done(((bf16[24,24,1280]{2,1,0:T(8,128)(2,1)}), bf16[24,96,1280]{2,1,0:T(8,128)(2,1)}) %all-gather.2.cloned.1.call-update) | async-done | bytes 5898256 | tf_op jit(solution)/shard_map/all_gather | solution.py:43
  81.3 0.0 copy-done
  81.3 11.0 %fusion = bf16[3,4,24,96,80]{3,4,1,0,2:T(8,128)(2,1)} fusion(f32[3,4,80]{2,1,0:T(4,128)S(1)} %reshape.25, bf16[3,1280,4,80,1]{1,3,2,0,4:T(8,128)(2,1)S(1)} %bitcast.15, bf16[24,96,1280]{2,1,0:T(8,128)(2,1)} %all-gather.2.cloned.1.call-done), kind=kOutput, calls=%fused_computation.1 | convolution fusion | flops 5666734080 | bytes 12783360 | tf_op jit(solution)/shard_map/rcd,tdhe->thrce/dot_general | solution.py:41
  92.3 9.5 %copy.8 = bf16[3,4,24,96,80]{4,3,2,1,0:T(8,128)(2,1)} copy(bf16[3,4,24,96,80]{3,4,1,0,2:T(8,128)(2,1)} %fusion) | data formatting | bytes 8847360 | tf_op jit(solution)/shard_map/convert_element_type | solution.py:47
  101.8 13.7 %reshape.24 = bf16[3,4,24,7680]{3,2,1,0:T(8,128)(2,1)} reshape(bf16[3,4,24,96,80]{4,3,2,1,0:T(8,128)(2,1)} %copy.8) | data formatting | bytes 8847360 | tf_op jit(solution)/shard_map/reshape | solution.py:48
  (4 shorter events, 0.0 us)
Async XLA Ops:
  6.5 74.7 %copy-start = (bf16[3,1280,320]{1,2,0:T(8,128)(2,1)S(1)}, bf16[3,1280,320]{1,2,0:T(8,128)(2,1)}, u32[]{:S(2)}) copy-start(bf16[3,1280,320]{1,2,0:T(8,128)(2,1)} %param.12) | copy-start | bytes 7372804
  6.5 15.0 %copy-start.2 = (f32[3,3,1280]{2,1,0:T(4,128)S(1)}, f32[3,3,1280]{2,1,0:T(4,128)}, u32[]{:S(2)}) copy-start(f32[3,3,1280]{2,1,0:T(4,128)} %param.8) | copy-start | bytes 138244
  6.5 18.7 %copy-start.3 = (f32[1280]{0:T(1024)S(1)}, f32[1280]{0:T(1024)}, u32[]{:S(2)}) copy-start(f32[1280]{0:T(1024)} %param.9) | copy-start | bytes 15364
  6.5 74.7 %all-gather.2.cloned.1.call-start = ((), (), s32[]{:S(2)}) async-start(), calls=%async_computation | async-start | bytes 7372800 | tf_op jit(solution)/shard_map/all_gather | solution.py:43
  6.5 18.7 %copy-start.1 = (bf16[24,24,1280]{2,1,0:T(8,128)(2,1)S(1)}, bf16[24,24,1280]{2,1,0:T(8,128)(2,1)}, u32[]{:S(2)}) copy-start(bf16[24,24,1280]{2,1,0:T(8,128)(2,1)} %param.7) | copy-start | bytes 4423684
  7.6 6.9 %collective-permute-start = (bf16[1,24,1280]{2,1,0:T(8,128)(2,1)S(1)}, bf16[1,24,1280]{2,1,0:T(8,128)(2,1)S(1)}, u32[]{:S(2)}, u32[]{:S(2)}) collective-permute-start(bf16[1,24,1280]{2,1,0:T(8,128)(2,1)S(1)} %get-tuple-element.19), channel_id=1, source_target_pairs={{0,4},{4,8},{8,12},{12,16},{16,20},{20,24},{24,28},{1,5},{5,9},{9,... | collective-permute-start | bytes 184328 | tf_op jit(solution)/shard_map/ppermute | solution.py:17
  12.6 6.1 %collective-permute-start.1 = (bf16[1,24,1280]{2,1,0:T(8,128)(2,1)S(1)}, bf16[1,24,1280]{2,1,0:T(8,128)(2,1)S(1)}, u32[]{:S(2)}, u32[]{:S(2)}) collective-permute-start(bf16[1,24,1280]{2,1,0:T(8,128)(2,1)S(1)} %get-tuple-element.18), channel_id=1, source_target_pairs={{4,0},{8,4},{12,8},{16,12},{20,16},{24,20},{28,24},{5,1},{9,5},{13... | collective-permute-start | bytes 184328 | tf_op jit(solution)/shard_map/ppermute | solution.py:19
  18.9 2.7 %collective-permute-start.2 = (bf16[26,1,1280]{2,1,0:T(2,128)(2,1)S(1)}, bf16[26,1,1280]{2,1,0:T(2,128)(2,1)S(1)}, u32[]{:S(2)}, u32[]{:S(2)}) collective-permute-start(bf16[26,1,1280]{2,1,0:T(2,128)(2,1)S(1)} %get-tuple-element.16), channel_id=1, source_target_pairs={{0,1},{1,2},{2,3},{4,5},{5,6},{6,7},{8,9},{9,10},{10,11},{12,13},{... | collective-permute-start | bytes 199688 | tf_op jit(solution)/shard_map/ppermute | solution.py:17
  20.2 5.0 %collective-permute-start.3 = (bf16[26,1,1280]{2,1,0:T(2,128)(2,1)S(1)}, bf16[26,1,1280]{2,1,0:T(2,128)(2,1)S(1)}, u32[]{:S(2)}, u32[]{:S(2)}) collective-permute-start(bf16[26,1,1280]{2,1,0:T(2,128)(2,1)S(1)} %get-tuple-element.17), channel_id=1, source_target_pairs={{1,0},{2,1},{3,2},{5,4},{6,5},{7,6},{9,8},{10,9},{11,10},{13,12},{... | collective-permute-start | bytes 199688 | tf_op jit(solution)/shard_map/ppermute | solution.py:19
  31.1 0.7 copy-start.4
  31.2 0.7 copy-start.5
  31.9 1.7 %copy-start.6 = (bf16[3,320]{1,0:T(4,128)(2,1)S(1)}, bf16[3,320]{1,0:T(4,128)(2,1)}, u32[]{:S(2)}) copy-start(bf16[3,320]{1,0:T(4,128)(2,1)} %param.13) | copy-start | bytes 5764
Sparse Core Ops, SparseCore 0:
  33.7 47.5 all-gather.1
where the time goes:
time: 123 us; the launch traced here: 122 us
  waiting for transfers between devices  54.5 us (44%)
  local copies, waits for them, and re-layouts  26.3 us (21%)
  between operations  13.5 us (11%)
  matrix products  11 us (9%)
  starting transfers between devices  8.89 us (7%)
  other arithmetic  8.01 us (7%)
    all_gather x1, waiting for transfers between devices, local(): lax.all_gather(normed, 'cols', axis=1, tiled=True)  47.6 us
    reshape x1, local copies, waits for them, and re-layouts, local(): return result.reshape(3, result.shape[1], tile_rows, result.shape[3] * HD)  13.7 us
    dot_general x1, matrix products, local(): jnp.einsum('rcd,tdhe->thrce', lax.all_gather(normed, 'cols', axis=1, tile...  11 us
    convert_element_type x1, local copies, waits for them, and re-layouts, local(): result = (out + bias_own).astype(jnp.bfloat16)  9.5 us
    ppermute x2, waiting for transfers between devices, with_halo(): lax.ppermute(head, axis, [((i + 1) % count, i) for i in range(ends)])  6.3 us
    ppermute x2, starting transfers between devices, with_halo(): lax.ppermute(tail, axis, [(i, (i + 1) % count) for i in range(ends)])  6.3 us
    reduce_sum x1, other arithmetic, local(): mean = jnp.mean(mixed, axis=-1, keepdims=True)  5.94 us
    ppermute x2, starting transfers between devices, with_halo(): lax.ppermute(head, axis, [((i + 1) % count, i) for i in range(ends)])  2.58 us
  transfers between devices with their start and end apart: 5, of which 4 were waited for; matrix products, arithmetic and copies ran while one was open for 1% of the time, Pallas kernels for 0%

commit v1 on v0

v1 whole, which is shorter than its diff:
```python
import functools

import jax
import jax.numpy as jnp
from jax import lax
from jax.experimental import pallas as pl
from jax.experimental.pallas import tpu as pltpu
from jax.sharding import PartitionSpec as P

HD = 80
GROUP = 8
LANES = 128
EPS = 1e-06
VMEM_LIMIT = 16 * 1024 * 1024
EARLY = 4
PIECE = 96
BF16 = jnp.bfloat16
F32 = jnp.float32

VMEM = pl.BlockSpec(memory_space=pltpu.VMEM)
HBM = pl.BlockSpec(memory_space=pltpu.HBM)


def call(body, name, outs, specs, out_specs, scratch, aliases=None):
    return pl.pallas_call(
        body,
        out_shape=outs,
        in_specs=specs,
        out_specs=out_specs,
        scratch_shapes=scratch,
        input_output_aliases=aliases or {},
        compiler_params=pltpu.CompilerParams(vmem_limit_bytes=VMEM_LIMIT),
        cost_estimate=pl.CostEstimate(flops=1024, bytes_accessed=1024, transcendentals=0),
        name=name,
    )


def stencil(taps_ref, bias_ref, lanes, cells, first, count, emit):
    taps = [[taps_ref[a, pl.ds(b, 1), lanes] for b in range(3)] for a in range(3)]
    bias = bias_ref[:, lanes]
    above = here = None
    for i in range(first - 1, first + count + 1):
        l, c, r = cells(i)
        part = [taps[a][0] * l + taps[a][1] * c + taps[a][2] * r for a in range(3)]
        if i > first:
            emit(i - 1, above + part[2])
        if i >= first:
            above = here + (part[1] + c)
        here = part[0] + bias


def normalize(mixed, count, gain_ref, nbias_ref, out_ref):
    width = mixed.shape[1]
    tiles = [pl.ds(k, LANES) for k in range(0, width, LANES)]
    total = mixed[:count, tiles[0]]
    for lanes in tiles[1:]:
        total = total + mixed[:count, lanes]
    mean = jnp.sum(total, axis=1, keepdims=True) * (1.0 / width)
    square = None
    for lanes in tiles:
        centered = mixed[:count, lanes] - mean
        square = centered * centered if square is None else square + centered * centered
    scale = lax.rsqrt(jnp.sum(square, axis=1, keepdims=True) * (1.0 / width) + EPS)
    for lanes in tiles:
        value = (mixed[:count, lanes] - mean) * scale * gain_ref[:, lanes] + nbias_ref[:, lanes]
        out_ref[:count, lanes] = value.astype(BF16)


def each_tile(width, body):
    def step(k, _):
        body(pl.ds(pl.multiple_of(k * LANES, LANES), LANES))
        return 0

    lax.fori_loop(0, width // LANES, step, 0)


def middle_cells(x_ref, lanes, span):
    cols = x_ref.shape[1]

    def cells(i):
        x = x_ref[i, :, lanes].astype(F32)
        return pltpu.roll(x, 1, 0)[span], x[span], pltpu.roll(x, cols - 1, 0)[span]

    return cells


def core_of(cols_axis):
    return lax.rem(lax.axis_index(cols_axis), 2)


def first_kernel(count, x_hbm, taps_hbm, cbias_hbm, gain_hbm, nbias_hbm, out_ref, inner_ref, x_ref, taps_ref, vec_ref, mixed, *rest):
    *flat, sems = rest
    rows, cols, width = x_ref.shape
    need = count + 2
    copies = [
        pltpu.make_async_copy(x_hbm.at[pl.ds(0, need)], x_ref.at[pl.ds(0, need)], sems.at[0]),
        pltpu.make_async_copy(taps_hbm, taps_ref, sems.at[1]),
        pltpu.make_async_copy(cbias_hbm, flat[0], sems.at[2]),
        pltpu.make_async_copy(gain_hbm, flat[1], sems.at[3]),
        pltpu.make_async_copy(nbias_hbm, flat[2], sems.at[4]),
        pltpu.make_async_copy(x_hbm.at[pl.ds(need, rows - need)], x_ref.at[pl.ds(need, rows - need)], sems.at[5]),
    ]
    for copy in copies:
        copy.start()
    for copy in copies[:-1]:
        copy.wait()
    for k in range(3):
        vec_ref[k] = flat[k][...].reshape(1, width)
    span = slice(GROUP, cols - GROUP)
    wide = cols - 2 * GROUP

    def tile(lanes):
        def emit(i, value):
            mixed[pl.ds((i - 1) * wide, wide), lanes] = value

        stencil(taps_ref, vec_ref.at[0], lanes, middle_cells(x_ref, lanes, span), 1, count, emit)

    each_tile(width, tile)
    normalize(mixed, count * wide, vec_ref.at[1], vec_ref.at[2], out_ref)
    copies[-1].wait()
    core = core_of("cols")

    def sides(lanes):
        left = [x_ref[i, pl.ds(0, GROUP), lanes].astype(F32)[:1] for i in range(rows)]
        right = [x_ref[i, pl.ds(cols - GROUP, GROUP), lanes].astype(F32)[GROUP - 1 :] for i in range(rows)]
        left, right = jnp.concatenate(left, axis=0), jnp.concatenate(right, axis=0)
        out_ref[count * wide :, lanes] = jnp.where(core == 1, right, left).astype(BF16)
        inner_ref[:, lanes] = jnp.where(core == 1, left, right).astype(BF16)

    each_tile(width, sides)


def second_kernel(start, x_ref, taps_ref, vec_ref, out_ref, mixed):
    rows, cols, width = x_ref.shape
    span = slice(GROUP, cols - GROUP)
    wide = cols - 2 * GROUP
    count = rows - 1 - start

    def tile(lanes):
        def emit(i, value):
            mixed[pl.ds((i - start) * wide, wide), lanes] = value

        stencil(taps_ref, vec_ref.at[0], lanes, middle_cells(x_ref, lanes, span), start, count, emit)

    each_tile(width, tile)
    normalize(mixed, count * wide, vec_ref.at[1], vec_ref.at[2], out_ref)


def relay_kernel(beside_ref, before_ref, behind_ref, _, out_ref):
    rows = beside_ref.shape[0]
    few = before_ref.shape[0] - rows
    col, count = lax.axis_index("cols"), lax.axis_size("cols")
    core = core_of("cols")
    none = jnp.logical_or(col == 1, col == count - 2)
    out_ref[:rows, :] = beside_ref[...]
    passed = jnp.where(core == 1, before_ref[few:, :].astype(F32), behind_ref[few:, :].astype(F32))
    out_ref[rows:, :] = jnp.where(none, 0.0, passed).astype(BF16)


def halves(sides_ref, rows, lanes):
    other, passed = sides_ref[:rows, lanes].astype(F32), sides_ref[rows:, lanes].astype(F32)
    core = core_of("cols")
    return jnp.where(core == 1, other, passed), jnp.where(core == 1, passed, other)


def sides_kernel(
    x_ref, sides_ref, taps_ref, vec_ref, near_ref, far_ref, top_ref, bottom_ref, lefts, rights, mixed
):
    rows, cols, width = x_ref.shape
    place = lax.broadcasted_iota(jnp.int32, (GROUP, LANES), 0)
    inner = rows - 2
    half = inner * GROUP
    lefts[...], rights[...] = halves(sides_ref, rows, slice(None))
    for ref, at in ((top_ref, 0), (bottom_ref, rows - 1)):
        ref[:cols, :] = x_ref[at]
        ends = jnp.concatenate([lefts[at : at + 1], rights[at : at + 1]], axis=0)
        ref[cols:, :] = ends.astype(BF16)

    def tile(lanes):
        def near(i):
            x = x_ref[i, :, lanes].astype(F32)
            l = jnp.where(place == 0, lefts[pl.ds(i, 1), lanes], pltpu.roll(x, 1, 0)[:GROUP])
            return l, x[:GROUP], pltpu.roll(x, cols - 1, 0)[:GROUP]

        def far(i):
            x = x_ref[i, :, lanes].astype(F32)
            r = jnp.where(place == GROUP - 1, rights[pl.ds(i, 1), lanes], pltpu.roll(x, cols - 1, 0)[cols - GROUP :])
            return pltpu.roll(x, 1, 0)[cols - GROUP :], x[cols - GROUP :], r

        def emit_near(i, value):
            mixed[pl.ds((i - 1) * GROUP, GROUP), lanes] = value

        def emit_far(i, value):
            mixed[pl.ds((inner + i - 1) * GROUP, GROUP), lanes] = value

        stencil(taps_ref, vec_ref.at[0], lanes, near, 1, inner, emit_near)
        stencil(taps_ref, vec_ref.at[0], lanes, far, 1, inner, emit_far)

    each_tile(width, tile)
    gain, nbias = vec_ref.at[1], vec_ref.at[2]
    normalize(mixed, half, gain, nbias, near_ref)
    normalize(mixed.at[pl.ds(half, half)], half, gain, nbias, far_ref)


def edges_kernel(x_ref, sides_ref, up_ref, down_ref, taps_ref, vec_ref, out_ref, mixed):
    rows, cols, width = x_ref.shape
    place = lax.broadcasted_iota(jnp.int32, (cols, LANES), 0)

    def tile(lanes):
        lefts, rights = halves(sides_ref, rows, lanes)
        up, down = up_ref[:, lanes].astype(F32), down_ref[:, lanes].astype(F32)

        def cells(i):
            if i < 0:
                x, l, r = up[:cols], up[cols : cols + 1], up[cols + 1 :]
            elif i == rows:
                x, l, r = down[:cols], down[cols : cols + 1], down[cols + 1 :]
            else:
                x, l, r = x_ref[i, :, lanes].astype(F32), lefts[i : i + 1], rights[i : i + 1]
            return (
                jnp.where(place == 0, l, pltpu.roll(x, 1, 0)),
                x,
                jnp.where(place == cols - 1, r, pltpu.roll(x, cols - 1, 0)),
            )

        def emit(i, value):
            for g in range(cols // GROUP):
                at = 2 * g * GROUP + (GROUP if i else 0)
                mixed[pl.ds(at, GROUP), lanes] = value[g * GROUP : (g + 1) * GROUP]

        stencil(taps_ref, vec_ref.at[0], lanes, cells, 0, 1, emit)
        stencil(taps_ref, vec_ref.at[0], lanes, cells, rows - 1, 1, emit)

    each_tile(width, tile)
    normalize(mixed, 2 * cols, vec_ref.at[1], vec_ref.at[2], out_ref)


def project_kernel(rows, plan, count, fresh, step, side_count, *refs):
    parts, (w_ref, b_ref), refs = refs[:count], refs[count : count + 2], refs[count + 2 :]
    if not fresh:
        refs = refs[1:]
    out_ref, sums, blocks, sems = refs
    heads = w_ref.shape[1] // HD
    width = w_ref.shape[2]
    total = 3 * heads * HD
    block = GROUP * HD
    weight = w_ref[...].reshape(total, width)
    bias = jnp.concatenate([b_ref[pl.ds(t, 1), :].astype(F32) for t in range(3)], axis=1)
    owner = lax.rem(lax.axis_index("cols") + 2 * step, side_count)
    copies = []
    for g, (pieces, other, group) in enumerate(plan):
        rows_of = [parts[ref][pl.ds(at, size), :] for ref, at, size in pieces]
        acc = (
            lax.dot_general(
                jnp.concatenate(rows_of, axis=0),
                weight,
                (((1,), (1,)), ((), ())),
                preferred_element_type=F32,
            )
            + bias
        )
        inner = acc.shape[0] - 2 * GROUP
        for k in range(0, total, LANES):
            piece = acc[:, k : k + LANES]
            span = pl.ds(0, piece.shape[1])
            sums[g % 2, k // LANES, pl.ds(GROUP, inner), span] = piece[:inner]
            sums[g % 2, k // LANES, pl.ds(0, GROUP), span] = piece[inner : inner + GROUP]
            sums[g % 2, k // LANES, pl.ds(inner + GROUP, GROUP), span] = piece[inner + GROUP :]
        position = owner ^ 1 if other else owner
        lane = pl.multiple_of(position * (out_ref.shape[3] // side_count) + group * block, LANES)
        for t in range(3):
            for h in range(heads):
                start = (t * heads + h) * HD
                lo, hi = start // LANES, (start + HD - 1) // LANES + 1
                cells = []
                for j in range(GROUP):
                    tiles = [sums[g % 2, k, pl.ds(j, rows, stride=GROUP), :] for k in range(lo, hi)]
                    cell = tiles[0] if len(tiles) == 1 else jnp.concatenate(tiles, axis=1)
                    cells.append(cell[:, start - lo * LANES : start - lo * LANES + HD])
                blocks[g, t, h] = jnp.concatenate(cells, axis=1).astype(BF16)
            copy = pltpu.make_async_copy(
                blocks.at[g, t], out_ref.at[t, :, :, pl.ds(lane, block)], sems.at[g, t]
            )
            copy.start()
            copies.append(copy)
    for copy in copies:
        copy.wait()


def project(out, parts, plan, step, weight, bias, rows, side_count, shape):
    count = len(parts)
    heads = weight.shape[1] // HD
    fresh = out is None
    operands = [*parts, weight, bias] + ([] if fresh else [out])
    return call(
        functools.partial(project_kernel, rows, plan, count, fresh, step, side_count),
        "project",
        jax.ShapeDtypeStruct(shape, BF16),
        [VMEM] * (count + 2) + ([] if fresh else [HBM]),
        HBM,
        [
            pltpu.VMEM((2, pl.cdiv(3 * heads * HD, LANES), rows * GROUP, LANES), F32),
            pltpu.VMEM((len(plan), 3, heads, rows, GROUP * HD), BF16),
            pltpu.SemaphoreType.DMA((len(plan), 3)),
        ],
        aliases={} if fresh else {len(operands) - 1: 0},
    )(*operands)


def local(patches, conv_taps, conv_bias, norm_gain, norm_bias, qkv_weight, qkv_bias):
    rows, cols, width = patches.shape
    up_count, side_count = lax.axis_size("rows"), lax.axis_size("cols")
    chips = side_count // 2
    wide = cols - 2 * GROUP
    inner = rows - 2
    half = inner * GROUP
    early = EARLY
    few = early * wide
    two = 2 * GROUP
    steps = range(1, chips)

    def array(*shape, dtype=BF16):
        return jax.ShapeDtypeStruct(shape, dtype)

    def across(value):
        return [
            lax.ppermute(value, "cols", [(q, (q + 2 * step) % side_count) for q in range(side_count)])
            for step in steps
        ]

    def swap(value):
        return lax.ppermute(value, "cols", [(q, q ^ 1) for q in range(side_count)])

    def shift(value, axis, count, step):
        return lax.ppermute(value, axis, [(i, i + step) for i in range(count) if 0 <= i + step < count])

    def after(values, others):
        joined = lax.optimization_barrier((*values, *others))
        return list(joined[: len(values)])

    def in_hbm(value):
        return pltpu.with_memory_space_constraint(value, pltpu.HBM)

    first, beside, x, taps, vectors = call(
        functools.partial(first_kernel, early),
        "first",
        [
            array(few + rows, width),
            array(rows, width),
            array(rows, cols, width),
            array(3, 3, width, dtype=F32),
            array(3, 1, width, dtype=F32),
        ],
        [HBM] * 5,
        [VMEM] * 5,
        [pltpu.VMEM((few, width), F32)] + [pltpu.VMEM((width,), F32)] * 3 + [pltpu.SemaphoreType.DMA((6,))],
    )(*[in_hbm(v) for v in (patches, conv_taps, conv_bias, norm_gain, norm_bias)])
    got_first = across(first)

    second = call(
        functools.partial(second_kernel, early + 1),
        "second",
        array(half - few, width),
        [VMEM] * 3,
        VMEM,
        [pltpu.VMEM((half - few, width), F32)],
    )(x, taps, vectors)
    got_second = across(second)

    sides = swap(
        call(
            relay_kernel,
            "relay",
            array(2 * rows, width),
            [VMEM] * 4,
            VMEM,
            [],
        )(beside, got_first[0], got_first[-1], second)
    )

    near, far, top, bottom = call(
        sides_kernel,
        "sides",
        [array(half, width)] * 2 + [array(cols + 2, width)] * 2,
        [VMEM] * 4,
        [VMEM] * 4,
        [pltpu.VMEM((rows, width), F32)] * 2 + [pltpu.VMEM((2 * half, width), F32)],
    )(x, sides, taps, vectors)
    up = shift(bottom, "rows", up_count, 1)
    down = shift(top, "rows", up_count, -1)
    got_near = across(near)
    up, down = after((up, down), got_second)
    edge = call(
        edges_kernel,
        "edges",
        array(2 * cols, width),
        [VMEM] * 6,
        VMEM,
        [pltpu.VMEM((2 * cols, width), F32)],
    )(x, sides, up, down, taps, vectors)
    got_edge = across(edge)
    got_far = across(far)

    shape = (3, qkv_weight.shape[2] // HD, rows, side_count * cols * HD)
    weight = jnp.swapaxes(qkv_weight, 1, 2)
    run = functools.partial(project, weight=weight, bias=qkv_bias, rows=rows, side_count=side_count, shape=shape)

    def cut(value):
        return [value[at : at + PIECE] for at in range(0, value.shape[0], PIECE)]

    def plan(groups, other):
        arrays, entries = [], []
        for group, pieces in groups:
            entry = []
            for value, at, size in pieces:
                entry.append((len(arrays), at, size))
                arrays.append(value)
            entries.append((tuple(entry), other, group))
        return arrays, entries

    def whole(values):
        return [(value, 0, value.shape[0]) for value in values]

    def groups_of(near, first, second, edge, far):
        return [
            (0, whole(near) + [(edge, 0, two)]),
            (1, [(first, 0, few)] + whole(second) + [(edge, two, two)]),
            (2, whole(far) + [(edge, 2 * two, two)]),
        ]

    def step_on(out, groups, other, step):
        arrays, entries = plan(groups, other)
        return run(out, arrays, entries, step)

    out = step_on(None, groups_of([near], first, [second], edge, [far]), 0, 0)
    other_edge = edge
    theirs = groups_of([swap(near)], swap(first), [swap(second)], swap(other_edge), [swap(far)])
    out = step_on(out, theirs, 1, 0)
    for step in steps:
        mine = [v[step - 1] for v in (got_near, got_first, got_second, got_edge)]
        *mine, out = lax.optimization_barrier((*mine, out))
        near, first, second, edge = mine
        other = [swap(v) for v in cut(near)], swap(first), [swap(v) for v in cut(second)], swap(edge)
        out = step_on(out, groups_of([near], first, [second], edge, [])[:2], 0, chips - step)
        out = step_on(out, groups_of(*other, [])[:2], 1, chips - step)
        far, out = lax.optimization_barrier((got_far[step - 1], out))
        out = step_on(out, groups_of([], first, [], edge, [far])[2:], 0, chips - step)
        out = step_on(out, groups_of([], first, [], other[3], [swap(far)])[2:], 1, chips - step)
    return out


def solution(mesh):
    placed = (P("rows", "cols", None), P(), P(), P(), P(), P(None, None, "cols"), P(None, "cols"))
    return jax.shard_map(
        local, mesh=mesh, in_specs=placed, out_specs=P(None, "cols", "rows", None), check_vma=False
    )
```

time: 123 us -> 50.9 us (0.41)
  the two profiles are of different devices: /device:TPU:0 before, /device:TPU:15 now
where the time goes in v1:
time: 50.9 us; the launch traced here: 50.7 us
  starting transfers between devices  23 us (45%)
  Pallas kernels  21.2 us (42%)
  waiting for transfers between devices  6.35 us (12%)
    pallas_call x6, Pallas kernels, project(): call(functools.partial(project_kernel, rows, plan, count, fresh, step, si...  15 us
    ppermute x13, starting transfers between devices, swap(): return lax.ppermute(value, 'cols', [(q, q ^ 1) for q in range(side_count)])  13.4 us
    ppermute x2, starting transfers between devices, shift(): lax.ppermute(value, axis, [(i, i + step) for i in range(count) if 0 <= i...  5.28 us
    ppermute x5, starting transfers between devices, across(): lax.ppermute(value, 'cols', [(q, (q + 2 * step) % side_count) for q in ra...  4.25 us
    pallas_call x1, Pallas kernels, local(): call(sides_kernel, 'sides', [array(half, width)] * 2 + [array(cols + 2, w...  2.54 us
    ppermute x2, waiting for transfers between devices, shift(): lax.ppermute(value, axis, [(i, i + step) for i in range(count) if 0 <= i...  2.44 us
    ppermute x5, waiting for transfers between devices, across(): lax.ppermute(value, 'cols', [(q, (q + 2 * step) % side_count) for q in ra...  2.26 us
    pallas_call x1, Pallas kernels, local(): call(functools.partial(first_kernel, early), 'first', [array(few + rows,...  1.9 us
  transfers between devices with their start and end apart: 20, of which 6 were waited for; matrix products, arithmetic and copies ran while one was open for 0% of the time, Pallas kernels for 35%

profile of v1, /device:TPU:15, one launch (start us, length us, event | category | flops | bytes accessed | tf_op | source)
XLA Modules:
  0.0 50.7 jit_solution(3623445964520416364)
XLA Ops:
  0.0 0.0 copy-start.1
  0.0 0.0 copy-start
  0.0 1.9 %first.1 = (bf16[56,1280]{1,0:T(8,128)(2,1)S(1)}, bf16[24,1280]{1,0:T(8,128)(2,1)S(1)}, bf16[24,24,1280]{2,1,0:T(8,128)(2,1)S(1)}, f32[3,3,1280]{2,1,0:T(4,128)S(1)}, f32[3,1,1280]{2,1,0:T(1,128)S(1)}) custom-call(bf16[24,24,1280]{2,1,0:T(8,128)(2,1)} %x_hbm.1, f32[3,3,1280]{2,1,0:T(4,128)} %taps_hbm.1, f32[1280]{0:T(1024)} %cbias_hbm.1, f32[1280]{0:T(1024)} %gain_hbm.1, ...), custom_call_target="tpu_custom_call" | custom-call | flops 1024 | bytes 1024 | tf_op jit(solution)/shard_map/first/pallas_call | solution.py:344
  1.9 0.3 collective-permute-start
  2.2 1.1 %second.1._.refs_3_ = bf16[144,1280]{1,0:T(8,128)(2,1)S(1)} custom-call(bf16[24,24,1280]{2,1,0:T(8,128)(2,1)S(1)} %get-tuple-element.23.x_ref, f32[3,3,1280]{2,1,0:T(4,128)S(1)} %get-tuple-element.26.taps_ref, f32[3,1,1280]{2,1,0:T(1,128)S(1)} %get-tuple-element.27.vec_ref), custom_call_target="tpu_custom_call" | custom-call | flops 1024 | bytes 1024 | tf_op jit(solution)/shard_map/second/pallas_call | solution.py:360
  3.3 1.3 %collective-permute-start.4 = (bf16[144,1280]{1,0:T(8,128)(2,1)S(1)}, bf16[144,1280]{1,0:T(8,128)(2,1)S(1)}, u32[]{:S(2)}, u32[]{:S(2)}) collective-permute-start(bf16[144,1280]{1,0:T(8,128)(2,1)S(1)} %second.1._.refs_3_), channel_id=1, source_target_pairs={{0,2},{1,3},{2,0},{3,1},{4,6},{5,7},{6,4},{7,5},{8,10},{9,11},{10,... | collective-permute-start | bytes 1105928 | tf_op jit(solution)/shard_map/ppermute | solution.py:327
  4.6 2.0 %collective-permute-done.before_ref.behind_ref.refs_2_ = bf16[56,1280]{1,0:T(8,128)(2,1)S(1)} collective-permute-done((bf16[56,1280]{1,0:T(8,128)(2,1)S(1)}, bf16[56,1280]{1,0:T(8,128)(2,1)S(1)}, u32[]{:S(2)}, u32[]{:S(2)}) %collective-permute-start) | collective-permute-done | bytes 143392 | tf_op jit(solution)/shard_map/ppermute | solution.py:327
  6.6 2.8 %collective-permute-start.1 = (bf16[48,1280]{1,0:T(8,128)(2,1)S(1)}, bf16[48,1280]{1,0:T(8,128)(2,1)S(1)}, u32[]{:S(2)}, u32[]{:S(2)}) collective-permute-start(bf16[48,1280]{1,0:T(8,128)(2,1)S(1)} %relay.1), channel_id=1, source_target_pairs={{0,1},{1,0},{2,3},{3,2},{4,5},{5,4},{6,7},{7,6},{8,9},{9,8},{10,11... | collective-permute-start | bytes 368648 | tf_op jit(solution)/shard_map/ppermute | solution.py:332
  9.4 1.0 %collective-permute-done.1.sides_ref = bf16[48,1280]{1,0:T(8,128)(2,1)S(1)} collective-permute-done((bf16[48,1280]{1,0:T(8,128)(2,1)S(1)}, bf16[48,1280]{1,0:T(8,128)(2,1)S(1)}, u32[]{:S(2)}, u32[]{:S(2)}) %collective-permute-start.1) | collective-permute-done | bytes 122912 | tf_op jit(solution)/shard_map/ppermute | solution.py:332
  10.4 2.5 %sides.1 = (bf16[176,1280]{1,0:T(8,128)(2,1)S(1)}, bf16[176,1280]{1,0:T(8,128)(2,1)S(1)}, bf16[26,1280]{1,0:T(8,128)(2,1)S(1)}, bf16[26,1280]{1,0:T(8,128)(2,1)S(1)}) custom-call(bf16[24,24,1280]{2,1,0:T(8,128)(2,1)S(1)} %get-tuple-element.23.x_ref, bf16[48,1280]{1,0:T(8,128)(2,1)S(1)} %collective-permute-done.1.sides_ref, ...), custom_call_target="tpu_custom_call" | custom-call | flops 1024 | bytes 1024 | tf_op jit(solution)/shard_map/sides/pallas_call | solution.py:381
  12.9 3.1 %collective-permute-start.5 = (bf16[26,1280]{1,0:T(8,128)(2,1)S(1)}, bf16[26,1280]{1,0:T(8,128)(2,1)S(1)}, u32[]{:S(2)}, u32[]{:S(2)}) collective-permute-start(bf16[26,1280]{1,0:T(8,128)(2,1)S(1)} %get-tuple-element.30), channel_id=1, source_target_pairs={{0,4},{4,8},{8,12},{12,16},{16,20},{20,24},{24,28},{1,5},{5,9},{9,... | collective-permute-start | bytes 199688 | tf_op jit(solution)/shard_map/ppermute | solution.py:335
  16.1 2.1 %collective-permute-start.6 = (bf16[26,1280]{1,0:T(8,128)(2,1)S(1)}, bf16[26,1280]{1,0:T(8,128)(2,1)S(1)}, u32[]{:S(2)}, u32[]{:S(2)}) collective-permute-start(bf16[26,1280]{1,0:T(8,128)(2,1)S(1)} %get-tuple-element.31), channel_id=1, source_target_pairs={{4,0},{8,4},{12,8},{16,12},{20,16},{24,20},{28,24},{5,1},{9,5},{13... | collective-permute-start | bytes 199688 | tf_op jit(solution)/shard_map/ppermute | solution.py:335
  18.2 1.0 %collective-permute-start.11 = (bf16[144,1280]{1,0:T(8,128)(2,1)S(1)}, bf16[144,1280]{1,0:T(8,128)(2,1)S(1)}, u32[]{:S(2)}, u32[]{:S(2)}) collective-permute-start(bf16[144,1280]{1,0:T(8,128)(2,1)S(1)} %second.1._.refs_3_), channel_id=1, source_target_pairs={{0,1},{1,0},{2,3},{3,2},{4,5},{5,4},{6,7},{7,6},{8,9},{9,8},{10,11... | collective-permute-start | bytes 1105928 | tf_op jit(solution)/shard_map/ppermute | solution.py:332
  19.2 0.1 collective-permute-start.12
  19.3 0.0 collective-permute-done.5.up_ref
  19.3 0.4 collective-permute-start.8
  19.7 2.4 %collective-permute-done.6.down_ref = bf16[26,1280]{1,0:T(8,128)(2,1)S(1)} collective-permute-done((bf16[26,1280]{1,0:T(8,128)(2,1)S(1)}, bf16[26,1280]{1,0:T(8,128)(2,1)S(1)}, u32[]{:S(2)}, u32[]{:S(2)}) %collective-permute-start.6) | collective-permute-done | bytes 66592 | tf_op jit(solution)/shard_map/ppermute | solution.py:335
  22.2 0.0 collective-permute-start.3
  22.2 0.0 collective-permute-done.4.refs_3_
  22.2 1.9 %collective-permute-start.10 = (bf16[56,1280]{1,0:T(8,128)(2,1)S(1)}, bf16[56,1280]{1,0:T(8,128)(2,1)S(1)}, u32[]{:S(2)}, u32[]{:S(2)}) collective-permute-start(bf16[56,1280]{1,0:T(8,128)(2,1)S(1)} %get-tuple-element.25.refs_2_), channel_id=1, source_target_pairs={{0,1},{1,0},{2,3},{3,2},{4,5},{5,4},{6,7},{7,6},{8,9},{9,8},{10,11... | collective-permute-start | bytes 430088 | tf_op jit(solution)/shard_map/ppermute | solution.py:332
  24.0 0.6 %edges.1.refs_1_.refs_4_.refs_6_ = bf16[48,1280]{1,0:T(8,128)(2,1)S(1)} custom-call(bf16[24,24,1280]{2,1,0:T(8,128)(2,1)S(1)} %get-tuple-element.23.x_ref, bf16[48,1280]{1,0:T(8,128)(2,1)S(1)} %collective-permute-done.1.sides_ref, bf16[26,1280]{1,0:T(8,128)(2,1)S(1)} %collective-permute-done.5.up_ref, bf16[26,1280]{1,0:T(8,128)(2,1)S(1)} %collective-permute-done.6.down_ref, ...), custom_call_target="tpu_custom_call" | custom-call | flops 1024 | bytes 1024 | tf_op jit(solution)/shard_map/edges/pallas_call | solution.py:393
  24.6 0.4 collective-permute-done.10.refs_2_
  25.0 0.4 collective-permute-start.9
  25.4 0.0 collective-permute-done.11.refs_3_
  25.4 1.7 %collective-permute-start.7 = (bf16[48,1280]{1,0:T(8,128)(2,1)S(1)}, bf16[48,1280]{1,0:T(8,128)(2,1)S(1)}, u32[]{:S(2)}, u32[]{:S(2)}) collective-permute-start(bf16[48,1280]{1,0:T(8,128)(2,1)S(1)} %edges.1.refs_1_.refs_4_.refs_6_), channel_id=1, source_target_pairs={{0,2},{1,3},{2,0},{3,1},{4,6},{5,7},{6,4},{7,5},{8,10},{9,11},{10,... | collective-permute-start | bytes 368648 | tf_op jit(solution)/shard_map/ppermute | solution.py:327
  27.1 0.0 collective-permute-done.9.refs_1_.refs_4_.refs_6_
  27.1 1.0 %collective-permute-start.2 = (bf16[176,1280]{1,0:T(8,128)(2,1)S(1)}, bf16[176,1280]{1,0:T(8,128)(2,1)S(1)}, u32[]{:S(2)}, u32[]{:S(2)}) collective-permute-start(bf16[176,1280]{1,0:T(8,128)(2,1)S(1)} %get-tuple-element.28.refs_5_), channel_id=1, source_target_pairs={{0,2},{1,3},{2,0},{3,1},{4,6},{5,7},{6,4},{7,5},{8,10},{9,11},{10,... | collective-permute-start | bytes 1351688 | tf_op jit(solution)/shard_map/ppermute | solution.py:327
  28.0 0.0 copy-done.1
  28.0 0.0 copy-done
  28.0 3.3 %project.6.refs_9_ = bf16[3,4,24,7680]{3,2,1,0:T(8,128)(2,1)} custom-call(bf16[176,1280]{1,0:T(8,128)(2,1)S(1)} %get-tuple-element.29.refs_0_, bf16[48,1280]{1,0:T(8,128)(2,1)S(1)} %edges.1.refs_1_.refs_4_.refs_6_, bf16[56,1280]{1,0:T(8,128)(2,1)S(1)} %get-tuple-element.25.refs_2_, bf16[144,1280]{1,0:T(8,128)(2,1)S(1)} %second.1._.refs_3_, ...), custom_call_target="tpu_custom_call" | custom-call | flops 1024 | bytes 1024 | tf_op jit(solution)/shard_map/project/pallas_call | solution.py:295
  31.3 0.0 collective-permute-done.12.refs_5_
  31.3 0.0 collective-permute-done.8.refs_0_
  31.3 3.3 %project.7.refs_7_ = bf16[3,4,24,7680]{3,2,1,0:T(8,128)(2,1)} custom-call(bf16[176,1280]{1,0:T(8,128)(2,1)S(1)} %collective-permute-done.8.refs_0_, bf16[48,1280]{1,0:T(8,128)(2,1)S(1)} %collective-permute-done.9.refs_1_.refs_4_.refs_6_, bf16[56,1280]{1,0:T(8,128)(2,1)S(1)} %collective-permute-done.10.refs_2_, ...), custom_call_target="tpu_custom_call", output_to_operand_aliasing={{}: (9, {})} | custom-call | flops 1024 | bytes 1024 | tf_op jit(solution)/shard_map/project/pallas_call | solution.py:295
  34.6 0.2 collective-permute-done.7.refs_1_.refs_4_
  34.8 0.0 collective-permute-done.3.refs_0_
  34.8 5.1 %collective-permute-start.18 = (bf16[48,1280]{1,0:T(8,128)(2,1)S(1)}, bf16[48,1280]{1,0:T(8,128)(2,1)S(1)}, u32[]{:S(2)}, u32[]{:S(2)}) collective-permute-start(bf16[48,1280]{1,0:T(8,128)(2,1)S(1)} %slice.15), channel_id=1, source_target_pairs={{0,1},{1,0},{2,3},{3,2},{4,5},{5,4},{6,7},{7,6},{8,9},{9,8},{10,11... | collective-permute-start | bytes 368648 | tf_op jit(solution)/shard_map/ppermute | solution.py:332
  39.9 0.1 collective-permute-start.15
  40.1 0.5 collective-permute-start.13
  40.6 0.1 collective-permute-start.17
  40.7 0.3 collective-permute-done.18.refs_5_
  40.9 0.4 collective-permute-start.14
  41.3 0.0 collective-permute-done.15.refs_2_.refs_6_.refs_1_
  41.3 0.2 collective-permute-start.16
  41.5 2.5 %project.8.refs_9_ = bf16[3,4,24,7680]{3,2,1,0:T(8,128)(2,1)} custom-call(bf16[176,1280]{1,0:T(8,128)(2,1)S(1)} %collective-permute-done.3.refs_0_, bf16[48,1280]{1,0:T(8,128)(2,1)S(1)} %collective-permute-done.7.refs_1_.refs_4_, bf16[56,1280]{1,0:T(8,128)(2,1)S(1)} %collective-permute-done.before_ref.behind_ref.refs_2_, ...), custom_call_target="tpu_custom_call", output_to_operand_aliasing={{}: (7, {})} | custom-call | flops 1024 | bytes 1024 | tf_op jit(solution)/shard_map/project/pallas_call | solution.py:295
  44.0 0.0 collective-permute-done.16.refs_3_
  44.0 0.0 collective-permute-done.14.refs_1_
  44.0 0.0 collective-permute-done.13.refs_0_
  44.0 0.0 collective-permute-done.17.refs_4_
  44.0 2.5 %project.9.refs_4_ = bf16[3,4,24,7680]{3,2,1,0:T(8,128)(2,1)} custom-call(bf16[96,1280]{1,0:T(8,128)(2,1)S(1)} %collective-permute-done.13.refs_0_, bf16[80,1280]{1,0:T(8,128)(2,1)S(1)} %collective-permute-done.14.refs_1_, bf16[48,1280]{1,0:T(8,128)(2,1)S(1)} %collective-permute-done.15.refs_2_.refs_6_.refs_1_, ...), custom_call_target="tpu_custom_call", output_to_operand_aliasing={{}: (9, {})} | custom-call | flops 1024 | bytes 1024 | tf_op jit(solution)/shard_map/project/pallas_call | solution.py:295
  46.5 0.0 collective-permute-done.2.refs_0_
  46.5 0.7 %collective-permute-start.19 = (bf16[176,1280]{1,0:T(8,128)(2,1)S(1)}, bf16[176,1280]{1,0:T(8,128)(2,1)S(1)}, u32[]{:S(2)}, u32[]{:S(2)}) collective-permute-start(bf16[176,1280]{1,0:T(8,128)(2,1)S(1)} %collective-permute-done.2.refs_0_), channel_id=1, source_target_pairs={{0,1},{1,0},{2,3},{3,2},{4,5},{5,4},{6,7},{7,6},{8,9},{9,8},{10,11... | collective-permute-start | bytes 1351688 | tf_op jit(solution)/shard_map/ppermute | solution.py:332
  47.2 1.7 %project.10.refs_4_ = bf16[3,4,24,7680]{3,2,1,0:T(8,128)(2,1)} custom-call(bf16[176,1280]{1,0:T(8,128)(2,1)S(1)} %collective-permute-done.2.refs_0_, bf16[48,1280]{1,0:T(8,128)(2,1)S(1)} %collective-permute-done.7.refs_1_.refs_4_, bf16[3,320,1280]{2,1,0:T(8,128)(2,1)S(1)} %bitcast.5, bf16[3,320]{1,0:T(4,128)(2,1)S(1)} %copy-done.1, ...), custom_call_target="tpu_custom_call", output_to_operand_aliasing={{}: (4, {})} | custom-call | flops 1024 | bytes 1024 | tf_op jit(solution)/shard_map/project/pallas_call | solution.py:295
  49.0 0.0 collective-permute-done.19.refs_0_
  49.0 1.8 %project.11 = bf16[3,4,24,7680]{3,2,1,0:T(8,128)(2,1)} custom-call(bf16[176,1280]{1,0:T(8,128)(2,1)S(1)} %collective-permute-done.19.refs_0_, bf16[48,1280]{1,0:T(8,128)(2,1)S(1)} %collective-permute-done.15.refs_2_.refs_6_.refs_1_, bf16[3,320,1280]{2,1,0:T(8,128)(2,1)S(1)} %bitcast.6, bf16[3,320]{1,0:T(4,128)(2,1)S(1)} %copy-done.1, ...), custom_call_target="tpu_custom_call", output_to_operand_aliasing={{}: (4, {})} | custom-call | flops 1024 | bytes 1024 | tf_op jit(solution)/shard_map/project/pallas_call | solution.py:295
  (5 shorter events, 0.1 us)
Async XLA Ops:
  0.0 28.0 %copy-start.1 = (bf16[3,320]{1,0:T(4,128)(2,1)S(1)}, bf16[3,320]{1,0:T(4,128)(2,1)}, u32[]{:S(2)}) copy-start(bf16[3,320]{1,0:T(4,128)(2,1)} %refs_3_.3) | copy-start | bytes 5764
  0.0 28.0 %copy-start = (bf16[3,1280,320]{1,2,0:T(8,128)(2,1)S(1)}, bf16[3,1280,320]{1,2,0:T(8,128)(2,1)}, u32[]{:S(2)}) copy-start(bf16[3,1280,320]{1,2,0:T(8,128)(2,1)} %param.12) | copy-start | bytes 7372804
  1.9 4.7 %collective-permute-start = (bf16[56,1280]{1,0:T(8,128)(2,1)S(1)}, bf16[56,1280]{1,0:T(8,128)(2,1)S(1)}, u32[]{:S(2)}, u32[]{:S(2)}) collective-permute-start(bf16[56,1280]{1,0:T(8,128)(2,1)S(1)} %get-tuple-element.25.refs_2_), channel_id=1, source_target_pairs={{0,2},{1,3},{2,0},{3,1},{4,6},{5,7},{6,4},{7,5},{8,10},{9,11},{10,... | collective-permute-start | bytes 430088 | tf_op jit(solution)/shard_map/ppermute | solution.py:327
  3.3 18.8 %collective-permute-start.4 = (bf16[144,1280]{1,0:T(8,128)(2,1)S(1)}, bf16[144,1280]{1,0:T(8,128)(2,1)S(1)}, u32[]{:S(2)}, u32[]{:S(2)}) collective-permute-start(bf16[144,1280]{1,0:T(8,128)(2,1)S(1)} %second.1._.refs_3_), channel_id=1, source_target_pairs={{0,2},{1,3},{2,0},{3,1},{4,6},{5,7},{6,4},{7,5},{8,10},{9,11},{10,... | collective-permute-start | bytes 1105928 | tf_op jit(solution)/shard_map/ppermute | solution.py:327
  6.6 3.7 %collective-permute-start.1 = (bf16[48,1280]{1,0:T(8,128)(2,1)S(1)}, bf16[48,1280]{1,0:T(8,128)(2,1)S(1)}, u32[]{:S(2)}, u32[]{:S(2)}) collective-permute-start(bf16[48,1280]{1,0:T(8,128)(2,1)S(1)} %relay.1), channel_id=1, source_target_pairs={{0,1},{1,0},{2,3},{3,2},{4,5},{5,4},{6,7},{7,6},{8,9},{9,8},{10,11... | collective-permute-start | bytes 368648 | tf_op jit(solution)/shard_map/ppermute | solution.py:332
  12.9 6.4 %collective-permute-start.5 = (bf16[26,1280]{1,0:T(8,128)(2,1)S(1)}, bf16[26,1280]{1,0:T(8,128)(2,1)S(1)}, u32[]{:S(2)}, u32[]{:S(2)}) collective-permute-start(bf16[26,1280]{1,0:T(8,128)(2,1)S(1)} %get-tuple-element.30), channel_id=1, source_target_pairs={{0,4},{4,8},{8,12},{12,16},{16,20},{20,24},{24,28},{1,5},{5,9},{9,... | collective-permute-start | bytes 199688 | tf_op jit(solution)/shard_map/ppermute | solution.py:335
  16.1 6.1 %collective-permute-start.6 = (bf16[26,1280]{1,0:T(8,128)(2,1)S(1)}, bf16[26,1280]{1,0:T(8,128)(2,1)S(1)}, u32[]{:S(2)}, u32[]{:S(2)}) collective-permute-start(bf16[26,1280]{1,0:T(8,128)(2,1)S(1)} %get-tuple-element.31), channel_id=1, source_target_pairs={{4,0},{8,4},{12,8},{16,12},{20,16},{24,20},{28,24},{5,1},{9,5},{13... | collective-permute-start | bytes 199688 | tf_op jit(solution)/shard_map/ppermute | solution.py:335
  18.2 7.2 %collective-permute-start.11 = (bf16[144,1280]{1,0:T(8,128)(2,1)S(1)}, bf16[144,1280]{1,0:T(8,128)(2,1)S(1)}, u32[]{:S(2)}, u32[]{:S(2)}) collective-permute-start(bf16[144,1280]{1,0:T(8,128)(2,1)S(1)} %second.1._.refs_3_), channel_id=1, source_target_pairs={{0,1},{1,0},{2,3},{3,2},{4,5},{5,4},{6,7},{7,6},{8,9},{9,8},{10,11... | collective-permute-start | bytes 1105928 | tf_op jit(solution)/shard_map/ppermute | solution.py:332
  19.2 12.1 %collective-permute-start.12 = (bf16[176,1280]{1,0:T(8,128)(2,1)S(1)}, bf16[176,1280]{1,0:T(8,128)(2,1)S(1)}, u32[]{:S(2)}, u32[]{:S(2)}) collective-permute-start(bf16[176,1280]{1,0:T(8,128)(2,1)S(1)} %get-tuple-element.28.refs_5_), channel_id=1, source_target_pairs={{0,1},{1,0},{2,3},{3,2},{4,5},{5,4},{6,7},{7,6},{8,9},{9,8},{10,11... | collective-permute-start | bytes 1351688 | tf_op jit(solution)/shard_map/ppermute | solution.py:332
  19.3 12.0 %collective-permute-start.8 = (bf16[176,1280]{1,0:T(8,128)(2,1)S(1)}, bf16[176,1280]{1,0:T(8,128)(2,1)S(1)}, u32[]{:S(2)}, u32[]{:S(2)}) collective-permute-start(bf16[176,1280]{1,0:T(8,128)(2,1)S(1)} %get-tuple-element.29.refs_0_), channel_id=1, source_target_pairs={{0,1},{1,0},{2,3},{3,2},{4,5},{5,4},{6,7},{7,6},{8,9},{9,8},{10,11... | collective-permute-start | bytes 1351688 | tf_op jit(solution)/shard_map/ppermute | solution.py:332
  22.2 12.7 %collective-permute-start.3 = (bf16[176,1280]{1,0:T(8,128)(2,1)S(1)}, bf16[176,1280]{1,0:T(8,128)(2,1)S(1)}, u32[]{:S(2)}, u32[]{:S(2)}) collective-permute-start(bf16[176,1280]{1,0:T(8,128)(2,1)S(1)} %get-tuple-element.29.refs_0_), channel_id=1, source_target_pairs={{0,2},{1,3},{2,0},{3,1},{4,6},{5,7},{6,4},{7,5},{8,10},{9,11},{10,... | collective-permute-start | bytes 1351688 | tf_op jit(solution)/shard_map/ppermute | solution.py:327
  22.2 2.9 %collective-permute-start.10 = (bf16[56,1280]{1,0:T(8,128)(2,1)S(1)}, bf16[56,1280]{1,0:T(8,128)(2,1)S(1)}, u32[]{:S(2)}, u32[]{:S(2)}) collective-permute-start(bf16[56,1280]{1,0:T(8,128)(2,1)S(1)} %get-tuple-element.25.refs_2_), channel_id=1, source_target_pairs={{0,1},{1,0},{2,3},{3,2},{4,5},{5,4},{6,7},{7,6},{8,9},{9,8},{10,11... | collective-permute-start | bytes 430088 | tf_op jit(solution)/shard_map/ppermute | solution.py:332
  25.0 2.0 %collective-permute-start.9 = (bf16[48,1280]{1,0:T(8,128)(2,1)S(1)}, bf16[48,1280]{1,0:T(8,128)(2,1)S(1)}, u32[]{:S(2)}, u32[]{:S(2)}) collective-permute-start(bf16[48,1280]{1,0:T(8,128)(2,1)S(1)} %edges.1.refs_1_.refs_4_.refs_6_), channel_id=1, source_target_pairs={{0,1},{1,0},{2,3},{3,2},{4,5},{5,4},{6,7},{7,6},{8,9},{9,8},{10,11... | collective-permute-start | bytes 368648 | tf_op jit(solution)/shard_map/ppermute | solution.py:332
  25.4 9.4 %collective-permute-start.7 = (bf16[48,1280]{1,0:T(8,128)(2,1)S(1)}, bf16[48,1280]{1,0:T(8,128)(2,1)S(1)}, u32[]{:S(2)}, u32[]{:S(2)}) collective-permute-start(bf16[48,1280]{1,0:T(8,128)(2,1)S(1)} %edges.1.refs_1_.refs_4_.refs_6_), channel_id=1, source_target_pairs={{0,2},{1,3},{2,0},{3,1},{4,6},{5,7},{6,4},{7,5},{8,10},{9,11},{10,... | collective-permute-start | bytes 368648 | tf_op jit(solution)/shard_map/ppermute | solution.py:327
  27.1 19.4 %collective-permute-start.2 = (bf16[176,1280]{1,0:T(8,128)(2,1)S(1)}, bf16[176,1280]{1,0:T(8,128)(2,1)S(1)}, u32[]{:S(2)}, u32[]{:S(2)}) collective-permute-start(bf16[176,1280]{1,0:T(8,128)(2,1)S(1)} %get-tuple-element.28.refs_5_), channel_id=1, source_target_pairs={{0,2},{1,3},{2,0},{3,1},{4,6},{5,7},{6,4},{7,5},{8,10},{9,11},{10,... | collective-permute-start | bytes 1351688 | tf_op jit(solution)/shard_map/ppermute | solution.py:327
  34.8 6.1 %collective-permute-start.18 = (bf16[48,1280]{1,0:T(8,128)(2,1)S(1)}, bf16[48,1280]{1,0:T(8,128)(2,1)S(1)}, u32[]{:S(2)}, u32[]{:S(2)}) collective-permute-start(bf16[48,1280]{1,0:T(8,128)(2,1)S(1)} %slice.15), channel_id=1, source_target_pairs={{0,1},{1,0},{2,3},{3,2},{4,5},{5,4},{6,7},{7,6},{8,9},{9,8},{10,11... | collective-permute-start | bytes 368648 | tf_op jit(solution)/shard_map/ppermute | solution.py:332
  39.9 1.3 %collective-permute-start.15 = (bf16[48,1280]{1,0:T(8,128)(2,1)S(1)}, bf16[48,1280]{1,0:T(8,128)(2,1)S(1)}, u32[]{:S(2)}, u32[]{:S(2)}) collective-permute-start(bf16[48,1280]{1,0:T(8,128)(2,1)S(1)} %collective-permute-done.7.refs_1_.refs_4_), channel_id=1, source_target_pairs={{0,1},{1,0},{2,3},{3,2},{4,5},{5,4},{6,7},{7,6},{8,9},{9,8},{10,11... | collective-permute-start | bytes 368648 | tf_op jit(solution)/shard_map/ppermute | solution.py:332
  40.1 3.9 %collective-permute-start.13 = (bf16[96,1280]{1,0:T(8,128)(2,1)S(1)}, bf16[96,1280]{1,0:T(8,128)(2,1)S(1)}, u32[]{:S(2)}, u32[]{:S(2)}) collective-permute-start(bf16[96,1280]{1,0:T(8,128)(2,1)S(1)} %slice.12), channel_id=1, source_target_pairs={{0,1},{1,0},{2,3},{3,2},{4,5},{5,4},{6,7},{7,6},{8,9},{9,8},{10,11... | collective-permute-start | bytes 737288 | tf_op jit(solution)/shard_map/ppermute | solution.py:332
  40.6 3.4 %collective-permute-start.17 = (bf16[96,1280]{1,0:T(8,128)(2,1)S(1)}, bf16[96,1280]{1,0:T(8,128)(2,1)S(1)}, u32[]{:S(2)}, u32[]{:S(2)}) collective-permute-start(bf16[96,1280]{1,0:T(8,128)(2,1)S(1)} %slice.14), channel_id=1, source_target_pairs={{0,1},{1,0},{2,3},{3,2},{4,5},{5,4},{6,7},{7,6},{8,9},{9,8},{10,11... | collective-permute-start | bytes 737288 | tf_op jit(solution)/shard_map/ppermute | solution.py:332
  40.9 3.0 %collective-permute-start.14 = (bf16[80,1280]{1,0:T(8,128)(2,1)S(1)}, bf16[80,1280]{1,0:T(8,128)(2,1)S(1)}, u32[]{:S(2)}, u32[]{:S(2)}) collective-permute-start(bf16[80,1280]{1,0:T(8,128)(2,1)S(1)} %slice.13), channel_id=1, source_target_pairs={{0,1},{1,0},{2,3},{3,2},{4,5},{5,4},{6,7},{7,6},{8,9},{9,8},{10,11... | collective-permute-start | bytes 614408 | tf_op jit(solution)/shard_map/ppermute | solution.py:332
  41.3 2.7 %collective-permute-start.16 = (bf16[56,1280]{1,0:T(8,128)(2,1)S(1)}, bf16[56,1280]{1,0:T(8,128)(2,1)S(1)}, u32[]{:S(2)}, u32[]{:S(2)}) collective-permute-start(bf16[56,1280]{1,0:T(8,128)(2,1)S(1)} %collective-permute-done.before_ref.behind_ref.refs_2_), channel_id=1, source_target_pairs={{0,1},{1,0},{2,3},{3,2},{4,5},{5,4},{6,7},{7,6},{8,9},{9,8},{10,11... | collective-permute-start | bytes 430088 | tf_op jit(solution)/shard_map/ppermute | solution.py:332
  46.5 2.4 %collective-permute-start.19 = (bf16[176,1280]{1,0:T(8,128)(2,1)S(1)}, bf16[176,1280]{1,0:T(8,128)(2,1)S(1)}, u32[]{:S(2)}, u32[]{:S(2)}) collective-permute-start(bf16[176,1280]{1,0:T(8,128)(2,1)S(1)} %collective-permute-done.2.refs_0_), channel_id=1, source_target_pairs={{0,1},{1,0},{2,3},{3,2},{4,5},{5,4},{6,7},{7,6},{8,9},{9,8},{10,11... | collective-permute-start | bytes 1351688 | tf_op jit(solution)/shard_map/ppermute | solution.py:332

commit v2 on v1

--- a/solution.py
+++ b/solution.py
@@ -11,9 +11,8 @@
 GROUP = 8
 LANES = 128
 EPS = 1e-06
-VMEM_LIMIT = 16 * 1024 * 1024
-EARLY = 4
-PIECE = 96
+VMEM_LIMIT = 32 * 1024 * 1024
+K = {'early': 8, 'piece': 96, 'pieceA': 64, 'bsplit': 0, 'csplit': 0, 'A2': 'edges', 'B': 'X', 'C1': None, 'D': None, 'swA': 'X', 'swB': 'X', 'swD': 'X', 'z': 2, 'y': 2}
 BF16 = jnp.bfloat16
 F32 = jnp.float32
 
@@ -163,29 +162,40 @@
     return jnp.where(core == 1, other, passed), jnp.where(core == 1, passed, other)
 
 
+def ends_kernel(x_ref, sides_ref, pair_ref, cross_ref):
+    rows, cols, _ = x_ref.shape
+    lefts, rights = halves(sides_ref, rows, slice(None))
+    odd = lax.rem(lax.axis_index("rows"), 2) == 1
+
+    for ref, at in ((pair_ref, (0, rows - 1)), (cross_ref, (rows - 1, 0))):
+        ref[:cols, :] = jnp.where(odd, x_ref[at[0]].astype(F32), x_ref[at[1]].astype(F32)).astype(BF16)
+        ends = [
+            jnp.where(odd, column[at[0] : at[0] + 1], column[at[1] : at[1] + 1]) for column in (lefts, rights)
+        ]
+        ref[cols:, :] = jnp.concatenate(ends, axis=0).astype(BF16)
+
+
 def sides_kernel(
-    x_ref, sides_ref, taps_ref, vec_ref, near_ref, far_ref, top_ref, bottom_ref, lefts, rights, mixed
+    x_ref, sides_ref, taps_ref, vec_ref, *refs
 ):
     rows, cols, width = x_ref.shape
     place = lax.broadcasted_iota(jnp.int32, (GROUP, LANES), 0)
+    *outs, lefts, rights, mixed = refs
     inner = rows - 2
     half = inner * GROUP
     lefts[...], rights[...] = halves(sides_ref, rows, slice(None))
-    for ref, at in ((top_ref, 0), (bottom_ref, rows - 1)):
-        ref[:cols, :] = x_ref[at]
-        ends = jnp.concatenate([lefts[at : at + 1], rights[at : at + 1]], axis=0)
-        ref[cols:, :] = ends.astype(BF16)
-
     def tile(lanes):
         def near(i):
             x = x_ref[i, :, lanes].astype(F32)
-            l = jnp.where(place == 0, lefts[pl.ds(i, 1), lanes], pltpu.roll(x, 1, 0)[:GROUP])
-            return l, x[:GROUP], pltpu.roll(x, cols - 1, 0)[:GROUP]
+            here, both = x[:GROUP], x[: 2 * GROUP]
+            l = jnp.where(place == 0, lefts[pl.ds(i, 1), lanes], pltpu.roll(here, 1, 0))
+            return l, here, pltpu.roll(both, 2 * GROUP - 1, 0)[:GROUP]
 
         def far(i):
             x = x_ref[i, :, lanes].astype(F32)
-            r = jnp.where(place == GROUP - 1, rights[pl.ds(i, 1), lanes], pltpu.roll(x, cols - 1, 0)[cols - GROUP :])
-            return pltpu.roll(x, 1, 0)[cols - GROUP :], x[cols - GROUP :], r
+            here, both = x[cols - GROUP :], x[cols - 2 * GROUP :]
+            r = jnp.where(place == GROUP - 1, rights[pl.ds(i, 1), lanes], pltpu.roll(here, GROUP - 1, 0))
+            return pltpu.roll(both, 1, 0)[GROUP:], here, r
 
         def emit_near(i, value):
             mixed[pl.ds((i - 1) * GROUP, GROUP), lanes] = value
@@ -198,17 +208,22 @@
 
     each_tile(width, tile)
     gain, nbias = vec_ref.at[1], vec_ref.at[2]
-    normalize(mixed, half, gain, nbias, near_ref)
-    normalize(mixed.at[pl.ds(half, half)], half, gain, nbias, far_ref)
-
-
-def edges_kernel(x_ref, sides_ref, up_ref, down_ref, taps_ref, vec_ref, out_ref, mixed):
+    base = 0
+    for ref in outs:
+        count = ref.shape[0]
+        normalize(mixed.at[pl.ds(base, count)], count, gain, nbias, ref)
+        base += count
+
+
+def edges_kernel(x_ref, sides_ref, pair_ref, cross_ref, taps_ref, vec_ref, out_ref, mixed):
     rows, cols, width = x_ref.shape
     place = lax.broadcasted_iota(jnp.int32, (cols, LANES), 0)
+    odd = lax.rem(lax.axis_index("rows"), 2) == 1
 
     def tile(lanes):
         lefts, rights = halves(sides_ref, rows, lanes)
-        up, down = up_ref[:, lanes].astype(F32), down_ref[:, lanes].astype(F32)
+        pair, cross = pair_ref[:, lanes].astype(F32), cross_ref[:, lanes].astype(F32)
+        up, down = jnp.where(odd, pair, cross), jnp.where(odd, cross, pair)
 
         def cells(i):
             if i < 0:
@@ -247,25 +262,25 @@
     weight = w_ref[...].reshape(total, width)
     bias = jnp.concatenate([b_ref[pl.ds(t, 1), :].astype(F32) for t in range(3)], axis=1)
     owner = lax.rem(lax.axis_index("cols") + 2 * step, side_count)
-    copies = []
-    for g, (pieces, other, group) in enumerate(plan):
-        rows_of = [parts[ref][pl.ds(at, size), :] for ref, at, size in pieces]
+    side = rows * GROUP
+    for batch in batches_of(len(plan)):
+        pieces = [parts[ref][pl.ds(at, size), :] for g in batch for ref, at, size in plan[g][0]]
         acc = (
             lax.dot_general(
-                jnp.concatenate(rows_of, axis=0),
-                weight,
-                (((1,), (1,)), ((), ())),
-                preferred_element_type=F32,
+                jnp.concatenate(pieces, axis=0), weight, (((1,), (1,)), ((), ())), preferred_element_type=F32
             )
             + bias
         )
-        inner = acc.shape[0] - 2 * GROUP
-        for k in range(0, total, LANES):
-            piece = acc[:, k : k + LANES]
-            span = pl.ds(0, piece.shape[1])
-            sums[g % 2, k // LANES, pl.ds(GROUP, inner), span] = piece[:inner]
-            sums[g % 2, k // LANES, pl.ds(0, GROUP), span] = piece[inner : inner + GROUP]
-            sums[g % 2, k // LANES, pl.ds(inner + GROUP, GROUP), span] = piece[inner + GROUP :]
+        inner = side - 2 * GROUP
+        for n, g in enumerate(batch):
+            for k in range(0, total, LANES):
+                piece = acc[n * side : (n + 1) * side, k : k + LANES]
+                span = pl.ds(0, piece.shape[1])
+                sums[g, k // LANES, pl.ds(GROUP, inner), span] = piece[:inner]
+                sums[g, k // LANES, pl.ds(0, GROUP), span] = piece[inner : inner + GROUP]
+                sums[g, k // LANES, pl.ds(inner + GROUP, GROUP), span] = piece[inner + GROUP :]
+    copies = []
+    for g, (_, other, group) in enumerate(plan):
         position = owner ^ 1 if other else owner
         lane = pl.multiple_of(position * (out_ref.shape[3] // side_count) + group * block, LANES)
         for t in range(3):
@@ -274,7 +289,7 @@
                 lo, hi = start // LANES, (start + HD - 1) // LANES + 1
                 cells = []
                 for j in range(GROUP):
-                    tiles = [sums[g % 2, k, pl.ds(j, rows, stride=GROUP), :] for k in range(lo, hi)]
+                    tiles = [sums[g, k, pl.ds(j, rows, stride=GROUP), :] for k in range(lo, hi)]
                     cell = tiles[0] if len(tiles) == 1 else jnp.concatenate(tiles, axis=1)
                     cells.append(cell[:, start - lo * LANES : start - lo * LANES + HD])
                 blocks[g, t, h] = jnp.concatenate(cells, axis=1).astype(BF16)
@@ -285,6 +300,11 @@
             copies.append(copy)
     for copy in copies:
         copy.wait()
+
+
+def batches_of(count):
+    size = 3 if count % 3 == 0 else 2
+    return [range(at, min(at + size, count)) for at in range(0, count, size)]
 
 
 def project(out, parts, plan, step, weight, bias, rows, side_count, shape):
@@ -299,7 +319,7 @@
         [VMEM] * (count + 2) + ([] if fresh else [HBM]),
         HBM,
         [
-            pltpu.VMEM((2, pl.cdiv(3 * heads * HD, LANES), rows * GROUP, LANES), F32),
+            pltpu.VMEM((len(plan), pl.cdiv(3 * heads * HD, LANES), rows * GROUP, LANES), F32),
             pltpu.VMEM((len(plan), 3, heads, rows, GROUP * HD), BF16),
             pltpu.SemaphoreType.DMA((len(plan), 3)),
         ],
@@ -314,7 +334,7 @@
     wide = cols - 2 * GROUP
     inner = rows - 2
     half = inner * GROUP
-    early = EARLY
+    early = K['early']
     few = early * wide
     two = 2 * GROUP
     steps = range(1, chips)
@@ -331,8 +351,9 @@
     def swap(value):
         return lax.ppermute(value, "cols", [(q, q ^ 1) for q in range(side_count)])
 
-    def shift(value, axis, count, step):
-        return lax.ppermute(value, axis, [(i, i + step) for i in range(count) if 0 <= i + step < count])
+    def exchange(value, start):
+        pairs = [(i, i + 1) for i in range(start, up_count - 1, 2)]
+        return lax.ppermute(value, "rows", pairs + [(j, i) for i, j in pairs])
 
     def after(values, others):
         joined = lax.optimization_barrier((*values, *others))
@@ -378,18 +399,39 @@
         )(beside, got_first[0], got_first[-1], second)
     )
 
-    near, far, top, bottom = call(
+    def cuts(size):
+        return [size, half - size] if size else [half]
+
+    sizes = cuts(K["bsplit"]) + cuts(K["csplit"])
+    pair, cross = call(
+        ends_kernel,
+        "ends",
+        [array(cols + 2, width)] * 2,
+        [VMEM] * 2,
+        [VMEM] * 2,
+        [],
+    )(x, sides)
+    parts = call(
         sides_kernel,
         "sides",
-        [array(half, width)] * 2 + [array(cols + 2, width)] * 2,
+        [array(size, width) for size in sizes],
         [VMEM] * 4,
-        [VMEM] * 4,
+        [VMEM] * len(sizes),
         [pltpu.VMEM((rows, width), F32)] * 2 + [pltpu.VMEM((2 * half, width), F32)],
     )(x, sides, taps, vectors)
-    up = shift(bottom, "rows", up_count, 1)
-    down = shift(top, "rows", up_count, -1)
-    got_near = across(near)
-    up, down = after((up, down), got_second)
+    count = len(cuts(K["bsplit"]))
+    near, far = parts[:count], parts[count:]
+    got_near = [across(v) for v in near]
+    got_far = [across(v) for v in far]
+    marks = {"A2": got_second, "B": sum(got_near, []), "C1": got_far[0]}
+
+    def hold(place, values):
+        others = sum([marks[k] for k in marks if K[k] == place], [])
+        return after(values, others) if others else list(values)
+
+    pair, cross = hold("up", (pair, cross))
+    pair, cross = exchange(pair, 0), exchange(cross, 1)
+    pair, cross = hold("edges", (pair, cross))
     edge = call(
         edges_kernel,
         "edges",
@@ -397,55 +439,71 @@
         [VMEM] * 6,
         VMEM,
         [pltpu.VMEM((2 * cols, width), F32)],
-    )(x, sides, up, down, taps, vectors)
+    )(x, sides, pair, cross, taps, vectors)
     got_edge = across(edge)
-    got_far = across(far)
+    marks["D"] = got_edge
 
     shape = (3, qkv_weight.shape[2] // HD, rows, side_count * cols * HD)
     weight = jnp.swapaxes(qkv_weight, 1, 2)
     run = functools.partial(project, weight=weight, bias=qkv_bias, rows=rows, side_count=side_count, shape=shape)
 
-    def cut(value):
-        return [value[at : at + PIECE] for at in range(0, value.shape[0], PIECE)]
-
-    def plan(groups, other):
+    def whole(values):
+        return [(value, 0, value.shape[0]) for value in values]
+
+    def groups_of(near, first, second, edge, far, other):
+        return [
+            (whole(near) + [(edge, 0, two)], other, 0),
+            ([(first, 0, few)] + whole(second) + [(edge, two, two)], other, 1),
+            (whole(far) + [(edge, 2 * two, two)], other, 2),
+        ]
+
+    def step_on(out, groups, step):
         arrays, entries = [], []
-        for group, pieces in groups:
+        for pieces, other, group in groups:
             entry = []
             for value, at, size in pieces:
                 entry.append((len(arrays), at, size))
                 arrays.append(value)
             entries.append((tuple(entry), other, group))
-        return arrays, entries
-
-    def whole(values):
-        return [(value, 0, value.shape[0]) for value in values]
-
-    def groups_of(near, first, second, edge, far):
-        return [
-            (0, whole(near) + [(edge, 0, two)]),
-            (1, [(first, 0, few)] + whole(second) + [(edge, two, two)]),
-            (2, whole(far) + [(edge, 2 * two, two)]),
-        ]
-
-    def step_on(out, groups, other, step):
-        arrays, entries = plan(groups, other)
         return run(out, arrays, entries, step)
 
-    out = step_on(None, groups_of([near], first, [second], edge, [far]), 0, 0)
-    other_edge = edge
-    theirs = groups_of([swap(near)], swap(first), [swap(second)], swap(other_edge), [swap(far)])
-    out = step_on(out, theirs, 1, 0)
+    (late,) = hold("eswap", (edge,))
+    (held,) = hold("X", (first,))
+    out = step_on(
+        None,
+        groups_of(near, held, [second], edge, far, 0)
+        + groups_of([swap(v) for v in near], swap(first), [swap(second)], swap(late), [swap(v) for v in far], 1),
+        0,
+    )
     for step in steps:
-        mine = [v[step - 1] for v in (got_near, got_first, got_second, got_edge)]
-        *mine, out = lax.optimization_barrier((*mine, out))
-        near, first, second, edge = mine
-        other = [swap(v) for v in cut(near)], swap(first), [swap(v) for v in cut(second)], swap(edge)
-        out = step_on(out, groups_of([near], first, [second], edge, [])[:2], 0, chips - step)
-        out = step_on(out, groups_of(*other, [])[:2], 1, chips - step)
-        far, out = lax.optimization_barrier((got_far[step - 1], out))
-        out = step_on(out, groups_of([], first, [], edge, [far])[2:], 0, chips - step)
-        out = step_on(out, groups_of([], first, [], other[3], [swap(far)])[2:], 1, chips - step)
+        at = step - 1
+        pick = dict(
+            swA=[got_first[at], got_second[at]], swB=[v[at] for v in got_near], swD=[got_edge[at]]
+        )
+        for key in pick:
+            if K[key] == "X":
+                *pick[key], out = lax.optimization_barrier((*pick[key], out))
+        c1 = [v[at] for v in got_far]
+        if K["C1"] == "dswap":
+            pick["swD"] = after(pick["swD"], c1[:1])
+        (got1, got2), gotb, (gote,) = pick["swA"], pick["swB"], pick["swD"]
+        other_near = [swap(v[p : p + K["piece"]]) for v in gotb for p in range(0, v.shape[0], K["piece"])]
+        other1, other2, othere = swap(got1), swap(got2), swap(gote)
+        mine = groups_of(gotb, got1, [got2], gote, [], 0)[:2]
+        theirs = groups_of(other_near, other1, [other2], othere, [], 1)[:2]
+        if K["y"] == 2:
+            out = step_on(out, mine, chips - step)
+            out = step_on(out, theirs, chips - step)
+        else:
+            out = step_on(out, mine + theirs, chips - step)
+        *c1, out = lax.optimization_barrier((*c1, out))
+        last = groups_of([], got1, [], gote, c1, 0)[2:]
+        other = groups_of([], got1, [], othere, [swap(v) for v in c1], 1)[2:]
+        if K["z"] == 2:
+            out = step_on(out, last, chips - step)
+            out = step_on(out, other, chips - step)
+        else:
+            out = step_on(out, last + other, chips - step)
     return out
 
 

time: 50.9 us -> 46.6 us (0.916)
  the two profiles are of different devices: /device:TPU:15 before, /device:TPU:25 now
where the time goes in v2:
time: 46.6 us; the launch traced here: 46.5 us
  Pallas kernels  19.1 us (41%)
  starting transfers between devices  17 us (36%)
  waiting for transfers between devices  10.2 us (22%)
    pallas_call x5, Pallas kernels, project(): call(functools.partial(project_kernel, rows, plan, count, fresh, step, si...  13 us
    ppermute x12, starting transfers between devices, swap(): return lax.ppermute(value, 'cols', [(q, q ^ 1) for q in range(side_count)])  9.34 us
    ppermute x5, waiting for transfers between devices, across(): lax.ppermute(value, 'cols', [(q, (q + 2 * step) % side_count) for q in ra...  5.26 us
    ppermute x5, starting transfers between devices, across(): lax.ppermute(value, 'cols', [(q, (q + 2 * step) % side_count) for q in ra...  4.34 us
    ppermute x2, starting transfers between devices, exchange(): return lax.ppermute(value, 'rows', pairs + [(j, i) for i, j in pairs])  3.31 us
    ppermute x2, waiting for transfers between devices, exchange(): return lax.ppermute(value, 'rows', pairs + [(j, i) for i, j in pairs])  3.16 us
    pallas_call x1, Pallas kernels, local(): call(sides_kernel, 'sides', [array(size, width) for size in sizes], [VMEM...  2.33 us
    pallas_call x1, Pallas kernels, local(): call(functools.partial(first_kernel, early), 'first', [array(few + rows,...  2.16 us
  transfers between devices with their start and end apart: 19, of which 6 were waited for; matrix products, arithmetic and copies ran while one was open for 0% of the time, Pallas kernels for 33%

profile of v2, /device:TPU:25, one launch (start us, length us, event | category | flops | bytes accessed | tf_op | source)
XLA Modules:
  0.0 46.5 jit_solution(12151193974926314822)
XLA Ops:
  0.0 0.0 copy-start.1
  0.0 0.0 copy-start
  0.0 2.2 %first.1 = (bf16[88,1280]{1,0:T(8,128)(2,1)S(1)}, bf16[24,1280]{1,0:T(8,128)(2,1)S(1)}, bf16[24,24,1280]{2,1,0:T(8,128)(2,1)S(1)}, f32[3,3,1280]{2,1,0:T(4,128)S(1)}, f32[3,1,1280]{2,1,0:T(1,128)S(1)}) custom-call(bf16[24,24,1280]{2,1,0:T(8,128)(2,1)} %x_hbm.1, f32[3,3,1280]{2,1,0:T(4,128)} %taps_hbm.1, f32[1280]{0:T(1024)} %cbias_hbm.1, f32[1280]{0:T(1024)} %gain_hbm.1, ...), custom_call_target="tpu_custom_call" | custom-call | flops 1024 | bytes 1024 | tf_op jit(solution)/shard_map/first/pallas_call | solution.py:365
  2.2 1.3 %collective-permute-start = (bf16[88,1280]{1,0:T(8,128)(2,1)S(1)}, bf16[88,1280]{1,0:T(8,128)(2,1)S(1)}, u32[]{:S(2)}, u32[]{:S(2)}) collective-permute-start(bf16[88,1280]{1,0:T(8,128)(2,1)S(1)} %get-tuple-element.37.refs_2_), channel_id=1, source_target_pairs={{0,2},{1,3},{2,0},{3,1},{4,6},{5,7},{6,4},{7,5},{8,10},{9,11},{10,... | collective-permute-start | bytes 675848 | tf_op jit(solution)/shard_map/ppermute | solution.py:347
  3.5 0.9 %second.1._.refs_3_ = bf16[112,1280]{1,0:T(8,128)(2,1)S(1)} custom-call(bf16[24,24,1280]{2,1,0:T(8,128)(2,1)S(1)} %get-tuple-element.26.x_ref, f32[3,3,1280]{2,1,0:T(4,128)S(1)} %get-tuple-element.29.taps_ref, f32[3,1,1280]{2,1,0:T(1,128)S(1)} %get-tuple-element.30.vec_ref), custom_call_target="tpu_custom_call" | custom-call | flops 1024 | bytes 1024 | tf_op jit(solution)/shard_map/second/pallas_call | solution.py:381
  4.4 0.3 collective-permute-start.4
  4.7 3.9 %collective-permute-done.before_ref.behind_ref.refs_2_ = bf16[88,1280]{1,0:T(8,128)(2,1)S(1)} collective-permute-done((bf16[88,1280]{1,0:T(8,128)(2,1)S(1)}, bf16[88,1280]{1,0:T(8,128)(2,1)S(1)}, u32[]{:S(2)}, u32[]{:S(2)}) %collective-permute-start) | collective-permute-done | bytes 225312 | tf_op jit(solution)/shard_map/ppermute | solution.py:347
  8.7 2.8 %collective-permute-start.1 = (bf16[48,1280]{1,0:T(8,128)(2,1)S(1)}, bf16[48,1280]{1,0:T(8,128)(2,1)S(1)}, u32[]{:S(2)}, u32[]{:S(2)}) collective-permute-start(bf16[48,1280]{1,0:T(8,128)(2,1)S(1)} %relay.1), channel_id=1, source_target_pairs={{0,1},{1,0},{2,3},{3,2},{4,5},{5,4},{6,7},{7,6},{8,9},{9,8},{10,11... | collective-permute-start | bytes 368648 | tf_op jit(solution)/shard_map/ppermute | solution.py:352
  11.4 1.0 %collective-permute-done.1.sides_ref = bf16[48,1280]{1,0:T(8,128)(2,1)S(1)} collective-permute-done((bf16[48,1280]{1,0:T(8,128)(2,1)S(1)}, bf16[48,1280]{1,0:T(8,128)(2,1)S(1)}, u32[]{:S(2)}, u32[]{:S(2)}) %collective-permute-start.1) | collective-permute-done | bytes 122912 | tf_op jit(solution)/shard_map/ppermute | solution.py:352
  12.4 2.3 %sides.1 = (bf16[176,1280]{1,0:T(8,128)(2,1)S(1)}, bf16[176,1280]{1,0:T(8,128)(2,1)S(1)}) custom-call(bf16[24,24,1280]{2,1,0:T(8,128)(2,1)S(1)} %get-tuple-element.26.x_ref, bf16[48,1280]{1,0:T(8,128)(2,1)S(1)} %collective-permute-done.1.sides_ref, f32[3,3,1280]{2,1,0:T(4,128)S(1)} %get-tuple-element.29.taps_ref, f32[3,1,1280]{2,1,0:T(1,128)S(1)} %get-tuple-element.30.vec_ref), custom_call_target="tpu_custom_call" | custom-call | flops 1024 | bytes 1024 | tf_op jit(solution)/shard_map/sides/pallas_call | solution.py:414
  14.7 1.3 %collective-permute-start.3 = (bf16[176,1280]{1,0:T(8,128)(2,1)S(1)}, bf16[176,1280]{1,0:T(8,128)(2,1)S(1)}, u32[]{:S(2)}, u32[]{:S(2)}) collective-permute-start(bf16[176,1280]{1,0:T(8,128)(2,1)S(1)} %get-tuple-element.32.refs_0_), channel_id=1, source_target_pairs={{0,2},{1,3},{2,0},{3,1},{4,6},{5,7},{6,4},{7,5},{8,10},{9,11},{10,... | collective-permute-start | bytes 1351688 | tf_op jit(solution)/shard_map/ppermute | solution.py:347
  16.0 0.1 ends.1
  16.1 1.3 %collective-permute-start.5 = (bf16[26,1280]{1,0:T(8,128)(2,1)S(1)}, bf16[26,1280]{1,0:T(8,128)(2,1)S(1)}, u32[]{:S(2)}, u32[]{:S(2)}) collective-permute-start(bf16[26,1280]{1,0:T(8,128)(2,1)S(1)} %get-tuple-element.33), channel_id=1, source_target_pairs={{0,4},{8,12},{16,20},{24,28},{4,0},{12,8},{20,16},{28,24},{1,5},{9... | collective-permute-start | bytes 199688 | tf_op jit(solution)/shard_map/ppermute | solution.py:356
  17.4 0.9 %collective-permute-start.11 = (bf16[176,1280]{1,0:T(8,128)(2,1)S(1)}, bf16[176,1280]{1,0:T(8,128)(2,1)S(1)}, u32[]{:S(2)}, u32[]{:S(2)}) collective-permute-start(bf16[176,1280]{1,0:T(8,128)(2,1)S(1)} %get-tuple-element.31.refs_5_), channel_id=1, source_target_pairs={{0,1},{1,0},{2,3},{3,2},{4,5},{5,4},{6,7},{7,6},{8,9},{9,8},{10,11... | collective-permute-start | bytes 1351688 | tf_op jit(solution)/shard_map/ppermute | solution.py:352
  18.3 0.0 collective-permute-start.7
  18.3 0.0 collective-permute-done.4.refs_3_
  18.3 2.0 %collective-permute-start.6 = (bf16[26,1280]{1,0:T(8,128)(2,1)S(1)}, bf16[26,1280]{1,0:T(8,128)(2,1)S(1)}, u32[]{:S(2)}, u32[]{:S(2)}) collective-permute-start(bf16[26,1280]{1,0:T(8,128)(2,1)S(1)} %get-tuple-element.34), channel_id=1, source_target_pairs={{4,8},{12,16},{20,24},{8,4},{16,12},{24,20},{5,9},{13,17},{21,25},... | collective-permute-start | bytes 199688 | tf_op jit(solution)/shard_map/ppermute | solution.py:356
  20.3 0.0 collective-permute-done.5.pair_ref
  20.3 0.9 %collective-permute-start.10 = (bf16[112,1280]{1,0:T(8,128)(2,1)S(1)}, bf16[112,1280]{1,0:T(8,128)(2,1)S(1)}, u32[]{:S(2)}, u32[]{:S(2)}) collective-permute-start(bf16[112,1280]{1,0:T(8,128)(2,1)S(1)} %second.1._.refs_3_), channel_id=1, source_target_pairs={{0,1},{1,0},{2,3},{3,2},{4,5},{5,4},{6,7},{7,6},{8,9},{9,8},{10,11... | collective-permute-start | bytes 860168 | tf_op jit(solution)/shard_map/ppermute | solution.py:352
  21.2 3.2 %collective-permute-done.6.cross_ref = bf16[26,1280]{1,0:T(8,128)(2,1)S(1)} collective-permute-done((bf16[26,1280]{1,0:T(8,128)(2,1)S(1)}, bf16[26,1280]{1,0:T(8,128)(2,1)S(1)}, u32[]{:S(2)}, u32[]{:S(2)}) %collective-permute-start.6) | collective-permute-done | bytes 66592 | tf_op jit(solution)/shard_map/ppermute | solution.py:356
  24.4 1.7 %collective-permute-start.9 = (bf16[88,1280]{1,0:T(8,128)(2,1)S(1)}, bf16[88,1280]{1,0:T(8,128)(2,1)S(1)}, u32[]{:S(2)}, u32[]{:S(2)}) collective-permute-start(bf16[88,1280]{1,0:T(8,128)(2,1)S(1)} %get-tuple-element.37.refs_2_), channel_id=1, source_target_pairs={{0,1},{1,0},{2,3},{3,2},{4,5},{5,4},{6,7},{7,6},{8,9},{9,8},{10,11... | collective-permute-start | bytes 675848 | tf_op jit(solution)/shard_map/ppermute | solution.py:352
  26.1 0.7 %edges.1.refs_1_.refs_4_.refs_6_ = bf16[48,1280]{1,0:T(8,128)(2,1)S(1)} custom-call(bf16[24,24,1280]{2,1,0:T(8,128)(2,1)S(1)} %get-tuple-element.26.x_ref, bf16[48,1280]{1,0:T(8,128)(2,1)S(1)} %collective-permute-done.1.sides_ref, bf16[26,1280]{1,0:T(8,128)(2,1)S(1)} %collective-permute-done.5.pair_ref, ...), custom_call_target="tpu_custom_call" | custom-call | flops 1024 | bytes 1024 | tf_op jit(solution)/shard_map/edges/pallas_call | solution.py:435
  26.7 0.5 collective-permute-done.9.refs_9_
  27.2 0.4 collective-permute-start.8
  27.5 0.0 collective-permute-done.10.refs_10_
  27.5 0.3 collective-permute-start.14
  27.8 0.0 collective-permute-done.3.refs_0_
  27.8 1.2 %collective-permute-start.2 = (bf16[176,1280]{1,0:T(8,128)(2,1)S(1)}, bf16[176,1280]{1,0:T(8,128)(2,1)S(1)}, u32[]{:S(2)}, u32[]{:S(2)}) collective-permute-start(bf16[176,1280]{1,0:T(8,128)(2,1)S(1)} %get-tuple-element.31.refs_5_), channel_id=1, source_target_pairs={{0,2},{1,3},{2,0},{3,1},{4,6},{5,7},{6,4},{7,5},{8,10},{9,11},{10,... | collective-permute-start | bytes 1351688 | tf_op jit(solution)/shard_map/ppermute | solution.py:347
  29.0 0.0 collective-permute-done.8.refs_8_.refs_11_.refs_13_
  29.0 0.0 collective-permute-done.11.refs_12_
  29.0 0.0 collective-permute-done.7.refs_7_
  29.0 0.0 copy-done.1
  29.0 0.0 copy-done
  29.0 4.9 %project.5.refs_7_ = bf16[3,4,24,7680]{3,2,1,0:T(8,128)(2,1)} custom-call(bf16[176,1280]{1,0:T(8,128)(2,1)S(1)} %get-tuple-element.32.refs_0_, bf16[48,1280]{1,0:T(8,128)(2,1)S(1)} %edges.1.refs_1_.refs_4_.refs_6_, bf16[88,1280]{1,0:T(8,128)(2,1)S(1)} %get-tuple-element.37.refs_2_, bf16[112,1280]{1,0:T(8,128)(2,1)S(1)} %second.1._.refs_3_, ...), custom_call_target="tpu_custom_call" | custom-call | flops 1024 | bytes 1024 | tf_op jit(solution)/shard_map/project/pallas_call | solution.py:315
  33.9 0.0 collective-permute-done.14.refs_1_.refs_4_
  33.9 0.8 %collective-permute-start.15 = (bf16[48,1280]{1,0:T(8,128)(2,1)S(1)}, bf16[48,1280]{1,0:T(8,128)(2,1)S(1)}, u32[]{:S(2)}, u32[]{:S(2)}) collective-permute-start(bf16[48,1280]{1,0:T(8,128)(2,1)S(1)} %collective-permute-done.14.refs_1_.refs_4_), channel_id=1, source_target_pairs={{0,1},{1,0},{2,3},{3,2},{4,5},{5,4},{6,7},{7,6},{8,9},{9,8},{10,11... | collective-permute-start | bytes 368648 | tf_op jit(solution)/shard_map/ppermute | solution.py:352
  34.7 0.1 collective-permute-start.17
  34.8 0.5 %collective-permute-start.12 = (bf16[96,1280]{1,0:T(8,128)(2,1)S(1)}, bf16[96,1280]{1,0:T(8,128)(2,1)S(1)}, u32[]{:S(2)}, u32[]{:S(2)}) collective-permute-start(bf16[96,1280]{1,0:T(8,128)(2,1)S(1)} %slice.6), channel_id=1, source_target_pairs={{0,1},{1,0},{2,3},{3,2},{4,5},{5,4},{6,7},{7,6},{8,9},{9,8},{10,11... | collective-permute-start | bytes 737288 | tf_op jit(solution)/shard_map/ppermute | solution.py:352
  35.3 0.1 collective-permute-start.16
  35.4 0.3 collective-permute-done.15.refs_2_.refs_5_.refs_1_
  35.7 0.4 collective-permute-start.13
  36.1 2.3 %project.6.refs_8_ = bf16[3,4,24,7680]{3,2,1,0:T(8,128)(2,1)} custom-call(bf16[176,1280]{1,0:T(8,128)(2,1)S(1)} %collective-permute-done.3.refs_0_, bf16[48,1280]{1,0:T(8,128)(2,1)S(1)} %collective-permute-done.14.refs_1_.refs_4_, bf16[88,1280]{1,0:T(8,128)(2,1)S(1)} %collective-permute-done.before_ref.behind_ref.refs_2_, ...), custom_call_target="tpu_custom_call", output_to_operand_aliasing={{}: (7, {})} | custom-call | flops 1024 | bytes 1024 | tf_op jit(solution)/shard_map/project/pallas_call | solution.py:315
  38.3 0.0 collective-permute-done.13.refs_1_
  38.3 0.0 collective-permute-done.16.refs_3_
  38.4 0.0 collective-permute-done.12.refs_0_
  38.4 0.0 collective-permute-done.17.refs_4_
  38.4 2.3 %project.7.refs_4_ = bf16[3,4,24,7680]{3,2,1,0:T(8,128)(2,1)} custom-call(bf16[96,1280]{1,0:T(8,128)(2,1)S(1)} %collective-permute-done.12.refs_0_, bf16[80,1280]{1,0:T(8,128)(2,1)S(1)} %collective-permute-done.13.refs_1_, bf16[48,1280]{1,0:T(8,128)(2,1)S(1)} %collective-permute-done.15.refs_2_.refs_5_.refs_1_, ...), custom_call_target="tpu_custom_call", output_to_operand_aliasing={{}: (8, {})} | custom-call | flops 1024 | bytes 1024 | tf_op jit(solution)/shard_map/project/pallas_call | solution.py:315
  40.7 1.3 %collective-permute-done.2.refs_0_ = bf16[176,1280]{1,0:T(8,128)(2,1)S(1)} collective-permute-done((bf16[176,1280]{1,0:T(8,128)(2,1)S(1)}, bf16[176,1280]{1,0:T(8,128)(2,1)S(1)}, u32[]{:S(2)}, u32[]{:S(2)}) %collective-permute-start.2) | collective-permute-done | bytes 450592 | tf_op jit(solution)/shard_map/ppermute | solution.py:347
  42.0 1.0 %collective-permute-start.18 = (bf16[176,1280]{1,0:T(8,128)(2,1)S(1)}, bf16[176,1280]{1,0:T(8,128)(2,1)S(1)}, u32[]{:S(2)}, u32[]{:S(2)}) collective-permute-start(bf16[176,1280]{1,0:T(8,128)(2,1)S(1)} %collective-permute-done.2.refs_0_), channel_id=1, source_target_pairs={{0,1},{1,0},{2,3},{3,2},{4,5},{5,4},{6,7},{7,6},{8,9},{9,8},{10,11... | collective-permute-start | bytes 1351688 | tf_op jit(solution)/shard_map/ppermute | solution.py:352
  42.9 1.8 %project.8.refs_4_ = bf16[3,4,24,7680]{3,2,1,0:T(8,128)(2,1)} custom-call(bf16[176,1280]{1,0:T(8,128)(2,1)S(1)} %collective-permute-done.2.refs_0_, bf16[48,1280]{1,0:T(8,128)(2,1)S(1)} %collective-permute-done.14.refs_1_.refs_4_, bf16[3,320,1280]{2,1,0:T(8,128)(2,1)S(1)} %bitcast.4, bf16[3,320]{1,0:T(4,128)(2,1)S(1)} %copy-done.1, ...), custom_call_target="tpu_custom_call", output_to_operand_aliasing={{}: (4, {})} | custom-call | flops 1024 | bytes 1024 | tf_op jit(solution)/shard_map/project/pallas_call | solution.py:315
  44.7 0.0 collective-permute-done.18.refs_0_
  44.7 1.8 %project.9 = bf16[3,4,24,7680]{3,2,1,0:T(8,128)(2,1)} custom-call(bf16[176,1280]{1,0:T(8,128)(2,1)S(1)} %collective-permute-done.18.refs_0_, bf16[48,1280]{1,0:T(8,128)(2,1)S(1)} %collective-permute-done.15.refs_2_.refs_5_.refs_1_, bf16[3,320,1280]{2,1,0:T(8,128)(2,1)S(1)} %bitcast.5, bf16[3,320]{1,0:T(4,128)(2,1)S(1)} %copy-done.1, ...), custom_call_target="tpu_custom_call", output_to_operand_aliasing={{}: (4, {})} | custom-call | flops 1024 | bytes 1024 | tf_op jit(solution)/shard_map/project/pallas_call | solution.py:315
  (3 shorter events, 0.1 us)
Async XLA Ops:
  0.0 29.0 %copy-start.1 = (bf16[3,320]{1,0:T(4,128)(2,1)S(1)}, bf16[3,320]{1,0:T(4,128)(2,1)}, u32[]{:S(2)}) copy-start(bf16[3,320]{1,0:T(4,128)(2,1)} %refs_3_.3) | copy-start | bytes 5764
  0.0 29.0 %copy-start = (bf16[3,1280,320]{1,2,0:T(8,128)(2,1)S(1)}, bf16[3,1280,320]{1,2,0:T(8,128)(2,1)}, u32[]{:S(2)}) copy-start(bf16[3,1280,320]{1,2,0:T(8,128)(2,1)} %param.12) | copy-start | bytes 7372804
  2.2 6.4 %collective-permute-start = (bf16[88,1280]{1,0:T(8,128)(2,1)S(1)}, bf16[88,1280]{1,0:T(8,128)(2,1)S(1)}, u32[]{:S(2)}, u32[]{:S(2)}) collective-permute-start(bf16[88,1280]{1,0:T(8,128)(2,1)S(1)} %get-tuple-element.37.refs_2_), channel_id=1, source_target_pairs={{0,2},{1,3},{2,0},{3,1},{4,6},{5,7},{6,4},{7,5},{8,10},{9,11},{10,... | collective-permute-start | bytes 675848 | tf_op jit(solution)/shard_map/ppermute | solution.py:347
  4.4 14.0 %collective-permute-start.4 = (bf16[112,1280]{1,0:T(8,128)(2,1)S(1)}, bf16[112,1280]{1,0:T(8,128)(2,1)S(1)}, u32[]{:S(2)}, u32[]{:S(2)}) collective-permute-start(bf16[112,1280]{1,0:T(8,128)(2,1)S(1)} %second.1._.refs_3_), channel_id=1, source_target_pairs={{0,2},{1,3},{2,0},{3,1},{4,6},{5,7},{6,4},{7,5},{8,10},{9,11},{10,... | collective-permute-start | bytes 860168 | tf_op jit(solution)/shard_map/ppermute | solution.py:347
  8.7 3.7 %collective-permute-start.1 = (bf16[48,1280]{1,0:T(8,128)(2,1)S(1)}, bf16[48,1280]{1,0:T(8,128)(2,1)S(1)}, u32[]{:S(2)}, u32[]{:S(2)}) collective-permute-start(bf16[48,1280]{1,0:T(8,128)(2,1)S(1)} %relay.1), channel_id=1, source_target_pairs={{0,1},{1,0},{2,3},{3,2},{4,5},{5,4},{6,7},{7,6},{8,9},{9,8},{10,11... | collective-permute-start | bytes 368648 | tf_op jit(solution)/shard_map/ppermute | solution.py:352
  14.7 13.1 %collective-permute-start.3 = (bf16[176,1280]{1,0:T(8,128)(2,1)S(1)}, bf16[176,1280]{1,0:T(8,128)(2,1)S(1)}, u32[]{:S(2)}, u32[]{:S(2)}) collective-permute-start(bf16[176,1280]{1,0:T(8,128)(2,1)S(1)} %get-tuple-element.32.refs_0_), channel_id=1, source_target_pairs={{0,2},{1,3},{2,0},{3,1},{4,6},{5,7},{6,4},{7,5},{8,10},{9,11},{10,... | collective-permute-start | bytes 1351688 | tf_op jit(solution)/shard_map/ppermute | solution.py:347
  16.1 4.3 %collective-permute-start.5 = (bf16[26,1280]{1,0:T(8,128)(2,1)S(1)}, bf16[26,1280]{1,0:T(8,128)(2,1)S(1)}, u32[]{:S(2)}, u32[]{:S(2)}) collective-permute-start(bf16[26,1280]{1,0:T(8,128)(2,1)S(1)} %get-tuple-element.33), channel_id=1, source_target_pairs={{0,4},{8,12},{16,20},{24,28},{4,0},{12,8},{20,16},{28,24},{1,5},{9... | collective-permute-start | bytes 199688 | tf_op jit(solution)/shard_map/ppermute | solution.py:356
  17.4 11.6 %collective-permute-start.11 = (bf16[176,1280]{1,0:T(8,128)(2,1)S(1)}, bf16[176,1280]{1,0:T(8,128)(2,1)S(1)}, u32[]{:S(2)}, u32[]{:S(2)}) collective-permute-start(bf16[176,1280]{1,0:T(8,128)(2,1)S(1)} %get-tuple-element.31.refs_5_), channel_id=1, source_target_pairs={{0,1},{1,0},{2,3},{3,2},{4,5},{5,4},{6,7},{7,6},{8,9},{9,8},{10,11... | collective-permute-start | bytes 1351688 | tf_op jit(solution)/shard_map/ppermute | solution.py:352
  18.3 10.7 %collective-permute-start.7 = (bf16[176,1280]{1,0:T(8,128)(2,1)S(1)}, bf16[176,1280]{1,0:T(8,128)(2,1)S(1)}, u32[]{:S(2)}, u32[]{:S(2)}) collective-permute-start(bf16[176,1280]{1,0:T(8,128)(2,1)S(1)} %get-tuple-element.32.refs_0_), channel_id=1, source_target_pairs={{0,1},{1,0},{2,3},{3,2},{4,5},{5,4},{6,7},{7,6},{8,9},{9,8},{10,11... | collective-permute-start | bytes 1351688 | tf_op jit(solution)/shard_map/ppermute | solution.py:352
  18.3 6.1 %collective-permute-start.6 = (bf16[26,1280]{1,0:T(8,128)(2,1)S(1)}, bf16[26,1280]{1,0:T(8,128)(2,1)S(1)}, u32[]{:S(2)}, u32[]{:S(2)}) collective-permute-start(bf16[26,1280]{1,0:T(8,128)(2,1)S(1)} %get-tuple-element.34), channel_id=1, source_target_pairs={{4,8},{12,16},{20,24},{8,4},{16,12},{24,20},{5,9},{13,17},{21,25},... | collective-permute-start | bytes 199688 | tf_op jit(solution)/shard_map/ppermute | solution.py:356
  20.3 7.2 %collective-permute-start.10 = (bf16[112,1280]{1,0:T(8,128)(2,1)S(1)}, bf16[112,1280]{1,0:T(8,128)(2,1)S(1)}, u32[]{:S(2)}, u32[]{:S(2)}) collective-permute-start(bf16[112,1280]{1,0:T(8,128)(2,1)S(1)} %second.1._.refs_3_), channel_id=1, source_target_pairs={{0,1},{1,0},{2,3},{3,2},{4,5},{5,4},{6,7},{7,6},{8,9},{9,8},{10,11... | collective-permute-start | bytes 860168 | tf_op jit(solution)/shard_map/ppermute | solution.py:352
  24.4 2.8 %collective-permute-start.9 = (bf16[88,1280]{1,0:T(8,128)(2,1)S(1)}, bf16[88,1280]{1,0:T(8,128)(2,1)S(1)}, u32[]{:S(2)}, u32[]{:S(2)}) collective-permute-start(bf16[88,1280]{1,0:T(8,128)(2,1)S(1)} %get-tuple-element.37.refs_2_), channel_id=1, source_target_pairs={{0,1},{1,0},{2,3},{3,2},{4,5},{5,4},{6,7},{7,6},{8,9},{9,8},{10,11... | collective-permute-start | bytes 675848 | tf_op jit(solution)/shard_map/ppermute | solution.py:352
  27.2 1.9 %collective-permute-start.8 = (bf16[48,1280]{1,0:T(8,128)(2,1)S(1)}, bf16[48,1280]{1,0:T(8,128)(2,1)S(1)}, u32[]{:S(2)}, u32[]{:S(2)}) collective-permute-start(bf16[48,1280]{1,0:T(8,128)(2,1)S(1)} %edges.1.refs_1_.refs_4_.refs_6_), channel_id=1, source_target_pairs={{0,1},{1,0},{2,3},{3,2},{4,5},{5,4},{6,7},{7,6},{8,9},{9,8},{10,11... | collective-permute-start | bytes 368648 | tf_op jit(solution)/shard_map/ppermute | solution.py:352
  27.5 6.4 %collective-permute-start.14 = (bf16[48,1280]{1,0:T(8,128)(2,1)S(1)}, bf16[48,1280]{1,0:T(8,128)(2,1)S(1)}, u32[]{:S(2)}, u32[]{:S(2)}) collective-permute-start(bf16[48,1280]{1,0:T(8,128)(2,1)S(1)} %edges.1.refs_1_.refs_4_.refs_6_), channel_id=1, source_target_pairs={{0,2},{1,3},{2,0},{3,1},{4,6},{5,7},{6,4},{7,5},{8,10},{9,11},{10,... | collective-permute-start | bytes 368648 | tf_op jit(solution)/shard_map/ppermute | solution.py:347
  27.8 14.2 %collective-permute-start.2 = (bf16[176,1280]{1,0:T(8,128)(2,1)S(1)}, bf16[176,1280]{1,0:T(8,128)(2,1)S(1)}, u32[]{:S(2)}, u32[]{:S(2)}) collective-permute-start(bf16[176,1280]{1,0:T(8,128)(2,1)S(1)} %get-tuple-element.31.refs_5_), channel_id=1, source_target_pairs={{0,2},{1,3},{2,0},{3,1},{4,6},{5,7},{6,4},{7,5},{8,10},{9,11},{10,... | collective-permute-start | bytes 1351688 | tf_op jit(solution)/shard_map/ppermute | solution.py:347
  33.9 1.8 %collective-permute-start.15 = (bf16[48,1280]{1,0:T(8,128)(2,1)S(1)}, bf16[48,1280]{1,0:T(8,128)(2,1)S(1)}, u32[]{:S(2)}, u32[]{:S(2)}) collective-permute-start(bf16[48,1280]{1,0:T(8,128)(2,1)S(1)} %collective-permute-done.14.refs_1_.refs_4_), channel_id=1, source_target_pairs={{0,1},{1,0},{2,3},{3,2},{4,5},{5,4},{6,7},{7,6},{8,9},{9,8},{10,11... | collective-permute-start | bytes 368648 | tf_op jit(solution)/shard_map/ppermute | solution.py:352
  34.7 3.6 %collective-permute-start.17 = (bf16[112,1280]{1,0:T(8,128)(2,1)S(1)}, bf16[112,1280]{1,0:T(8,128)(2,1)S(1)}, u32[]{:S(2)}, u32[]{:S(2)}) collective-permute-start(bf16[112,1280]{1,0:T(8,128)(2,1)S(1)} %collective-permute-done.4.refs_3_), channel_id=1, source_target_pairs={{0,1},{1,0},{2,3},{3,2},{4,5},{5,4},{6,7},{7,6},{8,9},{9,8},{10,11... | collective-permute-start | bytes 860168 | tf_op jit(solution)/shard_map/ppermute | solution.py:352
  34.8 3.5 %collective-permute-start.12 = (bf16[96,1280]{1,0:T(8,128)(2,1)S(1)}, bf16[96,1280]{1,0:T(8,128)(2,1)S(1)}, u32[]{:S(2)}, u32[]{:S(2)}) collective-permute-start(bf16[96,1280]{1,0:T(8,128)(2,1)S(1)} %slice.6), channel_id=1, source_target_pairs={{0,1},{1,0},{2,3},{3,2},{4,5},{5,4},{6,7},{7,6},{8,9},{9,8},{10,11... | collective-permute-start | bytes 737288 | tf_op jit(solution)/shard_map/ppermute | solution.py:352
  35.3 3.0 %collective-permute-start.16 = (bf16[88,1280]{1,0:T(8,128)(2,1)S(1)}, bf16[88,1280]{1,0:T(8,128)(2,1)S(1)}, u32[]{:S(2)}, u32[]{:S(2)}) collective-permute-start(bf16[88,1280]{1,0:T(8,128)(2,1)S(1)} %collective-permute-done.before_ref.behind_ref.refs_2_), channel_id=1, source_target_pairs={{0,1},{1,0},{2,3},{3,2},{4,5},{5,4},{6,7},{7,6},{8,9},{9,8},{10,11... | collective-permute-start | bytes 675848 | tf_op jit(solution)/shard_map/ppermute | solution.py:352
  35.7 2.6 %collective-permute-start.13 = (bf16[80,1280]{1,0:T(8,128)(2,1)S(1)}, bf16[80,1280]{1,0:T(8,128)(2,1)S(1)}, u32[]{:S(2)}, u32[]{:S(2)}) collective-permute-start(bf16[80,1280]{1,0:T(8,128)(2,1)S(1)} %slice.7), channel_id=1, source_target_pairs={{0,1},{1,0},{2,3},{3,2},{4,5},{5,4},{6,7},{7,6},{8,9},{9,8},{10,11... | collective-permute-start | bytes 614408 | tf_op jit(solution)/shard_map/ppermute | solution.py:352
  42.0 2.7 %collective-permute-start.18 = (bf16[176,1280]{1,0:T(8,128)(2,1)S(1)}, bf16[176,1280]{1,0:T(8,128)(2,1)S(1)}, u32[]{:S(2)}, u32[]{:S(2)}) collective-permute-start(bf16[176,1280]{1,0:T(8,128)(2,1)S(1)} %collective-permute-done.2.refs_0_), channel_id=1, source_target_pairs={{0,1},{1,0},{2,3},{3,2},{4,5},{5,4},{6,7},{7,6},{8,9},{9,8},{10,11... | collective-permute-start | bytes 1351688 | tf_op jit(solution)/shard_map/ppermute | solution.py:352

commit v3 on v2

--- a/solution.py
+++ b/solution.py
@@ -12,7 +12,7 @@
 LANES = 128
 EPS = 1e-06
 VMEM_LIMIT = 32 * 1024 * 1024
-K = {'early': 8, 'piece': 96, 'pieceA': 64, 'bsplit': 0, 'csplit': 0, 'A2': 'edges', 'B': 'X', 'C1': None, 'D': None, 'swA': 'X', 'swB': 'X', 'swD': 'X', 'z': 2, 'y': 2}
+K = {'piece': 96, 'pieceA': 96, 'bsplit': 0, 'csplit': 0, 'A2': 'edges', 'B': None, 'C1': None, 'D': None, 'swA': 'X', 'swB': 'X', 'swD': 'X', 'z': 2, 'y': 2}
 BF16 = jnp.bfloat16
 F32 = jnp.float32
 
@@ -87,50 +87,32 @@
     return lax.rem(lax.axis_index(cols_axis), 2)
 
 
-def first_kernel(count, x_hbm, taps_hbm, cbias_hbm, gain_hbm, nbias_hbm, out_ref, inner_ref, x_ref, taps_ref, vec_ref, mixed, *rest):
+def first_kernel(x_hbm, taps_hbm, cbias_hbm, gain_hbm, nbias_hbm, outer_ref, inner_ref, x_ref, taps_ref, vec_ref, *rest):
     *flat, sems = rest
     rows, cols, width = x_ref.shape
-    need = count + 2
-    copies = [
-        pltpu.make_async_copy(x_hbm.at[pl.ds(0, need)], x_ref.at[pl.ds(0, need)], sems.at[0]),
-        pltpu.make_async_copy(taps_hbm, taps_ref, sems.at[1]),
-        pltpu.make_async_copy(cbias_hbm, flat[0], sems.at[2]),
-        pltpu.make_async_copy(gain_hbm, flat[1], sems.at[3]),
-        pltpu.make_async_copy(nbias_hbm, flat[2], sems.at[4]),
-        pltpu.make_async_copy(x_hbm.at[pl.ds(need, rows - need)], x_ref.at[pl.ds(need, rows - need)], sems.at[5]),
-    ]
+    pairs = ((x_hbm, x_ref), (taps_hbm, taps_ref), (cbias_hbm, flat[0]), (gain_hbm, flat[1]), (nbias_hbm, flat[2]))
+    copies = [pltpu.make_async_copy(source, target, sems.at[k]) for k, (source, target) in enumerate(pairs)]
     for copy in copies:
         copy.start()
-    for copy in copies[:-1]:
+    for copy in copies:
         copy.wait()
-    for k in range(3):
-        vec_ref[k] = flat[k][...].reshape(1, width)
-    span = slice(GROUP, cols - GROUP)
-    wide = cols - 2 * GROUP
-
-    def tile(lanes):
-        def emit(i, value):
-            mixed[pl.ds((i - 1) * wide, wide), lanes] = value
-
-        stencil(taps_ref, vec_ref.at[0], lanes, middle_cells(x_ref, lanes, span), 1, count, emit)
-
-    each_tile(width, tile)
-    normalize(mixed, count * wide, vec_ref.at[1], vec_ref.at[2], out_ref)
-    copies[-1].wait()
+    for k, ref in enumerate(flat):
+        vec_ref[k] = ref[...].reshape(1, width)
     core = core_of("cols")
 
     def sides(lanes):
         left = [x_ref[i, pl.ds(0, GROUP), lanes].astype(F32)[:1] for i in range(rows)]
         right = [x_ref[i, pl.ds(cols - GROUP, GROUP), lanes].astype(F32)[GROUP - 1 :] for i in range(rows)]
         left, right = jnp.concatenate(left, axis=0), jnp.concatenate(right, axis=0)
-        out_ref[count * wide :, lanes] = jnp.where(core == 1, right, left).astype(BF16)
+        outer_ref[:, lanes] = jnp.where(core == 1, right, left).astype(BF16)
         inner_ref[:, lanes] = jnp.where(core == 1, left, right).astype(BF16)
 
     each_tile(width, sides)
 
 
-def second_kernel(start, x_ref, taps_ref, vec_ref, out_ref, mixed):
+def middle_kernel(x_ref, taps_ref, vec_ref, out_ref, mixed):
     rows, cols, width = x_ref.shape
+    start = 1
     span = slice(GROUP, cols - GROUP)
     wide = cols - 2 * GROUP
     count = rows - 1 - start
@@ -147,12 +129,11 @@
 
 def relay_kernel(beside_ref, before_ref, behind_ref, _, out_ref):
     rows = beside_ref.shape[0]
-    few = before_ref.shape[0] - rows
     col, count = lax.axis_index("cols"), lax.axis_size("cols")
     core = core_of("cols")
     none = jnp.logical_or(col == 1, col == count - 2)
     out_ref[:rows, :] = beside_ref[...]
-    passed = jnp.where(core == 1, before_ref[few:, :].astype(F32), behind_ref[few:, :].astype(F32))
+    passed = jnp.where(core == 1, before_ref[...].astype(F32), behind_ref[...].astype(F32))
     out_ref[rows:, :] = jnp.where(none, 0.0, passed).astype(BF16)
 
 
@@ -334,8 +315,6 @@
     wide = cols - 2 * GROUP
     inner = rows - 2
     half = inner * GROUP
-    early = K['early']
-    few = early * wide
     two = 2 * GROUP
     steps = range(1, chips)
 
@@ -362,11 +341,11 @@
     def in_hbm(value):
         return pltpu.with_memory_space_constraint(value, pltpu.HBM)
 
-    first, beside, x, taps, vectors = call(
-        functools.partial(first_kernel, early),
+    outer, beside, x, taps, vectors = call(
+        first_kernel,
         "first",
         [
-            array(few + rows, width),
+            array(rows, width),
             array(rows, width),
             array(rows, cols, width),
             array(3, 3, width, dtype=F32),
@@ -374,19 +353,19 @@
         ],
         [HBM] * 5,
         [VMEM] * 5,
-        [pltpu.VMEM((few, width), F32)] + [pltpu.VMEM((width,), F32)] * 3 + [pltpu.SemaphoreType.DMA((6,))],
+        [pltpu.VMEM((width,), F32)] * 3 + [pltpu.SemaphoreType.DMA((5,))],
     )(*[in_hbm(v) for v in (patches, conv_taps, conv_bias, norm_gain, norm_bias)])
-    got_first = across(first)
-
-    second = call(
-        functools.partial(second_kernel, early + 1),
-        "second",
-        array(half - few, width),
+    got_outer = across(outer)
+
+    middle = call(
+        middle_kernel,
+        "middle",
+        array(half, width),
         [VMEM] * 3,
         VMEM,
-        [pltpu.VMEM((half - few, width), F32)],
+        [pltpu.VMEM((half, width), F32)],
     )(x, taps, vectors)
-    got_second = across(second)
+    got_middle = across(middle)
 
     sides = swap(
         call(
@@ -396,7 +375,7 @@
             [VMEM] * 4,
             VMEM,
             [],
-        )(beside, got_first[0], got_first[-1], second)
+        )(beside, got_outer[0], got_outer[-1], middle)
     )
 
     def cuts(size):
@@ -423,7 +402,7 @@
     near, far = parts[:count], parts[count:]
     got_near = [across(v) for v in near]
     got_far = [across(v) for v in far]
-    marks = {"A2": got_second, "B": sum(got_near, []), "C1": got_far[0]}
+    marks = {"A2": got_middle, "B": sum(got_near, []), "C1": got_far[0]}
 
     def hold(place, values):
         others = sum([marks[k] for k in marks if K[k] == place], [])
@@ -450,10 +429,10 @@
     def whole(values):
         return [(value, 0, value.shape[0]) for value in values]
 
-    def groups_of(near, first, second, edge, far, other):
+    def groups_of(near, middle, edge, far, other):
         return [
             (whole(near) + [(edge, 0, two)], other, 0),
-            ([(first, 0, few)] + whole(second) + [(edge, two, two)], other, 1),
+            (whole(middle) + [(edge, two, two)], other, 1),
             (whole(far) + [(edge, 2 * two, two)], other, 2),
         ]
 
@@ -468,17 +447,17 @@
         return run(out, arrays, entries, step)
 
     (late,) = hold("eswap", (edge,))
-    (held,) = hold("X", (first,))
+    (held,) = hold("X", (middle,))
     out = step_on(
         None,
-        groups_of(near, held, [second], edge, far, 0)
-        + groups_of([swap(v) for v in near], swap(first), [swap(second)], swap(late), [swap(v) for v in far], 1),
+        groups_of(near, [held], edge, far, 0)
+        + groups_of([swap(v) for v in near], [swap(middle)], swap(late), [swap(v) for v in far], 1),
         0,
     )
     for step in steps:
         at = step - 1
         pick = dict(
-            swA=[got_first[at], got_second[at]], swB=[v[at] for v in got_near], swD=[got_edge[at]]
+            swA=[got_middle[at]], swB=[v[at] for v in got_near], swD=[got_edge[at]]
         )
         for key in pick:
             if K[key] == "X":
@@ -486,19 +465,20 @@
         c1 = [v[at] for v in got_far]
         if K["C1"] == "dswap":
             pick["swD"] = after(pick["swD"], c1[:1])
-        (got1, got2), gotb, (gote,) = pick["swA"], pick["swB"], pick["swD"]
+        gota, gotb, (gote,) = pick["swA"], pick["swB"], pick["swD"]
         other_near = [swap(v[p : p + K["piece"]]) for v in gotb for p in range(0, v.shape[0], K["piece"])]
-        other1, other2, othere = swap(got1), swap(got2), swap(gote)
-        mine = groups_of(gotb, got1, [got2], gote, [], 0)[:2]
-        theirs = groups_of(other_near, other1, [other2], othere, [], 1)[:2]
+        other_middle = [swap(v[p : p + K["pieceA"]]) for v in gota for p in range(0, v.shape[0], K["pieceA"])]
+        othere = swap(gote)
+        mine = groups_of(gotb, gota, gote, [], 0)[:2]
+        theirs = groups_of(other_near, other_middle, othere, [], 1)[:2]
         if K["y"] == 2:
             out = step_on(out, mine, chips - step)
             out = step_on(out, theirs, chips - step)
         else:
             out = step_on(out, mine + theirs, chips - step)
         *c1, out = lax.optimization_barrier((*c1, out))
-        last = groups_of([], got1, [], gote, c1, 0)[2:]
-        other = groups_of([], got1, [], othere, [swap(v) for v in c1], 1)[2:]
+        last = groups_of([], [], gote, c1, 0)[2:]
+        other = groups_of([], [], othere, [swap(v) for v in c1], 1)[2:]
         if K["z"] == 2:
             out = step_on(out, last, chips - step)
             out = step_on(out, other, chips - step)

time: 46.6 us -> 44.8 us (0.961)
  the two profiles are of different devices: /device:TPU:25 before, /device:TPU:15 now
where the time goes in v3:
time: 44.8 us; the launch traced here: 44.7 us
  Pallas kernels  19.1 us (43%)
  starting transfers between devices  17 us (38%)
  waiting for transfers between devices  8.28 us (18%)
    pallas_call x5, Pallas kernels, project(): call(functools.partial(project_kernel, rows, plan, count, fresh, step, si...  12.9 us
    ppermute x11, starting transfers between devices, swap(): return lax.ppermute(value, 'cols', [(q, q ^ 1) for q in range(side_count)])  8.52 us
    ppermute x5, waiting for transfers between devices, across(): lax.ppermute(value, 'cols', [(q, (q + 2 * step) % side_count) for q in ra...  7.19 us
    ppermute x2, starting transfers between devices, exchange(): return lax.ppermute(value, 'rows', pairs + [(j, i) for i, j in pairs])  4.44 us
    ppermute x5, starting transfers between devices, across(): lax.ppermute(value, 'cols', [(q, (q + 2 * step) % side_count) for q in ra...  4.05 us
    pallas_call x1, Pallas kernels, local(): call(sides_kernel, 'sides', [array(size, width) for size in sizes], [VMEM...  2.34 us
    pallas_call x1, Pallas kernels, local(): call(first_kernel, 'first', [array(rows, width), array(rows, width), arra...  1.82 us
    pallas_call x1, Pallas kernels, local(): call(middle_kernel, 'middle', array(half, width), [VMEM] * 3, VMEM, [pltp...  1.27 us
  transfers between devices with their start and end apart: 18, of which 6 were waited for; matrix products, arithmetic and copies ran while one was open for 0% of the time, Pallas kernels for 35%

profile of v3, /device:TPU:15, one launch (start us, length us, event | category | flops | bytes accessed | tf_op | source)
XLA Modules:
  0.0 44.7 jit_solution(12062864525755226466)
XLA Ops:
  0.0 0.0 copy-start.1
  0.0 0.0 copy-start
  0.0 1.8 %first.1 = (bf16[24,1280]{1,0:T(8,128)(2,1)S(1)}, bf16[24,1280]{1,0:T(8,128)(2,1)S(1)}, bf16[24,24,1280]{2,1,0:T(8,128)(2,1)S(1)}, f32[3,3,1280]{2,1,0:T(4,128)S(1)}, f32[3,1,1280]{2,1,0:T(1,128)S(1)}) custom-call(bf16[24,24,1280]{2,1,0:T(8,128)(2,1)} %x_hbm.1, f32[3,3,1280]{2,1,0:T(4,128)} %taps_hbm.1, f32[1280]{0:T(1024)} %cbias_hbm.1, f32[1280]{0:T(1024)} %gain_hbm.1, ...), custom_call_target="tpu_custom_call" | custom-call | flops 1024 | bytes 1024 | tf_op jit(solution)/shard_map/first/pallas_call | solution.py:344
  1.8 0.3 collective-permute-start
  2.1 1.3 %middle.1._.refs_2_ = bf16[176,1280]{1,0:T(8,128)(2,1)S(1)} custom-call(bf16[24,24,1280]{2,1,0:T(8,128)(2,1)S(1)} %get-tuple-element.24.x_ref, f32[3,3,1280]{2,1,0:T(4,128)S(1)} %get-tuple-element.27.taps_ref, f32[3,1,1280]{2,1,0:T(1,128)S(1)} %get-tuple-element.28.vec_ref), custom_call_target="tpu_custom_call" | custom-call | flops 1024 | bytes 1024 | tf_op jit(solution)/shard_map/middle/pallas_call | solution.py:360
  3.4 1.3 %collective-permute-start.4 = (bf16[176,1280]{1,0:T(8,128)(2,1)S(1)}, bf16[176,1280]{1,0:T(8,128)(2,1)S(1)}, u32[]{:S(2)}, u32[]{:S(2)}) collective-permute-start(bf16[176,1280]{1,0:T(8,128)(2,1)S(1)} %middle.1._.refs_2_), channel_id=1, source_target_pairs={{0,2},{1,3},{2,0},{3,1},{4,6},{5,7},{6,4},{7,5},{8,10},{9,11},{10,... | collective-permute-start | bytes 1351688 | tf_op jit(solution)/shard_map/ppermute | solution.py:326
  4.7 0.3 collective-permute-done.before_ref.behind_ref
  5.0 2.2 %collective-permute-start.1 = (bf16[48,1280]{1,0:T(8,128)(2,1)S(1)}, bf16[48,1280]{1,0:T(8,128)(2,1)S(1)}, u32[]{:S(2)}, u32[]{:S(2)}) collective-permute-start(bf16[48,1280]{1,0:T(8,128)(2,1)S(1)} %relay.1), channel_id=1, source_target_pairs={{0,1},{1,0},{2,3},{3,2},{4,5},{5,4},{6,7},{7,6},{8,9},{9,8},{10,11... | collective-permute-start | bytes 368648 | tf_op jit(solution)/shard_map/ppermute | solution.py:331
  7.2 0.1 collective-permute-start.9
  7.2 0.9 %collective-permute-done.1.sides_ref = bf16[48,1280]{1,0:T(8,128)(2,1)S(1)} collective-permute-done((bf16[48,1280]{1,0:T(8,128)(2,1)S(1)}, bf16[48,1280]{1,0:T(8,128)(2,1)S(1)}, u32[]{:S(2)}, u32[]{:S(2)}) %collective-permute-start.1) | collective-permute-done | bytes 122912 | tf_op jit(solution)/shard_map/ppermute | solution.py:331
  8.1 0.1 ends.1
  8.2 0.3 collective-permute-start.5
  8.5 4.1 %collective-permute-start.6 = (bf16[26,1280]{1,0:T(8,128)(2,1)S(1)}, bf16[26,1280]{1,0:T(8,128)(2,1)S(1)}, u32[]{:S(2)}, u32[]{:S(2)}) collective-permute-start(bf16[26,1280]{1,0:T(8,128)(2,1)S(1)} %get-tuple-element.32), channel_id=1, source_target_pairs={{4,8},{12,16},{20,24},{8,4},{16,12},{24,20},{5,9},{13,17},{21,25},... | collective-permute-start | bytes 199688 | tf_op jit(solution)/shard_map/ppermute | solution.py:335
  12.7 2.3 %sides.1 = (bf16[176,1280]{1,0:T(8,128)(2,1)S(1)}, bf16[176,1280]{1,0:T(8,128)(2,1)S(1)}) custom-call(bf16[24,24,1280]{2,1,0:T(8,128)(2,1)S(1)} %get-tuple-element.24.x_ref, bf16[48,1280]{1,0:T(8,128)(2,1)S(1)} %collective-permute-done.1.sides_ref, f32[3,3,1280]{2,1,0:T(4,128)S(1)} %get-tuple-element.27.taps_ref, f32[3,1,1280]{2,1,0:T(1,128)S(1)} %get-tuple-element.28.vec_ref), custom_call_target="tpu_custom_call" | custom-call | flops 1024 | bytes 1024 | tf_op jit(solution)/shard_map/sides/pallas_call | solution.py:393
  15.0 1.0 %collective-permute-start.10 = (bf16[176,1280]{1,0:T(8,128)(2,1)S(1)}, bf16[176,1280]{1,0:T(8,128)(2,1)S(1)}, u32[]{:S(2)}, u32[]{:S(2)}) collective-permute-start(bf16[176,1280]{1,0:T(8,128)(2,1)S(1)} %get-tuple-element.29.refs_4_), channel_id=1, source_target_pairs={{0,1},{1,0},{2,3},{3,2},{4,5},{5,4},{6,7},{7,6},{8,9},{9,8},{10,11... | collective-permute-start | bytes 1351688 | tf_op jit(solution)/shard_map/ppermute | solution.py:331
  16.0 0.0 collective-permute-done.5.pair_ref
  16.0 0.1 collective-permute-start.7
  16.1 0.0 collective-permute-done.6.cross_ref
  16.1 0.0 collective-permute-start.3
  16.1 0.0 collective-permute-done.4.refs_2_
  16.1 0.7 %edges.1.refs_1_.refs_3_.refs_5_ = bf16[48,1280]{1,0:T(8,128)(2,1)S(1)} custom-call(bf16[24,24,1280]{2,1,0:T(8,128)(2,1)S(1)} %get-tuple-element.24.x_ref, bf16[48,1280]{1,0:T(8,128)(2,1)S(1)} %collective-permute-done.1.sides_ref, bf16[26,1280]{1,0:T(8,128)(2,1)S(1)} %collective-permute-done.5.pair_ref, ...), custom_call_target="tpu_custom_call" | custom-call | flops 1024 | bytes 1024 | tf_op jit(solution)/shard_map/edges/pallas_call | solution.py:414
  16.8 0.7 %collective-permute-start.8 = (bf16[48,1280]{1,0:T(8,128)(2,1)S(1)}, bf16[48,1280]{1,0:T(8,128)(2,1)S(1)}, u32[]{:S(2)}, u32[]{:S(2)}) collective-permute-start(bf16[48,1280]{1,0:T(8,128)(2,1)S(1)} %edges.1.refs_1_.refs_3_.refs_5_), channel_id=1, source_target_pairs={{0,1},{1,0},{2,3},{3,2},{4,5},{5,4},{6,7},{7,6},{8,9},{9,8},{10,11... | collective-permute-start | bytes 368648 | tf_op jit(solution)/shard_map/ppermute | solution.py:331
  17.5 0.0 collective-permute-done.9.refs_8_
  17.5 1.5 %collective-permute-start.13 = (bf16[48,1280]{1,0:T(8,128)(2,1)S(1)}, bf16[48,1280]{1,0:T(8,128)(2,1)S(1)}, u32[]{:S(2)}, u32[]{:S(2)}) collective-permute-start(bf16[48,1280]{1,0:T(8,128)(2,1)S(1)} %edges.1.refs_1_.refs_3_.refs_5_), channel_id=1, source_target_pairs={{0,2},{1,3},{2,0},{3,1},{4,6},{5,7},{6,4},{7,5},{8,10},{9,11},{10,... | collective-permute-start | bytes 368648 | tf_op jit(solution)/shard_map/ppermute | solution.py:326
  19.0 0.0 collective-permute-done.8.refs_7_.refs_9_.refs_11_
  19.0 1.0 %collective-permute-start.2 = (bf16[176,1280]{1,0:T(8,128)(2,1)S(1)}, bf16[176,1280]{1,0:T(8,128)(2,1)S(1)}, u32[]{:S(2)}, u32[]{:S(2)}) collective-permute-start(bf16[176,1280]{1,0:T(8,128)(2,1)S(1)} %get-tuple-element.29.refs_4_), channel_id=1, source_target_pairs={{0,2},{1,3},{2,0},{3,1},{4,6},{5,7},{6,4},{7,5},{8,10},{9,11},{10,... | collective-permute-start | bytes 1351688 | tf_op jit(solution)/shard_map/ppermute | solution.py:326
  20.0 0.0 collective-permute-done.10.refs_10_
  20.0 0.0 collective-permute-done.7.refs_6_
  20.0 0.0 copy-done.1
  20.0 0.0 copy-done
  20.0 4.9 %project.5.refs_6_ = bf16[3,4,24,7680]{3,2,1,0:T(8,128)(2,1)} custom-call(bf16[176,1280]{1,0:T(8,128)(2,1)S(1)} %get-tuple-element.30.refs_0_, bf16[48,1280]{1,0:T(8,128)(2,1)S(1)} %edges.1.refs_1_.refs_3_.refs_5_, bf16[176,1280]{1,0:T(8,128)(2,1)S(1)} %middle.1._.refs_2_, bf16[48,1280]{1,0:T(8,128)(2,1)S(1)} %edges.1.refs_1_.refs_3_.refs_5_, ...), custom_call_target="tpu_custom_call" | custom-call | flops 1024 | bytes 1024 | tf_op jit(solution)/shard_map/project/pallas_call | solution.py:296
  24.9 2.7 %collective-permute-done.3.refs_0_ = bf16[176,1280]{1,0:T(8,128)(2,1)S(1)} collective-permute-done((bf16[176,1280]{1,0:T(8,128)(2,1)S(1)}, bf16[176,1280]{1,0:T(8,128)(2,1)S(1)}, u32[]{:S(2)}, u32[]{:S(2)}) %collective-permute-start.3) | collective-permute-done | bytes 450592 | tf_op jit(solution)/shard_map/ppermute | solution.py:326
  27.6 2.6 %collective-permute-done.13.refs_1_.refs_3_ = bf16[48,1280]{1,0:T(8,128)(2,1)S(1)} collective-permute-done((bf16[48,1280]{1,0:T(8,128)(2,1)S(1)}, bf16[48,1280]{1,0:T(8,128)(2,1)S(1)}, u32[]{:S(2)}, u32[]{:S(2)}) %collective-permute-start.13) | collective-permute-done | bytes 122912 | tf_op jit(solution)/shard_map/ppermute | solution.py:326
  30.2 2.1 %collective-permute-start.14 = (bf16[48,1280]{1,0:T(8,128)(2,1)S(1)}, bf16[48,1280]{1,0:T(8,128)(2,1)S(1)}, u32[]{:S(2)}, u32[]{:S(2)}) collective-permute-start(bf16[48,1280]{1,0:T(8,128)(2,1)S(1)} %collective-permute-done.13.refs_1_.refs_3_), channel_id=1, source_target_pairs={{0,1},{1,0},{2,3},{3,2},{4,5},{5,4},{6,7},{7,6},{8,9},{9,8},{10,11... | collective-permute-start | bytes 368648 | tf_op jit(solution)/shard_map/ppermute | solution.py:331
  32.4 0.1 collective-permute-start.15
  32.5 0.5 %collective-permute-start.11 = (bf16[96,1280]{1,0:T(8,128)(2,1)S(1)}, bf16[96,1280]{1,0:T(8,128)(2,1)S(1)}, u32[]{:S(2)}, u32[]{:S(2)}) collective-permute-start(bf16[96,1280]{1,0:T(8,128)(2,1)S(1)} %slice.12), channel_id=1, source_target_pairs={{0,1},{1,0},{2,3},{3,2},{4,5},{5,4},{6,7},{7,6},{8,9},{9,8},{10,11... | collective-permute-start | bytes 737288 | tf_op jit(solution)/shard_map/ppermute | solution.py:331
  33.0 0.1 collective-permute-start.16
  33.2 0.2 collective-permute-done.14.refs_2_.refs_5_.refs_1_
  33.3 0.4 collective-permute-start.12
  33.7 2.3 %project.6.refs_8_ = bf16[3,4,24,7680]{3,2,1,0:T(8,128)(2,1)} custom-call(bf16[176,1280]{1,0:T(8,128)(2,1)S(1)} %collective-permute-done.3.refs_0_, bf16[48,1280]{1,0:T(8,128)(2,1)S(1)} %collective-permute-done.13.refs_1_.refs_3_, bf16[176,1280]{1,0:T(8,128)(2,1)S(1)} %collective-permute-done.4.refs_2_, ...), custom_call_target="tpu_custom_call", output_to_operand_aliasing={{}: (6, {})} | custom-call | flops 1024 | bytes 1024 | tf_op jit(solution)/shard_map/project/pallas_call | solution.py:296
  36.0 0.0 collective-permute-done.16.refs_4_
  36.0 0.0 collective-permute-done.12.refs_1_
  36.0 0.0 collective-permute-done.15.refs_3_
  36.0 0.0 collective-permute-done.11.refs_0_
  36.0 2.3 %project.7.refs_4_ = bf16[3,4,24,7680]{3,2,1,0:T(8,128)(2,1)} custom-call(bf16[96,1280]{1,0:T(8,128)(2,1)S(1)} %collective-permute-done.11.refs_0_, bf16[80,1280]{1,0:T(8,128)(2,1)S(1)} %collective-permute-done.12.refs_1_, bf16[48,1280]{1,0:T(8,128)(2,1)S(1)} %collective-permute-done.14.refs_2_.refs_5_.refs_1_, ...), custom_call_target="tpu_custom_call", output_to_operand_aliasing={{}: (8, {})} | custom-call | flops 1024 | bytes 1024 | tf_op jit(solution)/shard_map/project/pallas_call | solution.py:296
  38.3 1.6 %collective-permute-done.2.refs_0_ = bf16[176,1280]{1,0:T(8,128)(2,1)S(1)} collective-permute-done((bf16[176,1280]{1,0:T(8,128)(2,1)S(1)}, bf16[176,1280]{1,0:T(8,128)(2,1)S(1)}, u32[]{:S(2)}, u32[]{:S(2)}) %collective-permute-start.2) | collective-permute-done | bytes 450592 | tf_op jit(solution)/shard_map/ppermute | solution.py:326
  39.9 1.3 %collective-permute-start.17 = (bf16[176,1280]{1,0:T(8,128)(2,1)S(1)}, bf16[176,1280]{1,0:T(8,128)(2,1)S(1)}, u32[]{:S(2)}, u32[]{:S(2)}) collective-permute-start(bf16[176,1280]{1,0:T(8,128)(2,1)S(1)} %collective-permute-done.2.refs_0_), channel_id=1, source_target_pairs={{0,1},{1,0},{2,3},{3,2},{4,5},{5,4},{6,7},{7,6},{8,9},{9,8},{10,11... | collective-permute-start | bytes 1351688 | tf_op jit(solution)/shard_map/ppermute | solution.py:331
  41.1 1.8 %project.8.refs_4_ = bf16[3,4,24,7680]{3,2,1,0:T(8,128)(2,1)} custom-call(bf16[176,1280]{1,0:T(8,128)(2,1)S(1)} %collective-permute-done.2.refs_0_, bf16[48,1280]{1,0:T(8,128)(2,1)S(1)} %collective-permute-done.13.refs_1_.refs_3_, bf16[3,320,1280]{2,1,0:T(8,128)(2,1)S(1)} %bitcast.4, bf16[3,320]{1,0:T(4,128)(2,1)S(1)} %copy-done.1, ...), custom_call_target="tpu_custom_call", output_to_operand_aliasing={{}: (4, {})} | custom-call | flops 1024 | bytes 1024 | tf_op jit(solution)/shard_map/project/pallas_call | solution.py:296
  42.9 0.0 collective-permute-done.17.refs_0_
  42.9 1.7 %project.9 = bf16[3,4,24,7680]{3,2,1,0:T(8,128)(2,1)} custom-call(bf16[176,1280]{1,0:T(8,128)(2,1)S(1)} %collective-permute-done.17.refs_0_, bf16[48,1280]{1,0:T(8,128)(2,1)S(1)} %collective-permute-done.14.refs_2_.refs_5_.refs_1_, bf16[3,320,1280]{2,1,0:T(8,128)(2,1)S(1)} %bitcast.5, bf16[3,320]{1,0:T(4,128)(2,1)S(1)} %copy-done.1, ...), custom_call_target="tpu_custom_call", output_to_operand_aliasing={{}: (4, {})} | custom-call | flops 1024 | bytes 1024 | tf_op jit(solution)/shard_map/project/pallas_call | solution.py:296
  (5 shorter events, 0.1 us)
Async XLA Ops:
  0.0 20.0 %copy-start.1 = (bf16[3,320]{1,0:T(4,128)(2,1)S(1)}, bf16[3,320]{1,0:T(4,128)(2,1)}, u32[]{:S(2)}) copy-start(bf16[3,320]{1,0:T(4,128)(2,1)} %refs_3_.3) | copy-start | bytes 5764
  0.0 20.0 %copy-start = (bf16[3,1280,320]{1,2,0:T(8,128)(2,1)S(1)}, bf16[3,1280,320]{1,2,0:T(8,128)(2,1)}, u32[]{:S(2)}) copy-start(bf16[3,1280,320]{1,2,0:T(8,128)(2,1)} %param.12) | copy-start | bytes 7372804
  1.8 3.1 %collective-permute-start = (bf16[24,1280]{1,0:T(8,128)(2,1)S(1)}, bf16[24,1280]{1,0:T(8,128)(2,1)S(1)}, u32[]{:S(2)}, u32[]{:S(2)}) collective-permute-start(bf16[24,1280]{1,0:T(8,128)(2,1)S(1)} %get-tuple-element.26), channel_id=1, source_target_pairs={{0,2},{1,3},{2,0},{3,1},{4,6},{5,7},{6,4},{7,5},{8,10},{9,11},{10,... | collective-permute-start | bytes 184328 | tf_op jit(solution)/shard_map/ppermute | solution.py:326
  3.4 12.7 %collective-permute-start.4 = (bf16[176,1280]{1,0:T(8,128)(2,1)S(1)}, bf16[176,1280]{1,0:T(8,128)(2,1)S(1)}, u32[]{:S(2)}, u32[]{:S(2)}) collective-permute-start(bf16[176,1280]{1,0:T(8,128)(2,1)S(1)} %middle.1._.refs_2_), channel_id=1, source_target_pairs={{0,2},{1,3},{2,0},{3,1},{4,6},{5,7},{6,4},{7,5},{8,10},{9,11},{10,... | collective-permute-start | bytes 1351688 | tf_op jit(solution)/shard_map/ppermute | solution.py:326
  5.0 3.1 %collective-permute-start.1 = (bf16[48,1280]{1,0:T(8,128)(2,1)S(1)}, bf16[48,1280]{1,0:T(8,128)(2,1)S(1)}, u32[]{:S(2)}, u32[]{:S(2)}) collective-permute-start(bf16[48,1280]{1,0:T(8,128)(2,1)S(1)} %relay.1), channel_id=1, source_target_pairs={{0,1},{1,0},{2,3},{3,2},{4,5},{5,4},{6,7},{7,6},{8,9},{9,8},{10,11... | collective-permute-start | bytes 368648 | tf_op jit(solution)/shard_map/ppermute | solution.py:331
  7.2 10.4 %collective-permute-start.9 = (bf16[176,1280]{1,0:T(8,128)(2,1)S(1)}, bf16[176,1280]{1,0:T(8,128)(2,1)S(1)}, u32[]{:S(2)}, u32[]{:S(2)}) collective-permute-start(bf16[176,1280]{1,0:T(8,128)(2,1)S(1)} %middle.1._.refs_2_), channel_id=1, source_target_pairs={{0,1},{1,0},{2,3},{3,2},{4,5},{5,4},{6,7},{7,6},{8,9},{9,8},{10,11... | collective-permute-start | bytes 1351688 | tf_op jit(solution)/shard_map/ppermute | solution.py:331
  8.2 7.8 %collective-permute-start.5 = (bf16[26,1280]{1,0:T(8,128)(2,1)S(1)}, bf16[26,1280]{1,0:T(8,128)(2,1)S(1)}, u32[]{:S(2)}, u32[]{:S(2)}) collective-permute-start(bf16[26,1280]{1,0:T(8,128)(2,1)S(1)} %get-tuple-element.31), channel_id=1, source_target_pairs={{0,4},{8,12},{16,20},{24,28},{4,0},{12,8},{20,16},{28,24},{1,5},{9... | collective-permute-start | bytes 199688 | tf_op jit(solution)/shard_map/ppermute | solution.py:335
  8.5 7.6 %collective-permute-start.6 = (bf16[26,1280]{1,0:T(8,128)(2,1)S(1)}, bf16[26,1280]{1,0:T(8,128)(2,1)S(1)}, u32[]{:S(2)}, u32[]{:S(2)}) collective-permute-start(bf16[26,1280]{1,0:T(8,128)(2,1)S(1)} %get-tuple-element.32), channel_id=1, source_target_pairs={{4,8},{12,16},{20,24},{8,4},{16,12},{24,20},{5,9},{13,17},{21,25},... | collective-permute-start | bytes 199688 | tf_op jit(solution)/shard_map/ppermute | solution.py:335
  15.0 5.0 %collective-permute-start.10 = (bf16[176,1280]{1,0:T(8,128)(2,1)S(1)}, bf16[176,1280]{1,0:T(8,128)(2,1)S(1)}, u32[]{:S(2)}, u32[]{:S(2)}) collective-permute-start(bf16[176,1280]{1,0:T(8,128)(2,1)S(1)} %get-tuple-element.29.refs_4_), channel_id=1, source_target_pairs={{0,1},{1,0},{2,3},{3,2},{4,5},{5,4},{6,7},{7,6},{8,9},{9,8},{10,11... | collective-permute-start | bytes 1351688 | tf_op jit(solution)/shard_map/ppermute | solution.py:331
  16.0 4.0 %collective-permute-start.7 = (bf16[176,1280]{1,0:T(8,128)(2,1)S(1)}, bf16[176,1280]{1,0:T(8,128)(2,1)S(1)}, u32[]{:S(2)}, u32[]{:S(2)}) collective-permute-start(bf16[176,1280]{1,0:T(8,128)(2,1)S(1)} %get-tuple-element.30.refs_0_), channel_id=1, source_target_pairs={{0,1},{1,0},{2,3},{3,2},{4,5},{5,4},{6,7},{7,6},{8,9},{9,8},{10,11... | collective-permute-start | bytes 1351688 | tf_op jit(solution)/shard_map/ppermute | solution.py:331
  16.1 11.5 %collective-permute-start.3 = (bf16[176,1280]{1,0:T(8,128)(2,1)S(1)}, bf16[176,1280]{1,0:T(8,128)(2,1)S(1)}, u32[]{:S(2)}, u32[]{:S(2)}) collective-permute-start(bf16[176,1280]{1,0:T(8,128)(2,1)S(1)} %get-tuple-element.30.refs_0_), channel_id=1, source_target_pairs={{0,2},{1,3},{2,0},{3,1},{4,6},{5,7},{6,4},{7,5},{8,10},{9,11},{10,... | collective-permute-start | bytes 1351688 | tf_op jit(solution)/shard_map/ppermute | solution.py:326
  16.8 2.2 %collective-permute-start.8 = (bf16[48,1280]{1,0:T(8,128)(2,1)S(1)}, bf16[48,1280]{1,0:T(8,128)(2,1)S(1)}, u32[]{:S(2)}, u32[]{:S(2)}) collective-permute-start(bf16[48,1280]{1,0:T(8,128)(2,1)S(1)} %edges.1.refs_1_.refs_3_.refs_5_), channel_id=1, source_target_pairs={{0,1},{1,0},{2,3},{3,2},{4,5},{5,4},{6,7},{7,6},{8,9},{9,8},{10,11... | collective-permute-start | bytes 368648 | tf_op jit(solution)/shard_map/ppermute | solution.py:331
  17.5 12.7 %collective-permute-start.13 = (bf16[48,1280]{1,0:T(8,128)(2,1)S(1)}, bf16[48,1280]{1,0:T(8,128)(2,1)S(1)}, u32[]{:S(2)}, u32[]{:S(2)}) collective-permute-start(bf16[48,1280]{1,0:T(8,128)(2,1)S(1)} %edges.1.refs_1_.refs_3_.refs_5_), channel_id=1, source_target_pairs={{0,2},{1,3},{2,0},{3,1},{4,6},{5,7},{6,4},{7,5},{8,10},{9,11},{10,... | collective-permute-start | bytes 368648 | tf_op jit(solution)/shard_map/ppermute | solution.py:326
  19.0 20.9 %collective-permute-start.2 = (bf16[176,1280]{1,0:T(8,128)(2,1)S(1)}, bf16[176,1280]{1,0:T(8,128)(2,1)S(1)}, u32[]{:S(2)}, u32[]{:S(2)}) collective-permute-start(bf16[176,1280]{1,0:T(8,128)(2,1)S(1)} %get-tuple-element.29.refs_4_), channel_id=1, source_target_pairs={{0,2},{1,3},{2,0},{3,1},{4,6},{5,7},{6,4},{7,5},{8,10},{9,11},{10,... | collective-permute-start | bytes 1351688 | tf_op jit(solution)/shard_map/ppermute | solution.py:326
  30.2 3.1 %collective-permute-start.14 = (bf16[48,1280]{1,0:T(8,128)(2,1)S(1)}, bf16[48,1280]{1,0:T(8,128)(2,1)S(1)}, u32[]{:S(2)}, u32[]{:S(2)}) collective-permute-start(bf16[48,1280]{1,0:T(8,128)(2,1)S(1)} %collective-permute-done.13.refs_1_.refs_3_), channel_id=1, source_target_pairs={{0,1},{1,0},{2,3},{3,2},{4,5},{5,4},{6,7},{7,6},{8,9},{9,8},{10,11... | collective-permute-start | bytes 368648 | tf_op jit(solution)/shard_map/ppermute | solution.py:331
  32.4 3.6 %collective-permute-start.15 = (bf16[96,1280]{1,0:T(8,128)(2,1)S(1)}, bf16[96,1280]{1,0:T(8,128)(2,1)S(1)}, u32[]{:S(2)}, u32[]{:S(2)}) collective-permute-start(bf16[96,1280]{1,0:T(8,128)(2,1)S(1)} %slice.14), channel_id=1, source_target_pairs={{0,1},{1,0},{2,3},{3,2},{4,5},{5,4},{6,7},{7,6},{8,9},{9,8},{10,11... | collective-permute-start | bytes 737288 | tf_op jit(solution)/shard_map/ppermute | solution.py:331
  32.5 3.5 %collective-permute-start.11 = (bf16[96,1280]{1,0:T(8,128)(2,1)S(1)}, bf16[96,1280]{1,0:T(8,128)(2,1)S(1)}, u32[]{:S(2)}, u32[]{:S(2)}) collective-permute-start(bf16[96,1280]{1,0:T(8,128)(2,1)S(1)} %slice.12), channel_id=1, source_target_pairs={{0,1},{1,0},{2,3},{3,2},{4,5},{5,4},{6,7},{7,6},{8,9},{9,8},{10,11... | collective-permute-start | bytes 737288 | tf_op jit(solution)/shard_map/ppermute | solution.py:331
  33.0 3.0 %collective-permute-start.16 = (bf16[80,1280]{1,0:T(8,128)(2,1)S(1)}, bf16[80,1280]{1,0:T(8,128)(2,1)S(1)}, u32[]{:S(2)}, u32[]{:S(2)}) collective-permute-start(bf16[80,1280]{1,0:T(8,128)(2,1)S(1)} %slice.15), channel_id=1, source_target_pairs={{0,1},{1,0},{2,3},{3,2},{4,5},{5,4},{6,7},{7,6},{8,9},{9,8},{10,11... | collective-permute-start | bytes 614408 | tf_op jit(solution)/shard_map/ppermute | solution.py:331
  33.3 2.7 %collective-permute-start.12 = (bf16[80,1280]{1,0:T(8,128)(2,1)S(1)}, bf16[80,1280]{1,0:T(8,128)(2,1)S(1)}, u32[]{:S(2)}, u32[]{:S(2)}) collective-permute-start(bf16[80,1280]{1,0:T(8,128)(2,1)S(1)} %slice.13), channel_id=1, source_target_pairs={{0,1},{1,0},{2,3},{3,2},{4,5},{5,4},{6,7},{7,6},{8,9},{9,8},{10,11... | collective-permute-start | bytes 614408 | tf_op jit(solution)/shard_map/ppermute | solution.py:331
  39.9 3.0 %collective-permute-start.17 = (bf16[176,1280]{1,0:T(8,128)(2,1)S(1)}, bf16[176,1280]{1,0:T(8,128)(2,1)S(1)}, u32[]{:S(2)}, u32[]{:S(2)}) collective-permute-start(bf16[176,1280]{1,0:T(8,128)(2,1)S(1)} %collective-permute-done.2.refs_0_), channel_id=1, source_target_pairs={{0,1},{1,0},{2,3},{3,2},{4,5},{5,4},{6,7},{7,6},{8,9},{9,8},{10,11... | collective-permute-start | bytes 1351688 | tf_op jit(solution)/shard_map/ppermute | solution.py:331

commit v4 on v3

--- a/solution.py
+++ b/solution.py
@@ -12,7 +12,7 @@
 LANES = 128
 EPS = 1e-06
 VMEM_LIMIT = 32 * 1024 * 1024
-K = {'piece': 96, 'pieceA': 96, 'bsplit': 0, 'csplit': 0, 'A2': 'edges', 'B': None, 'C1': None, 'D': None, 'swA': 'X', 'swB': 'X', 'swD': 'X', 'z': 2, 'y': 2}
+K = {'extra': 32, 'early': 8, 'piece': 96, 'pieceA': 96, 'bsplit': 0, 'csplit': 0, 'A2': 'edges', 'B': None, 'C1': None, 'D': None, 'swA': 'X', 'swB': 'X', 'swD': 'X', 'z': 2, 'y': 2}
 BF16 = jnp.bfloat16
 F32 = jnp.float32
 
@@ -87,30 +87,36 @@
     return lax.rem(lax.axis_index(cols_axis), 2)
 
 
-def first_kernel(x_hbm, taps_hbm, cbias_hbm, gain_hbm, nbias_hbm, outer_ref, inner_ref, x_ref, taps_ref, vec_ref, *rest):
+def column(x_ref, first, count, last, lanes):
+    cols = x_ref.shape[1]
+    part = pl.multiple_of(jnp.where(last, cols - GROUP, 0), GROUP)
+    cells = [x_ref[i, pl.ds(part, GROUP), lanes].astype(F32) for i in range(first, first + count)]
+    cells = [jnp.where(last, cell[GROUP - 1 :], cell[:1]) for cell in cells]
+    return jnp.concatenate(cells, axis=0).astype(BF16)
+
+
+def first_kernel(x_hbm, taps_hbm, cbias_hbm, gain_hbm, nbias_hbm, outer_ref, x_ref, taps_ref, vec_ref, *rest):
     *flat, sems = rest
-    rows, cols, width = x_ref.shape
-    pairs = ((x_hbm, x_ref), (taps_hbm, taps_ref), (cbias_hbm, flat[0]), (gain_hbm, flat[1]), (nbias_hbm, flat[2]))
+    rows, _, width = x_ref.shape
+    spans = [pl.ds(at, GROUP) for at in range(0, rows, GROUP)]
+    pairs = [(x_hbm.at[span], x_ref.at[span]) for span in spans]
+    pairs += [(taps_hbm, taps_ref), (cbias_hbm, flat[0]), (gain_hbm, flat[1]), (nbias_hbm, flat[2])]
     copies = [pltpu.make_async_copy(source, target, sems.at[k]) for k, (source, target) in enumerate(pairs)]
     for copy in copies:
         copy.start()
-    for copy in copies:
+    last = core_of("cols") == 1
+    for k, span in enumerate(spans):
+        copies[k].wait()
+        for at in range(0, width, LANES):
+            lanes = pl.ds(at, LANES)
+            outer_ref[span, lanes] = column(x_ref, k * GROUP, GROUP, last, lanes)
+    for copy in copies[len(spans) :]:
         copy.wait()
     for k, ref in enumerate(flat):
         vec_ref[k] = ref[...].reshape(1, width)
-    core = core_of("cols")
-
-    def sides(lanes):
-        left = [x_ref[i, pl.ds(0, GROUP), lanes].astype(F32)[:1] for i in range(rows)]
-        right = [x_ref[i, pl.ds(cols - GROUP, GROUP), lanes].astype(F32)[GROUP - 1 :] for i in range(rows)]
-        left, right = jnp.concatenate(left, axis=0), jnp.concatenate(right, axis=0)
-        outer_ref[:, lanes] = jnp.where(core == 1, right, left).astype(BF16)
-        inner_ref[:, lanes] = jnp.where(core == 1, left, right).astype(BF16)
-
-    each_tile(width, sides)
-
-
-def middle_kernel(x_ref, taps_ref, vec_ref, out_ref, mixed):
+
+
+def middle_kernel(x_ref, taps_ref, vec_ref, out_ref, inner_ref, mixed):
     rows, cols, width = x_ref.shape
     start = 1
     span = slice(GROUP, cols - GROUP)
@@ -122,12 +128,13 @@
             mixed[pl.ds((i - start) * wide, wide), lanes] = value
 
         stencil(taps_ref, vec_ref.at[0], lanes, middle_cells(x_ref, lanes, span), start, count, emit)
+        inner_ref[:, lanes] = column(x_ref, 0, rows, core_of("cols") == 0, lanes)
 
     each_tile(width, tile)
     normalize(mixed, count * wide, vec_ref.at[1], vec_ref.at[2], out_ref)
 
 
-def relay_kernel(beside_ref, before_ref, behind_ref, _, out_ref):
+def relay_kernel(beside_ref, before_ref, behind_ref, out_ref):
     rows = beside_ref.shape[0]
     col, count = lax.axis_index("cols"), lax.axis_size("cols")
     core = core_of("cols")
@@ -341,28 +348,27 @@
     def in_hbm(value):
         return pltpu.with_memory_space_constraint(value, pltpu.HBM)
 
-    outer, beside, x, taps, vectors = call(
+    outer, x, taps, vectors = call(
         first_kernel,
         "first",
         [
-            array(rows, width),
             array(rows, width),
             array(rows, cols, width),
             array(3, 3, width, dtype=F32),
             array(3, 1, width, dtype=F32),
         ],
         [HBM] * 5,
-        [VMEM] * 5,
-        [pltpu.VMEM((width,), F32)] * 3 + [pltpu.SemaphoreType.DMA((5,))],
+        [VMEM] * 4,
+        [pltpu.VMEM((width,), F32)] * 3 + [pltpu.SemaphoreType.DMA((rows // GROUP + 4,))],
     )(*[in_hbm(v) for v in (patches, conv_taps, conv_bias, norm_gain, norm_bias)])
     got_outer = across(outer)
 
-    middle = call(
+    middle, beside = call(
         middle_kernel,
         "middle",
-        array(half, width),
+        [array(half, width), array(rows, width)],
         [VMEM] * 3,
-        VMEM,
+        [VMEM] * 2,
         [pltpu.VMEM((half, width), F32)],
     )(x, taps, vectors)
     got_middle = across(middle)
@@ -372,10 +378,10 @@
             relay_kernel,
             "relay",
             array(2 * rows, width),
-            [VMEM] * 4,
+            [VMEM] * 3,
             VMEM,
             [],
-        )(beside, got_outer[0], got_outer[-1], middle)
+        )(beside, got_outer[0], got_outer[-1])
     )
 
     def cuts(size):

time: 44.8 us -> 44.4 us (level)
  no operation moved by 1% of the time
where the time goes in v4:
time: 44.4 us; the launch traced here: 44.3 us
  Pallas kernels  19 us (43%)
  starting transfers between devices  16.9 us (38%)
  waiting for transfers between devices  8.14 us (18%)
    pallas_call x5, Pallas kernels, project(): call(functools.partial(project_kernel, rows, plan, count, fresh, step, si...  12.9 us
    ppermute x11, starting transfers between devices, swap(): return lax.ppermute(value, 'cols', [(q, q ^ 1) for q in range(side_count)])  8.39 us
    ppermute x5, waiting for transfers between devices, across(): lax.ppermute(value, 'cols', [(q, (q + 2 * step) % side_count) for q in ra...  7.04 us
    ppermute x2, starting transfers between devices, exchange(): return lax.ppermute(value, 'rows', pairs + [(j, i) for i, j in pairs])  4.44 us
    ppermute x5, starting transfers between devices, across(): lax.ppermute(value, 'cols', [(q, (q + 2 * step) % side_count) for q in ra...  4.03 us
    pallas_call x1, Pallas kernels, local(): call(sides_kernel, 'sides', [array(size, width) for size in sizes], [VMEM...  2.34 us
    pallas_call x1, Pallas kernels, local(): call(first_kernel, 'first', [array(rows, width), array(rows, cols, width)...  1.6 us
    pallas_call x1, Pallas kernels, local(): call(middle_kernel, 'middle', [array(half, width), array(rows, width)], [...  1.42 us
  transfers between devices with their start and end apart: 18, of which 6 were waited for; matrix products, arithmetic and copies ran while one was open for 0% of the time, Pallas kernels for 35%

profile of v4, /device:TPU:15, one launch (start us, length us, event | category | flops | bytes accessed | tf_op | source)
XLA Modules:
  0.0 44.3 jit_solution(13488713799309306503)
XLA Ops:
  0.0 0.0 copy-start.1
  0.0 0.0 copy-start
  0.0 1.6 %first.1 = (bf16[24,1280]{1,0:T(8,128)(2,1)S(1)}, bf16[24,24,1280]{2,1,0:T(8,128)(2,1)S(1)}, f32[3,3,1280]{2,1,0:T(4,128)S(1)}, f32[3,1,1280]{2,1,0:T(1,128)S(1)}) custom-call(bf16[24,24,1280]{2,1,0:T(8,128)(2,1)} %x_hbm.1, f32[3,3,1280]{2,1,0:T(4,128)} %taps_hbm.1, f32[1280]{0:T(1024)} %cbias_hbm.1, f32[1280]{0:T(1024)} %gain_hbm.1, f32[1280]{0:T(1024)} %nbias_hbm.1), custom_call_target="tpu_custom_call" | custom-call | flops 1024 | bytes 1024 | tf_op jit(solution)/shard_map/first/pallas_call | solution.py:351
  1.6 0.3 collective-permute-start
  1.9 1.4 %middle.1 = (bf16[176,1280]{1,0:T(8,128)(2,1)S(1)}, bf16[24,1280]{1,0:T(8,128)(2,1)S(1)}) custom-call(bf16[24,24,1280]{2,1,0:T(8,128)(2,1)S(1)} %get-tuple-element.25.x_ref, f32[3,3,1280]{2,1,0:T(4,128)S(1)} %get-tuple-element.26.taps_ref, f32[3,1,1280]{2,1,0:T(1,128)S(1)} %get-tuple-element.27.vec_ref), custom_call_target="tpu_custom_call" | custom-call | flops 1024 | bytes 1024 | tf_op jit(solution)/shard_map/middle/pallas_call | solution.py:366
  3.4 1.3 %collective-permute-start.4 = (bf16[176,1280]{1,0:T(8,128)(2,1)S(1)}, bf16[176,1280]{1,0:T(8,128)(2,1)S(1)}, u32[]{:S(2)}, u32[]{:S(2)}) collective-permute-start(bf16[176,1280]{1,0:T(8,128)(2,1)S(1)} %get-tuple-element.32.refs_2_), channel_id=1, source_target_pairs={{0,2},{1,3},{2,0},{3,1},{4,6},{5,7},{6,4},{7,5},{8,10},{9,11},{10,... | collective-permute-start | bytes 1351688 | tf_op jit(solution)/shard_map/ppermute | solution.py:333
  4.6 0.1 collective-permute-done.before_ref.behind_ref
  4.8 2.0 %collective-permute-start.1 = (bf16[48,1280]{1,0:T(8,128)(2,1)S(1)}, bf16[48,1280]{1,0:T(8,128)(2,1)S(1)}, u32[]{:S(2)}, u32[]{:S(2)}) collective-permute-start(bf16[48,1280]{1,0:T(8,128)(2,1)S(1)} %relay.1), channel_id=1, source_target_pairs={{0,1},{1,0},{2,3},{3,2},{4,5},{5,4},{6,7},{7,6},{8,9},{9,8},{10,11... | collective-permute-start | bytes 368648 | tf_op jit(solution)/shard_map/ppermute | solution.py:338
  6.8 0.1 collective-permute-start.9
  6.9 0.9 %collective-permute-done.1.sides_ref = bf16[48,1280]{1,0:T(8,128)(2,1)S(1)} collective-permute-done((bf16[48,1280]{1,0:T(8,128)(2,1)S(1)}, bf16[48,1280]{1,0:T(8,128)(2,1)S(1)}, u32[]{:S(2)}, u32[]{:S(2)}) %collective-permute-start.1) | collective-permute-done | bytes 122912 | tf_op jit(solution)/shard_map/ppermute | solution.py:338
  7.8 0.1 ends.1
  7.8 0.3 collective-permute-start.5
  8.1 4.1 %collective-permute-start.6 = (bf16[26,1280]{1,0:T(8,128)(2,1)S(1)}, bf16[26,1280]{1,0:T(8,128)(2,1)S(1)}, u32[]{:S(2)}, u32[]{:S(2)}) collective-permute-start(bf16[26,1280]{1,0:T(8,128)(2,1)S(1)} %get-tuple-element.34), channel_id=1, source_target_pairs={{4,8},{12,16},{20,24},{8,4},{16,12},{24,20},{5,9},{13,17},{21,25},... | collective-permute-start | bytes 199688 | tf_op jit(solution)/shard_map/ppermute | solution.py:342
  12.3 2.3 %sides.1 = (bf16[176,1280]{1,0:T(8,128)(2,1)S(1)}, bf16[176,1280]{1,0:T(8,128)(2,1)S(1)}) custom-call(bf16[24,24,1280]{2,1,0:T(8,128)(2,1)S(1)} %get-tuple-element.25.x_ref, bf16[48,1280]{1,0:T(8,128)(2,1)S(1)} %collective-permute-done.1.sides_ref, f32[3,3,1280]{2,1,0:T(4,128)S(1)} %get-tuple-element.26.taps_ref, f32[3,1,1280]{2,1,0:T(1,128)S(1)} %get-tuple-element.27.vec_ref), custom_call_target="tpu_custom_call" | custom-call | flops 1024 | bytes 1024 | tf_op jit(solution)/shard_map/sides/pallas_call | solution.py:399
  14.6 1.0 %collective-permute-start.10 = (bf16[176,1280]{1,0:T(8,128)(2,1)S(1)}, bf16[176,1280]{1,0:T(8,128)(2,1)S(1)}, u32[]{:S(2)}, u32[]{:S(2)}) collective-permute-start(bf16[176,1280]{1,0:T(8,128)(2,1)S(1)} %get-tuple-element.30.refs_4_), channel_id=1, source_target_pairs={{0,1},{1,0},{2,3},{3,2},{4,5},{5,4},{6,7},{7,6},{8,9},{9,8},{10,11... | collective-permute-start | bytes 1351688 | tf_op jit(solution)/shard_map/ppermute | solution.py:338
  15.6 0.0 collective-permute-done.5.pair_ref
  15.6 0.1 collective-permute-start.7
  15.7 0.0 collective-permute-done.6.cross_ref
  15.7 0.2 collective-permute-start.3
  15.9 0.0 collective-permute-done.4.refs_2_
  15.9 0.7 %edges.1.refs_1_.refs_3_.refs_5_ = bf16[48,1280]{1,0:T(8,128)(2,1)S(1)} custom-call(bf16[24,24,1280]{2,1,0:T(8,128)(2,1)S(1)} %get-tuple-element.25.x_ref, bf16[48,1280]{1,0:T(8,128)(2,1)S(1)} %collective-permute-done.1.sides_ref, bf16[26,1280]{1,0:T(8,128)(2,1)S(1)} %collective-permute-done.5.pair_ref, ...), custom_call_target="tpu_custom_call" | custom-call | flops 1024 | bytes 1024 | tf_op jit(solution)/shard_map/edges/pallas_call | solution.py:420
  16.5 0.8 %collective-permute-start.8 = (bf16[48,1280]{1,0:T(8,128)(2,1)S(1)}, bf16[48,1280]{1,0:T(8,128)(2,1)S(1)}, u32[]{:S(2)}, u32[]{:S(2)}) collective-permute-start(bf16[48,1280]{1,0:T(8,128)(2,1)S(1)} %edges.1.refs_1_.refs_3_.refs_5_), channel_id=1, source_target_pairs={{0,1},{1,0},{2,3},{3,2},{4,5},{5,4},{6,7},{7,6},{8,9},{9,8},{10,11... | collective-permute-start | bytes 368648 | tf_op jit(solution)/shard_map/ppermute | solution.py:338
  17.3 0.0 collective-permute-done.9.refs_8_
  17.3 1.3 %collective-permute-start.13 = (bf16[48,1280]{1,0:T(8,128)(2,1)S(1)}, bf16[48,1280]{1,0:T(8,128)(2,1)S(1)}, u32[]{:S(2)}, u32[]{:S(2)}) collective-permute-start(bf16[48,1280]{1,0:T(8,128)(2,1)S(1)} %edges.1.refs_1_.refs_3_.refs_5_), channel_id=1, source_target_pairs={{0,2},{1,3},{2,0},{3,1},{4,6},{5,7},{6,4},{7,5},{8,10},{9,11},{10,... | collective-permute-start | bytes 368648 | tf_op jit(solution)/shard_map/ppermute | solution.py:333
  18.6 0.0 collective-permute-done.8.refs_7_.refs_9_.refs_11_
  18.6 1.0 %collective-permute-start.2 = (bf16[176,1280]{1,0:T(8,128)(2,1)S(1)}, bf16[176,1280]{1,0:T(8,128)(2,1)S(1)}, u32[]{:S(2)}, u32[]{:S(2)}) collective-permute-start(bf16[176,1280]{1,0:T(8,128)(2,1)S(1)} %get-tuple-element.30.refs_4_), channel_id=1, source_target_pairs={{0,2},{1,3},{2,0},{3,1},{4,6},{5,7},{6,4},{7,5},{8,10},{9,11},{10,... | collective-permute-start | bytes 1351688 | tf_op jit(solution)/shard_map/ppermute | solution.py:333
  19.6 0.0 collective-permute-done.10.refs_10_
  19.6 0.0 collective-permute-done.7.refs_6_
  19.6 0.0 copy-done.1
  19.6 0.0 copy-done
  19.6 4.9 %project.5.refs_6_ = bf16[3,4,24,7680]{3,2,1,0:T(8,128)(2,1)} custom-call(bf16[176,1280]{1,0:T(8,128)(2,1)S(1)} %get-tuple-element.31.refs_0_, bf16[48,1280]{1,0:T(8,128)(2,1)S(1)} %edges.1.refs_1_.refs_3_.refs_5_, bf16[176,1280]{1,0:T(8,128)(2,1)S(1)} %get-tuple-element.32.refs_2_, bf16[48,1280]{1,0:T(8,128)(2,1)S(1)} %edges.1.refs_1_.refs_3_.refs_5_, ...), custom_call_target="tpu_custom_call" | custom-call | flops 1024 | bytes 1024 | tf_op jit(solution)/shard_map/project/pallas_call | solution.py:303
  24.5 2.7 %collective-permute-done.3.refs_0_ = bf16[176,1280]{1,0:T(8,128)(2,1)S(1)} collective-permute-done((bf16[176,1280]{1,0:T(8,128)(2,1)S(1)}, bf16[176,1280]{1,0:T(8,128)(2,1)S(1)}, u32[]{:S(2)}, u32[]{:S(2)}) %collective-permute-start.3) | collective-permute-done | bytes 450592 | tf_op jit(solution)/shard_map/ppermute | solution.py:333
  27.2 2.6 %collective-permute-done.13.refs_1_.refs_3_ = bf16[48,1280]{1,0:T(8,128)(2,1)S(1)} collective-permute-done((bf16[48,1280]{1,0:T(8,128)(2,1)S(1)}, bf16[48,1280]{1,0:T(8,128)(2,1)S(1)}, u32[]{:S(2)}, u32[]{:S(2)}) %collective-permute-start.13) | collective-permute-done | bytes 122912 | tf_op jit(solution)/shard_map/ppermute | solution.py:333
  29.8 2.1 %collective-permute-start.14 = (bf16[48,1280]{1,0:T(8,128)(2,1)S(1)}, bf16[48,1280]{1,0:T(8,128)(2,1)S(1)}, u32[]{:S(2)}, u32[]{:S(2)}) collective-permute-start(bf16[48,1280]{1,0:T(8,128)(2,1)S(1)} %collective-permute-done.13.refs_1_.refs_3_), channel_id=1, source_target_pairs={{0,1},{1,0},{2,3},{3,2},{4,5},{5,4},{6,7},{7,6},{8,9},{9,8},{10,11... | collective-permute-start | bytes 368648 | tf_op jit(solution)/shard_map/ppermute | solution.py:338
  32.0 0.1 collective-permute-start.15
  32.1 0.5 %collective-permute-start.11 = (bf16[96,1280]{1,0:T(8,128)(2,1)S(1)}, bf16[96,1280]{1,0:T(8,128)(2,1)S(1)}, u32[]{:S(2)}, u32[]{:S(2)}) collective-permute-start(bf16[96,1280]{1,0:T(8,128)(2,1)S(1)} %slice.12), channel_id=1, source_target_pairs={{0,1},{1,0},{2,3},{3,2},{4,5},{5,4},{6,7},{7,6},{8,9},{9,8},{10,11... | collective-permute-start | bytes 737288 | tf_op jit(solution)/shard_map/ppermute | solution.py:338
  32.6 0.1 collective-permute-start.16
  32.8 0.2 collective-permute-done.14.refs_2_.refs_5_.refs_1_
  32.9 0.4 collective-permute-start.12
  33.3 2.3 %project.6.refs_8_ = bf16[3,4,24,7680]{3,2,1,0:T(8,128)(2,1)} custom-call(bf16[176,1280]{1,0:T(8,128)(2,1)S(1)} %collective-permute-done.3.refs_0_, bf16[48,1280]{1,0:T(8,128)(2,1)S(1)} %collective-permute-done.13.refs_1_.refs_3_, bf16[176,1280]{1,0:T(8,128)(2,1)S(1)} %collective-permute-done.4.refs_2_, ...), custom_call_target="tpu_custom_call", output_to_operand_aliasing={{}: (6, {})} | custom-call | flops 1024 | bytes 1024 | tf_op jit(solution)/shard_map/project/pallas_call | solution.py:303
  35.6 0.0 collective-permute-done.16.refs_4_
  35.6 0.0 collective-permute-done.12.refs_1_
  35.6 0.0 collective-permute-done.15.refs_3_
  35.6 0.0 collective-permute-done.11.refs_0_
  35.6 2.3 %project.7.refs_4_ = bf16[3,4,24,7680]{3,2,1,0:T(8,128)(2,1)} custom-call(bf16[96,1280]{1,0:T(8,128)(2,1)S(1)} %collective-permute-done.11.refs_0_, bf16[80,1280]{1,0:T(8,128)(2,1)S(1)} %collective-permute-done.12.refs_1_, bf16[48,1280]{1,0:T(8,128)(2,1)S(1)} %collective-permute-done.14.refs_2_.refs_5_.refs_1_, ...), custom_call_target="tpu_custom_call", output_to_operand_aliasing={{}: (8, {})} | custom-call | flops 1024 | bytes 1024 | tf_op jit(solution)/shard_map/project/pallas_call | solution.py:303
  37.9 1.6 %collective-permute-done.2.refs_0_ = bf16[176,1280]{1,0:T(8,128)(2,1)S(1)} collective-permute-done((bf16[176,1280]{1,0:T(8,128)(2,1)S(1)}, bf16[176,1280]{1,0:T(8,128)(2,1)S(1)}, u32[]{:S(2)}, u32[]{:S(2)}) %collective-permute-start.2) | collective-permute-done | bytes 450592 | tf_op jit(solution)/shard_map/ppermute | solution.py:333
  39.5 1.3 %collective-permute-start.17 = (bf16[176,1280]{1,0:T(8,128)(2,1)S(1)}, bf16[176,1280]{1,0:T(8,128)(2,1)S(1)}, u32[]{:S(2)}, u32[]{:S(2)}) collective-permute-start(bf16[176,1280]{1,0:T(8,128)(2,1)S(1)} %collective-permute-done.2.refs_0_), channel_id=1, source_target_pairs={{0,1},{1,0},{2,3},{3,2},{4,5},{5,4},{6,7},{7,6},{8,9},{9,8},{10,11... | collective-permute-start | bytes 1351688 | tf_op jit(solution)/shard_map/ppermute | solution.py:338
  40.8 1.8 %project.8.refs_4_ = bf16[3,4,24,7680]{3,2,1,0:T(8,128)(2,1)} custom-call(bf16[176,1280]{1,0:T(8,128)(2,1)S(1)} %collective-permute-done.2.refs_0_, bf16[48,1280]{1,0:T(8,128)(2,1)S(1)} %collective-permute-done.13.refs_1_.refs_3_, bf16[3,320,1280]{2,1,0:T(8,128)(2,1)S(1)} %bitcast.4, bf16[3,320]{1,0:T(4,128)(2,1)S(1)} %copy-done.1, ...), custom_call_target="tpu_custom_call", output_to_operand_aliasing={{}: (4, {})} | custom-call | flops 1024 | bytes 1024 | tf_op jit(solution)/shard_map/project/pallas_call | solution.py:303
  42.5 0.0 collective-permute-done.17.refs_0_
  42.5 1.7 %project.9 = bf16[3,4,24,7680]{3,2,1,0:T(8,128)(2,1)} custom-call(bf16[176,1280]{1,0:T(8,128)(2,1)S(1)} %collective-permute-done.17.refs_0_, bf16[48,1280]{1,0:T(8,128)(2,1)S(1)} %collective-permute-done.14.refs_2_.refs_5_.refs_1_, bf16[3,320,1280]{2,1,0:T(8,128)(2,1)S(1)} %bitcast.5, bf16[3,320]{1,0:T(4,128)(2,1)S(1)} %copy-done.1, ...), custom_call_target="tpu_custom_call", output_to_operand_aliasing={{}: (4, {})} | custom-call | flops 1024 | bytes 1024 | tf_op jit(solution)/shard_map/project/pallas_call | solution.py:303
  (5 shorter events, 0.1 us)
Async XLA Ops:
  0.0 19.6 %copy-start.1 = (bf16[3,320]{1,0:T(4,128)(2,1)S(1)}, bf16[3,320]{1,0:T(4,128)(2,1)}, u32[]{:S(2)}) copy-start(bf16[3,320]{1,0:T(4,128)(2,1)} %refs_3_.3) | copy-start | bytes 5764
  0.0 19.6 %copy-start = (bf16[3,1280,320]{1,2,0:T(8,128)(2,1)S(1)}, bf16[3,1280,320]{1,2,0:T(8,128)(2,1)}, u32[]{:S(2)}) copy-start(bf16[3,1280,320]{1,2,0:T(8,128)(2,1)} %param.12) | copy-start | bytes 7372804
  1.6 3.1 %collective-permute-start = (bf16[24,1280]{1,0:T(8,128)(2,1)S(1)}, bf16[24,1280]{1,0:T(8,128)(2,1)S(1)}, u32[]{:S(2)}, u32[]{:S(2)}) collective-permute-start(bf16[24,1280]{1,0:T(8,128)(2,1)S(1)} %get-tuple-element.29), channel_id=1, source_target_pairs={{0,2},{1,3},{2,0},{3,1},{4,6},{5,7},{6,4},{7,5},{8,10},{9,11},{10,... | collective-permute-start | bytes 184328 | tf_op jit(solution)/shard_map/ppermute | solution.py:333
  3.4 12.5 %collective-permute-start.4 = (bf16[176,1280]{1,0:T(8,128)(2,1)S(1)}, bf16[176,1280]{1,0:T(8,128)(2,1)S(1)}, u32[]{:S(2)}, u32[]{:S(2)}) collective-permute-start(bf16[176,1280]{1,0:T(8,128)(2,1)S(1)} %get-tuple-element.32.refs_2_), channel_id=1, source_target_pairs={{0,2},{1,3},{2,0},{3,1},{4,6},{5,7},{6,4},{7,5},{8,10},{9,11},{10,... | collective-permute-start | bytes 1351688 | tf_op jit(solution)/shard_map/ppermute | solution.py:333
  4.8 3.0 %collective-permute-start.1 = (bf16[48,1280]{1,0:T(8,128)(2,1)S(1)}, bf16[48,1280]{1,0:T(8,128)(2,1)S(1)}, u32[]{:S(2)}, u32[]{:S(2)}) collective-permute-start(bf16[48,1280]{1,0:T(8,128)(2,1)S(1)} %relay.1), channel_id=1, source_target_pairs={{0,1},{1,0},{2,3},{3,2},{4,5},{5,4},{6,7},{7,6},{8,9},{9,8},{10,11... | collective-permute-start | bytes 368648 | tf_op jit(solution)/shard_map/ppermute | solution.py:338
  6.8 10.5 %collective-permute-start.9 = (bf16[176,1280]{1,0:T(8,128)(2,1)S(1)}, bf16[176,1280]{1,0:T(8,128)(2,1)S(1)}, u32[]{:S(2)}, u32[]{:S(2)}) collective-permute-start(bf16[176,1280]{1,0:T(8,128)(2,1)S(1)} %get-tuple-element.32.refs_2_), channel_id=1, source_target_pairs={{0,1},{1,0},{2,3},{3,2},{4,5},{5,4},{6,7},{7,6},{8,9},{9,8},{10,11... | collective-permute-start | bytes 1351688 | tf_op jit(solution)/shard_map/ppermute | solution.py:338
  7.8 7.8 %collective-permute-start.5 = (bf16[26,1280]{1,0:T(8,128)(2,1)S(1)}, bf16[26,1280]{1,0:T(8,128)(2,1)S(1)}, u32[]{:S(2)}, u32[]{:S(2)}) collective-permute-start(bf16[26,1280]{1,0:T(8,128)(2,1)S(1)} %get-tuple-element.33), channel_id=1, source_target_pairs={{0,4},{8,12},{16,20},{24,28},{4,0},{12,8},{20,16},{28,24},{1,5},{9... | collective-permute-start | bytes 199688 | tf_op jit(solution)/shard_map/ppermute | solution.py:342
  8.1 7.6 %collective-permute-start.6 = (bf16[26,1280]{1,0:T(8,128)(2,1)S(1)}, bf16[26,1280]{1,0:T(8,128)(2,1)S(1)}, u32[]{:S(2)}, u32[]{:S(2)}) collective-permute-start(bf16[26,1280]{1,0:T(8,128)(2,1)S(1)} %get-tuple-element.34), channel_id=1, source_target_pairs={{4,8},{12,16},{20,24},{8,4},{16,12},{24,20},{5,9},{13,17},{21,25},... | collective-permute-start | bytes 199688 | tf_op jit(solution)/shard_map/ppermute | solution.py:342
  14.6 5.0 %collective-permute-start.10 = (bf16[176,1280]{1,0:T(8,128)(2,1)S(1)}, bf16[176,1280]{1,0:T(8,128)(2,1)S(1)}, u32[]{:S(2)}, u32[]{:S(2)}) collective-permute-start(bf16[176,1280]{1,0:T(8,128)(2,1)S(1)} %get-tuple-element.30.refs_4_), channel_id=1, source_target_pairs={{0,1},{1,0},{2,3},{3,2},{4,5},{5,4},{6,7},{7,6},{8,9},{9,8},{10,11... | collective-permute-start | bytes 1351688 | tf_op jit(solution)/shard_map/ppermute | solution.py:338
  15.6 4.0 %collective-permute-start.7 = (bf16[176,1280]{1,0:T(8,128)(2,1)S(1)}, bf16[176,1280]{1,0:T(8,128)(2,1)S(1)}, u32[]{:S(2)}, u32[]{:S(2)}) collective-permute-start(bf16[176,1280]{1,0:T(8,128)(2,1)S(1)} %get-tuple-element.31.refs_0_), channel_id=1, source_target_pairs={{0,1},{1,0},{2,3},{3,2},{4,5},{5,4},{6,7},{7,6},{8,9},{9,8},{10,11... | collective-permute-start | bytes 1351688 | tf_op jit(solution)/shard_map/ppermute | solution.py:338
  15.7 11.5 %collective-permute-start.3 = (bf16[176,1280]{1,0:T(8,128)(2,1)S(1)}, bf16[176,1280]{1,0:T(8,128)(2,1)S(1)}, u32[]{:S(2)}, u32[]{:S(2)}) collective-permute-start(bf16[176,1280]{1,0:T(8,128)(2,1)S(1)} %get-tuple-element.31.refs_0_), channel_id=1, source_target_pairs={{0,2},{1,3},{2,0},{3,1},{4,6},{5,7},{6,4},{7,5},{8,10},{9,11},{10,... | collective-permute-start | bytes 1351688 | tf_op jit(solution)/shard_map/ppermute | solution.py:333
  16.5 2.1 %collective-permute-start.8 = (bf16[48,1280]{1,0:T(8,128)(2,1)S(1)}, bf16[48,1280]{1,0:T(8,128)(2,1)S(1)}, u32[]{:S(2)}, u32[]{:S(2)}) collective-permute-start(bf16[48,1280]{1,0:T(8,128)(2,1)S(1)} %edges.1.refs_1_.refs_3_.refs_5_), channel_id=1, source_target_pairs={{0,1},{1,0},{2,3},{3,2},{4,5},{5,4},{6,7},{7,6},{8,9},{9,8},{10,11... | collective-permute-start | bytes 368648 | tf_op jit(solution)/shard_map/ppermute | solution.py:338
  17.3 12.5 %collective-permute-start.13 = (bf16[48,1280]{1,0:T(8,128)(2,1)S(1)}, bf16[48,1280]{1,0:T(8,128)(2,1)S(1)}, u32[]{:S(2)}, u32[]{:S(2)}) collective-permute-start(bf16[48,1280]{1,0:T(8,128)(2,1)S(1)} %edges.1.refs_1_.refs_3_.refs_5_), channel_id=1, source_target_pairs={{0,2},{1,3},{2,0},{3,1},{4,6},{5,7},{6,4},{7,5},{8,10},{9,11},{10,... | collective-permute-start | bytes 368648 | tf_op jit(solution)/shard_map/ppermute | solution.py:333
  18.6 20.9 %collective-permute-start.2 = (bf16[176,1280]{1,0:T(8,128)(2,1)S(1)}, bf16[176,1280]{1,0:T(8,128)(2,1)S(1)}, u32[]{:S(2)}, u32[]{:S(2)}) collective-permute-start(bf16[176,1280]{1,0:T(8,128)(2,1)S(1)} %get-tuple-element.30.refs_4_), channel_id=1, source_target_pairs={{0,2},{1,3},{2,0},{3,1},{4,6},{5,7},{6,4},{7,5},{8,10},{9,11},{10,... | collective-permute-start | bytes 1351688 | tf_op jit(solution)/shard_map/ppermute | solution.py:333
  29.8 3.1 %collective-permute-start.14 = (bf16[48,1280]{1,0:T(8,128)(2,1)S(1)}, bf16[48,1280]{1,0:T(8,128)(2,1)S(1)}, u32[]{:S(2)}, u32[]{:S(2)}) collective-permute-start(bf16[48,1280]{1,0:T(8,128)(2,1)S(1)} %collective-permute-done.13.refs_1_.refs_3_), channel_id=1, source_target_pairs={{0,1},{1,0},{2,3},{3,2},{4,5},{5,4},{6,7},{7,6},{8,9},{9,8},{10,11... | collective-permute-start | bytes 368648 | tf_op jit(solution)/shard_map/ppermute | solution.py:338
  32.0 3.6 %collective-permute-start.15 = (bf16[96,1280]{1,0:T(8,128)(2,1)S(1)}, bf16[96,1280]{1,0:T(8,128)(2,1)S(1)}, u32[]{:S(2)}, u32[]{:S(2)}) collective-permute-start(bf16[96,1280]{1,0:T(8,128)(2,1)S(1)} %slice.14), channel_id=1, source_target_pairs={{0,1},{1,0},{2,3},{3,2},{4,5},{5,4},{6,7},{7,6},{8,9},{9,8},{10,11... | collective-permute-start | bytes 737288 | tf_op jit(solution)/shard_map/ppermute | solution.py:338
  32.1 3.5 %collective-permute-start.11 = (bf16[96,1280]{1,0:T(8,128)(2,1)S(1)}, bf16[96,1280]{1,0:T(8,128)(2,1)S(1)}, u32[]{:S(2)}, u32[]{:S(2)}) collective-permute-start(bf16[96,1280]{1,0:T(8,128)(2,1)S(1)} %slice.12), channel_id=1, source_target_pairs={{0,1},{1,0},{2,3},{3,2},{4,5},{5,4},{6,7},{7,6},{8,9},{9,8},{10,11... | collective-permute-start | bytes 737288 | tf_op jit(solution)/shard_map/ppermute | solution.py:338
  32.6 3.0 %collective-permute-start.16 = (bf16[80,1280]{1,0:T(8,128)(2,1)S(1)}, bf16[80,1280]{1,0:T(8,128)(2,1)S(1)}, u32[]{:S(2)}, u32[]{:S(2)}) collective-permute-start(bf16[80,1280]{1,0:T(8,128)(2,1)S(1)} %slice.15), channel_id=1, source_target_pairs={{0,1},{1,0},{2,3},{3,2},{4,5},{5,4},{6,7},{7,6},{8,9},{9,8},{10,11... | collective-permute-start | bytes 614408 | tf_op jit(solution)/shard_map/ppermute | solution.py:338
  32.9 2.7 %collective-permute-start.12 = (bf16[80,1280]{1,0:T(8,128)(2,1)S(1)}, bf16[80,1280]{1,0:T(8,128)(2,1)S(1)}, u32[]{:S(2)}, u32[]{:S(2)}) collective-permute-start(bf16[80,1280]{1,0:T(8,128)(2,1)S(1)} %slice.13), channel_id=1, source_target_pairs={{0,1},{1,0},{2,3},{3,2},{4,5},{5,4},{6,7},{7,6},{8,9},{9,8},{10,11... | collective-permute-start | bytes 614408 | tf_op jit(solution)/shard_map/ppermute | solution.py:338
  39.5 3.0 %collective-permute-start.17 = (bf16[176,1280]{1,0:T(8,128)(2,1)S(1)}, bf16[176,1280]{1,0:T(8,128)(2,1)S(1)}, u32[]{:S(2)}, u32[]{:S(2)}) collective-permute-start(bf16[176,1280]{1,0:T(8,128)(2,1)S(1)} %collective-permute-done.2.refs_0_), channel_id=1, source_target_pairs={{0,1},{1,0},{2,3},{3,2},{4,5},{5,4},{6,7},{7,6},{8,9},{9,8},{10,11... | collective-permute-start | bytes 1351688 | tf_op jit(solution)/shard_map/ppermute | solution.py:338

commit v5 on v4

--- a/solution.py
+++ b/solution.py
@@ -12,7 +12,7 @@
 LANES = 128
 EPS = 1e-06
 VMEM_LIMIT = 32 * 1024 * 1024
-K = {'extra': 32, 'early': 8, 'piece': 96, 'pieceA': 96, 'bsplit': 0, 'csplit': 0, 'A2': 'edges', 'B': None, 'C1': None, 'D': None, 'swA': 'X', 'swB': 'X', 'swD': 'X', 'z': 2, 'y': 2}
+K = {'pieceF': 128, 'extra': 32, 'early': 8, 'piece': 96, 'pieceA': 96, 'bsplit': 0, 'csplit': 0, 'A2': 'edges', 'B': None, 'C1': None, 'D': None, 'swA': 'X', 'swB': 'X', 'swD': 'X', 'z': 2, 'y': 2}
 BF16 = jnp.bfloat16
 F32 = jnp.float32
 
@@ -163,44 +163,30 @@
         ref[cols:, :] = jnp.concatenate(ends, axis=0).astype(BF16)
 
 
-def sides_kernel(
-    x_ref, sides_ref, taps_ref, vec_ref, *refs
-):
+def side_kernel(last, x_ref, sides_ref, taps_ref, vec_ref, out_ref, beside, mixed):
     rows, cols, width = x_ref.shape
     place = lax.broadcasted_iota(jnp.int32, (GROUP, LANES), 0)
-    *outs, lefts, rights, mixed = refs
-    inner = rows - 2
-    half = inner * GROUP
-    lefts[...], rights[...] = halves(sides_ref, rows, slice(None))
+    beside[...] = halves(sides_ref, rows, slice(None))[last]
+
     def tile(lanes):
-        def near(i):
+        def cells(i):
             x = x_ref[i, :, lanes].astype(F32)
+            edge = beside[pl.ds(i, 1), lanes]
+            if last:
+                here, both = x[cols - GROUP :], x[cols - 2 * GROUP :]
+                r = jnp.where(place == GROUP - 1, edge, pltpu.roll(here, GROUP - 1, 0))
+                return pltpu.roll(both, 1, 0)[GROUP:], here, r
             here, both = x[:GROUP], x[: 2 * GROUP]
-            l = jnp.where(place == 0, lefts[pl.ds(i, 1), lanes], pltpu.roll(here, 1, 0))
+            l = jnp.where(place == 0, edge, pltpu.roll(here, 1, 0))
             return l, here, pltpu.roll(both, 2 * GROUP - 1, 0)[:GROUP]
 
-        def far(i):
-            x = x_ref[i, :, lanes].astype(F32)
-            here, both = x[cols - GROUP :], x[cols - 2 * GROUP :]
-            r = jnp.where(place == GROUP - 1, rights[pl.ds(i, 1), lanes], pltpu.roll(here, GROUP - 1, 0))
-            return pltpu.roll(both, 1, 0)[GROUP:], here, r
-
-        def emit_near(i, value):
+        def emit(i, value):
             mixed[pl.ds((i - 1) * GROUP, GROUP), lanes] = value
 
-        def emit_far(i, value):
-            mixed[pl.ds((inner + i - 1) * GROUP, GROUP), lanes] = value
-
-        stencil(taps_ref, vec_ref.at[0], lanes, near, 1, inner, emit_near)
-        stencil(taps_ref, vec_ref.at[0], lanes, far, 1, inner, emit_far)
+        stencil(taps_ref, vec_ref.at[0], lanes, cells, 1, rows - 2, emit)
 
     each_tile(width, tile)
-    gain, nbias = vec_ref.at[1], vec_ref.at[2]
-    base = 0
-    for ref in outs:
-        count = ref.shape[0]
-        normalize(mixed.at[pl.ds(base, count)], count, gain, nbias, ref)
-        base += count
+    normalize(mixed, mixed.shape[0], vec_ref.at[1], vec_ref.at[2], out_ref)
 
 
 def edges_kernel(x_ref, sides_ref, pair_ref, cross_ref, taps_ref, vec_ref, out_ref, mixed):
@@ -384,10 +370,6 @@
         )(beside, got_outer[0], got_outer[-1])
     )
 
-    def cuts(size):
-        return [size, half - size] if size else [half]
-
-    sizes = cuts(K["bsplit"]) + cuts(K["csplit"])
     pair, cross = call(
         ends_kernel,
         "ends",
@@ -396,16 +378,17 @@
         [VMEM] * 2,
         [],
     )(x, sides)
-    parts = call(
-        sides_kernel,
-        "sides",
-        [array(size, width) for size in sizes],
-        [VMEM] * 4,
-        [VMEM] * len(sizes),
-        [pltpu.VMEM((rows, width), F32)] * 2 + [pltpu.VMEM((2 * half, width), F32)],
-    )(x, sides, taps, vectors)
-    count = len(cuts(K["bsplit"]))
-    near, far = parts[:count], parts[count:]
+    def side(last):
+        return call(
+            functools.partial(side_kernel, last),
+            "side",
+            array(half, width),
+            [VMEM] * 4,
+            VMEM,
+            [pltpu.VMEM((rows, width), F32), pltpu.VMEM((half, width), F32)],
+        )(x, sides, taps, vectors)
+
+    near, far = [side(0)], [side(1)]
     got_near = [across(v) for v in near]
     got_far = [across(v) for v in far]
     marks = {"A2": got_middle, "B": sum(got_near, []), "C1": got_far[0]}
@@ -457,7 +440,7 @@
     out = step_on(
         None,
         groups_of(near, [held], edge, far, 0)
-        + groups_of([swap(v) for v in near], [swap(middle)], swap(late), [swap(v) for v in far], 1),
+        + groups_of([swap(v) for v in near], [swap(middle)], swap(late), [swap(far[0][p : p + K['pieceF']]) for p in range(0, half, K['pieceF'])], 1),
         0,
     )
     for step in steps:

time: 44.4 us -> 43.4 us (0.977)
  starting transfers between devices: 16.9 us -> 15 us
  waiting for transfers between devices: 8.14 us -> 8.63 us
    ppermute x11 -> x12, starting transfers between devices: 8.39 us -> 7.3 us  [swap(): return lax.ppermute(value, 'cols', [(q, q ^ 1) for q in range(side_count)])]
    ppermute x5, starting transfers between devices: 4.03 us -> 3.23 us  [across(): lax.ppermute(value, 'cols', [(q, (q + 2 * step) % side_count) for q in ra...]
    ppermute x11 -> x12, waiting for transfers between devices: 1.09 us -> 1.64 us  [swap(): return lax.ppermute(value, 'cols', [(q, q ^ 1) for q in range(side_count)])]
    pallas_call x1 -> x2, Pallas kernels: 2.34 us -> 2.48 us  [side(): call(functools.partial(side_kernel, last), 'side', array(half, width), [V...]
  transfers between devices with their start and end apart: 18 -> 19, of which waited for: 6 -> 7; matrix products, arithmetic and copies ran while one was open for 0% -> 0% of each run, Pallas kernels for 35% -> 37%
where the time goes in v5:
time: 43.4 us; the launch traced here: 43 us
  Pallas kernels  19 us (44%)
  starting transfers between devices  15 us (35%)
  waiting for transfers between devices  8.63 us (20%)
    pallas_call x5, Pallas kernels, project(): call(functools.partial(project_kernel, rows, plan, count, fresh, step, si...  12.9 us
    ppermute x12, starting transfers between devices, swap(): return lax.ppermute(value, 'cols', [(q, q ^ 1) for q in range(side_count)])  7.3 us
    ppermute x5, waiting for transfers between devices, across(): lax.ppermute(value, 'cols', [(q, (q + 2 * step) % side_count) for q in ra...  6.99 us
    ppermute x2, starting transfers between devices, exchange(): return lax.ppermute(value, 'rows', pairs + [(j, i) for i, j in pairs])  4.44 us
    ppermute x5, starting transfers between devices, across(): lax.ppermute(value, 'cols', [(q, (q + 2 * step) % side_count) for q in ra...  3.23 us
    pallas_call x2, Pallas kernels, side(): call(functools.partial(side_kernel, last), 'side', array(half, width), [V...  2.48 us
    ppermute x12, waiting for transfers between devices, swap(): return lax.ppermute(value, 'cols', [(q, q ^ 1) for q in range(side_count)])  1.64 us
    pallas_call x1, Pallas kernels, local(): call(first_kernel, 'first', [array(rows, width), array(rows, cols, width)...  1.45 us
  transfers between devices with their start and end apart: 19, of which 7 were waited for; matrix products, arithmetic and copies ran while one was open for 0% of the time, Pallas kernels for 37%

profile of v5, /device:TPU:15, one launch (start us, length us, event | category | flops | bytes accessed | tf_op | source)
XLA Modules:
  0.0 43.0 jit_solution(14507386841421527996)
XLA Ops:
  0.0 1.4 %first.1 = (bf16[24,1280]{1,0:T(8,128)(2,1)S(1)}, bf16[24,24,1280]{2,1,0:T(8,128)(2,1)S(1)}, f32[3,3,1280]{2,1,0:T(4,128)S(1)}, f32[3,1,1280]{2,1,0:T(1,128)S(1)}) custom-call(bf16[24,24,1280]{2,1,0:T(8,128)(2,1)} %x_hbm.1, f32[3,3,1280]{2,1,0:T(4,128)} %taps_hbm.1, f32[1280]{0:T(1024)} %cbias_hbm.1, f32[1280]{0:T(1024)} %gain_hbm.1, f32[1280]{0:T(1024)} %nbias_hbm.1), custom_call_target="tpu_custom_call" | custom-call | flops 1024 | bytes 1024 | tf_op jit(solution)/shard_map/first/pallas_call | solution.py:337
  1.5 0.3 collective-permute-start
  1.8 1.4 %middle.1 = (bf16[176,1280]{1,0:T(8,128)(2,1)S(1)}, bf16[24,1280]{1,0:T(8,128)(2,1)S(1)}) custom-call(bf16[24,24,1280]{2,1,0:T(8,128)(2,1)S(1)} %get-tuple-element.23.x_ref, f32[3,3,1280]{2,1,0:T(4,128)S(1)} %get-tuple-element.24.taps_ref, f32[3,1,1280]{2,1,0:T(1,128)S(1)} %get-tuple-element.25.vec_ref), custom_call_target="tpu_custom_call" | custom-call | flops 1024 | bytes 1024 | tf_op jit(solution)/shard_map/middle/pallas_call | solution.py:352
  3.2 1.3 %collective-permute-start.4 = (bf16[176,1280]{1,0:T(8,128)(2,1)S(1)}, bf16[176,1280]{1,0:T(8,128)(2,1)S(1)}, u32[]{:S(2)}, u32[]{:S(2)}) collective-permute-start(bf16[176,1280]{1,0:T(8,128)(2,1)S(1)} %get-tuple-element.28.refs_2_), channel_id=1, source_target_pairs={{0,2},{1,3},{2,0},{3,1},{4,6},{5,7},{6,4},{7,5},{8,10},{9,11},{10,... | collective-permute-start | bytes 1351688 | tf_op jit(solution)/shard_map/ppermute | solution.py:319
  4.5 0.1 collective-permute-done.before_ref.behind_ref
  4.6 0.0 copy-start
  4.6 0.0 copy-start.1
  4.7 2.0 %collective-permute-start.1 = (bf16[48,1280]{1,0:T(8,128)(2,1)S(1)}, bf16[48,1280]{1,0:T(8,128)(2,1)S(1)}, u32[]{:S(2)}, u32[]{:S(2)}) collective-permute-start(bf16[48,1280]{1,0:T(8,128)(2,1)S(1)} %relay.1), channel_id=1, source_target_pairs={{0,1},{1,0},{2,3},{3,2},{4,5},{5,4},{6,7},{7,6},{8,9},{9,8},{10,11... | collective-permute-start | bytes 368648 | tf_op jit(solution)/shard_map/ppermute | solution.py:324
  6.6 0.1 collective-permute-start.9
  6.7 0.9 %collective-permute-done.1.sides_ref = bf16[48,1280]{1,0:T(8,128)(2,1)S(1)} collective-permute-done((bf16[48,1280]{1,0:T(8,128)(2,1)S(1)}, bf16[48,1280]{1,0:T(8,128)(2,1)S(1)}, u32[]{:S(2)}, u32[]{:S(2)}) %collective-permute-start.1) | collective-permute-done | bytes 122912 | tf_op jit(solution)/shard_map/ppermute | solution.py:324
  7.6 0.1 ends.1
  7.7 0.3 collective-permute-start.5
  8.0 4.1 %collective-permute-start.6 = (bf16[26,1280]{1,0:T(8,128)(2,1)S(1)}, bf16[26,1280]{1,0:T(8,128)(2,1)S(1)}, u32[]{:S(2)}, u32[]{:S(2)}) collective-permute-start(bf16[26,1280]{1,0:T(8,128)(2,1)S(1)} %get-tuple-element.30), channel_id=1, source_target_pairs={{4,8},{12,16},{20,24},{8,4},{16,12},{24,20},{5,9},{13,17},{21,25},... | collective-permute-start | bytes 199688 | tf_op jit(solution)/shard_map/ppermute | solution.py:328
  12.2 1.2 %side.3.refs_0_ = bf16[176,1280]{1,0:T(8,128)(2,1)S(1)} custom-call(bf16[24,24,1280]{2,1,0:T(8,128)(2,1)S(1)} %get-tuple-element.23.x_ref, bf16[48,1280]{1,0:T(8,128)(2,1)S(1)} %collective-permute-done.1.sides_ref, f32[3,3,1280]{2,1,0:T(4,128)S(1)} %get-tuple-element.24.taps_ref, f32[3,1,1280]{2,1,0:T(1,128)S(1)} %get-tuple-element.25.vec_ref), custom_call_target="tpu_custom_call" | custom-call | flops 1024 | bytes 1024 | tf_op jit(solution)/shard_map/side/pallas_call | solution.py:382
  13.4 1.0 %collective-permute-start.7 = (bf16[176,1280]{1,0:T(8,128)(2,1)S(1)}, bf16[176,1280]{1,0:T(8,128)(2,1)S(1)}, u32[]{:S(2)}, u32[]{:S(2)}) collective-permute-start(bf16[176,1280]{1,0:T(8,128)(2,1)S(1)} %side.3.refs_0_), channel_id=1, source_target_pairs={{0,1},{1,0},{2,3},{3,2},{4,5},{5,4},{6,7},{7,6},{8,9},{9,8},{10,11... | collective-permute-start | bytes 1351688 | tf_op jit(solution)/shard_map/ppermute | solution.py:324
  14.4 0.0 collective-permute-done.5.pair_ref
  14.4 0.2 collective-permute-start.3
  14.5 1.2 %side.2.refs_4_ = bf16[176,1280]{1,0:T(8,128)(2,1)S(1)} custom-call(bf16[24,24,1280]{2,1,0:T(8,128)(2,1)S(1)} %get-tuple-element.23.x_ref, bf16[48,1280]{1,0:T(8,128)(2,1)S(1)} %collective-permute-done.1.sides_ref, f32[3,3,1280]{2,1,0:T(4,128)S(1)} %get-tuple-element.24.taps_ref, f32[3,1,1280]{2,1,0:T(1,128)S(1)} %get-tuple-element.25.vec_ref), custom_call_target="tpu_custom_call" | custom-call | flops 1024 | bytes 1024 | tf_op jit(solution)/shard_map/side/pallas_call | solution.py:382
  15.8 0.0 collective-permute-done.6.cross_ref
  15.8 0.4 collective-permute-start.10
  16.3 0.0 collective-permute-done.4.refs_2_
  16.3 0.2 collective-permute-start.11
  16.5 0.7 %edges.1.refs_1_.refs_3_.refs_5_ = bf16[48,1280]{1,0:T(8,128)(2,1)S(1)} custom-call(bf16[24,24,1280]{2,1,0:T(8,128)(2,1)S(1)} %get-tuple-element.23.x_ref, bf16[48,1280]{1,0:T(8,128)(2,1)S(1)} %collective-permute-done.1.sides_ref, bf16[26,1280]{1,0:T(8,128)(2,1)S(1)} %collective-permute-done.5.pair_ref, ...), custom_call_target="tpu_custom_call" | custom-call | flops 1024 | bytes 1024 | tf_op jit(solution)/shard_map/edges/pallas_call | solution.py:403
  17.2 0.5 %collective-permute-done.11.refs_11_ = bf16[48,1280]{1,0:T(8,128)(2,1)S(1)} collective-permute-done((bf16[48,1280]{1,0:T(8,128)(2,1)S(1)}, bf16[48,1280]{1,0:T(8,128)(2,1)S(1)}, u32[]{:S(2)}, u32[]{:S(2)}) %collective-permute-start.11) | collective-permute-done | bytes 122912 | tf_op jit(solution)/shard_map/ppermute | solution.py:324
  17.7 0.4 collective-permute-start.8
  18.1 0.0 collective-permute-done.9.refs_8_
  18.1 1.3 %collective-permute-start.14 = (bf16[48,1280]{1,0:T(8,128)(2,1)S(1)}, bf16[48,1280]{1,0:T(8,128)(2,1)S(1)}, u32[]{:S(2)}, u32[]{:S(2)}) collective-permute-start(bf16[48,1280]{1,0:T(8,128)(2,1)S(1)} %edges.1.refs_1_.refs_3_.refs_5_), channel_id=1, source_target_pairs={{0,2},{1,3},{2,0},{3,1},{4,6},{5,7},{6,4},{7,5},{8,10},{9,11},{10,... | collective-permute-start | bytes 368648 | tf_op jit(solution)/shard_map/ppermute | solution.py:319
  19.4 0.0 collective-permute-done.10.refs_10_
  19.4 0.2 collective-permute-start.2
  19.5 0.0 collective-permute-done.8.refs_7_.refs_9_.refs_12_
  19.5 0.0 collective-permute-done.7.refs_6_
  19.5 0.0 copy-done
  19.6 0.0 copy-done.1
  19.6 4.9 %project.5.refs_6_ = bf16[3,4,24,7680]{3,2,1,0:T(8,128)(2,1)} custom-call(bf16[176,1280]{1,0:T(8,128)(2,1)S(1)} %side.3.refs_0_, bf16[48,1280]{1,0:T(8,128)(2,1)S(1)} %edges.1.refs_1_.refs_3_.refs_5_, bf16[176,1280]{1,0:T(8,128)(2,1)S(1)} %get-tuple-element.28.refs_2_, bf16[48,1280]{1,0:T(8,128)(2,1)S(1)} %edges.1.refs_1_.refs_3_.refs_5_, ...), custom_call_target="tpu_custom_call" | custom-call | flops 1024 | bytes 1024 | tf_op jit(solution)/shard_map/project/pallas_call | solution.py:289
  24.4 1.9 %collective-permute-done.3.refs_0_ = bf16[176,1280]{1,0:T(8,128)(2,1)S(1)} collective-permute-done((bf16[176,1280]{1,0:T(8,128)(2,1)S(1)}, bf16[176,1280]{1,0:T(8,128)(2,1)S(1)}, u32[]{:S(2)}, u32[]{:S(2)}) %collective-permute-start.3) | collective-permute-done | bytes 450592 | tf_op jit(solution)/shard_map/ppermute | solution.py:319
  26.3 2.6 %collective-permute-done.14.refs_1_.refs_3_ = bf16[48,1280]{1,0:T(8,128)(2,1)S(1)} collective-permute-done((bf16[48,1280]{1,0:T(8,128)(2,1)S(1)}, bf16[48,1280]{1,0:T(8,128)(2,1)S(1)}, u32[]{:S(2)}, u32[]{:S(2)}) %collective-permute-start.14) | collective-permute-done | bytes 122912 | tf_op jit(solution)/shard_map/ppermute | solution.py:319
  28.9 1.3 %collective-permute-start.15 = (bf16[48,1280]{1,0:T(8,128)(2,1)S(1)}, bf16[48,1280]{1,0:T(8,128)(2,1)S(1)}, u32[]{:S(2)}, u32[]{:S(2)}) collective-permute-start(bf16[48,1280]{1,0:T(8,128)(2,1)S(1)} %collective-permute-done.14.refs_1_.refs_3_), channel_id=1, source_target_pairs={{0,1},{1,0},{2,3},{3,2},{4,5},{5,4},{6,7},{7,6},{8,9},{9,8},{10,11... | collective-permute-start | bytes 368648 | tf_op jit(solution)/shard_map/ppermute | solution.py:324
  30.3 0.1 collective-permute-start.16
  30.4 0.5 %collective-permute-start.12 = (bf16[96,1280]{1,0:T(8,128)(2,1)S(1)}, bf16[96,1280]{1,0:T(8,128)(2,1)S(1)}, u32[]{:S(2)}, u32[]{:S(2)}) collective-permute-start(bf16[96,1280]{1,0:T(8,128)(2,1)S(1)} %slice.20), channel_id=1, source_target_pairs={{0,1},{1,0},{2,3},{3,2},{4,5},{5,4},{6,7},{7,6},{8,9},{9,8},{10,11... | collective-permute-start | bytes 737288 | tf_op jit(solution)/shard_map/ppermute | solution.py:324
  30.9 0.1 collective-permute-start.17
  31.1 0.2 collective-permute-done.15.refs_2_.refs_5_.refs_1_
  31.2 0.4 collective-permute-start.13
  31.6 2.3 %project.6.refs_8_ = bf16[3,4,24,7680]{3,2,1,0:T(8,128)(2,1)} custom-call(bf16[176,1280]{1,0:T(8,128)(2,1)S(1)} %collective-permute-done.3.refs_0_, bf16[48,1280]{1,0:T(8,128)(2,1)S(1)} %collective-permute-done.14.refs_1_.refs_3_, bf16[176,1280]{1,0:T(8,128)(2,1)S(1)} %collective-permute-done.4.refs_2_, ...), custom_call_target="tpu_custom_call", output_to_operand_aliasing={{}: (6, {})} | custom-call | flops 1024 | bytes 1024 | tf_op jit(solution)/shard_map/project/pallas_call | solution.py:289
  33.9 0.0 collective-permute-done.17.refs_4_
  33.9 0.0 collective-permute-done.13.refs_1_
  33.9 0.0 collective-permute-done.16.refs_3_
  33.9 0.0 collective-permute-done.12.refs_0_
  33.9 2.3 %project.7.refs_4_ = bf16[3,4,24,7680]{3,2,1,0:T(8,128)(2,1)} custom-call(bf16[96,1280]{1,0:T(8,128)(2,1)S(1)} %collective-permute-done.12.refs_0_, bf16[80,1280]{1,0:T(8,128)(2,1)S(1)} %collective-permute-done.13.refs_1_, bf16[48,1280]{1,0:T(8,128)(2,1)S(1)} %collective-permute-done.15.refs_2_.refs_5_.refs_1_, ...), custom_call_target="tpu_custom_call", output_to_operand_aliasing={{}: (8, {})} | custom-call | flops 1024 | bytes 1024 | tf_op jit(solution)/shard_map/project/pallas_call | solution.py:289
  36.2 2.4 %collective-permute-done.2.refs_0_ = bf16[176,1280]{1,0:T(8,128)(2,1)S(1)} collective-permute-done((bf16[176,1280]{1,0:T(8,128)(2,1)S(1)}, bf16[176,1280]{1,0:T(8,128)(2,1)S(1)}, u32[]{:S(2)}, u32[]{:S(2)}) %collective-permute-start.2) | collective-permute-done | bytes 450592 | tf_op jit(solution)/shard_map/ppermute | solution.py:319
  38.6 0.9 %collective-permute-start.18 = (bf16[176,1280]{1,0:T(8,128)(2,1)S(1)}, bf16[176,1280]{1,0:T(8,128)(2,1)S(1)}, u32[]{:S(2)}, u32[]{:S(2)}) collective-permute-start(bf16[176,1280]{1,0:T(8,128)(2,1)S(1)} %collective-permute-done.2.refs_0_), channel_id=1, source_target_pairs={{0,1},{1,0},{2,3},{3,2},{4,5},{5,4},{6,7},{7,6},{8,9},{9,8},{10,11... | collective-permute-start | bytes 1351688 | tf_op jit(solution)/shard_map/ppermute | solution.py:324
  39.4 1.8 %project.8.refs_4_ = bf16[3,4,24,7680]{3,2,1,0:T(8,128)(2,1)} custom-call(bf16[176,1280]{1,0:T(8,128)(2,1)S(1)} %collective-permute-done.2.refs_0_, bf16[48,1280]{1,0:T(8,128)(2,1)S(1)} %collective-permute-done.14.refs_1_.refs_3_, bf16[3,320,1280]{2,1,0:T(8,128)(2,1)S(1)} %bitcast.4, bf16[3,320]{1,0:T(4,128)(2,1)S(1)} %copy-done.1, ...), custom_call_target="tpu_custom_call", output_to_operand_aliasing={{}: (4, {})} | custom-call | flops 1024 | bytes 1024 | tf_op jit(solution)/shard_map/project/pallas_call | solution.py:289
  41.2 0.0 collective-permute-done.18.refs_0_
  41.2 1.8 %project.9 = bf16[3,4,24,7680]{3,2,1,0:T(8,128)(2,1)} custom-call(bf16[176,1280]{1,0:T(8,128)(2,1)S(1)} %collective-permute-done.18.refs_0_, bf16[48,1280]{1,0:T(8,128)(2,1)S(1)} %collective-permute-done.15.refs_2_.refs_5_.refs_1_, bf16[3,320,1280]{2,1,0:T(8,128)(2,1)S(1)} %bitcast.5, bf16[3,320]{1,0:T(4,128)(2,1)S(1)} %copy-done.1, ...), custom_call_target="tpu_custom_call", output_to_operand_aliasing={{}: (4, {})} | custom-call | flops 1024 | bytes 1024 | tf_op jit(solution)/shard_map/project/pallas_call | solution.py:289
  (7 shorter events, 0.1 us)
Async XLA Ops:
  1.5 3.1 %collective-permute-start = (bf16[24,1280]{1,0:T(8,128)(2,1)S(1)}, bf16[24,1280]{1,0:T(8,128)(2,1)S(1)}, u32[]{:S(2)}, u32[]{:S(2)}) collective-permute-start(bf16[24,1280]{1,0:T(8,128)(2,1)S(1)} %get-tuple-element.27), channel_id=1, source_target_pairs={{0,2},{1,3},{2,0},{3,1},{4,6},{5,7},{6,4},{7,5},{8,10},{9,11},{10,... | collective-permute-start | bytes 184328 | tf_op jit(solution)/shard_map/ppermute | solution.py:319
  3.2 13.1 %collective-permute-start.4 = (bf16[176,1280]{1,0:T(8,128)(2,1)S(1)}, bf16[176,1280]{1,0:T(8,128)(2,1)S(1)}, u32[]{:S(2)}, u32[]{:S(2)}) collective-permute-start(bf16[176,1280]{1,0:T(8,128)(2,1)S(1)} %get-tuple-element.28.refs_2_), channel_id=1, source_target_pairs={{0,2},{1,3},{2,0},{3,1},{4,6},{5,7},{6,4},{7,5},{8,10},{9,11},{10,... | collective-permute-start | bytes 1351688 | tf_op jit(solution)/shard_map/ppermute | solution.py:319
  4.6 14.9 %copy-start = (bf16[3,1280,320]{1,2,0:T(8,128)(2,1)S(1)}, bf16[3,1280,320]{1,2,0:T(8,128)(2,1)}, u32[]{:S(2)}) copy-start(bf16[3,1280,320]{1,2,0:T(8,128)(2,1)} %param.12) | copy-start | bytes 7372804
  4.6 14.9 %copy-start.1 = (bf16[3,320]{1,0:T(4,128)(2,1)S(1)}, bf16[3,320]{1,0:T(4,128)(2,1)}, u32[]{:S(2)}) copy-start(bf16[3,320]{1,0:T(4,128)(2,1)} %refs_3_.3) | copy-start | bytes 5764
  4.7 3.0 %collective-permute-start.1 = (bf16[48,1280]{1,0:T(8,128)(2,1)S(1)}, bf16[48,1280]{1,0:T(8,128)(2,1)S(1)}, u32[]{:S(2)}, u32[]{:S(2)}) collective-permute-start(bf16[48,1280]{1,0:T(8,128)(2,1)S(1)} %relay.1), channel_id=1, source_target_pairs={{0,1},{1,0},{2,3},{3,2},{4,5},{5,4},{6,7},{7,6},{8,9},{9,8},{10,11... | collective-permute-start | bytes 368648 | tf_op jit(solution)/shard_map/ppermute | solution.py:324
  6.6 11.4 %collective-permute-start.9 = (bf16[176,1280]{1,0:T(8,128)(2,1)S(1)}, bf16[176,1280]{1,0:T(8,128)(2,1)S(1)}, u32[]{:S(2)}, u32[]{:S(2)}) collective-permute-start(bf16[176,1280]{1,0:T(8,128)(2,1)S(1)} %get-tuple-element.28.refs_2_), channel_id=1, source_target_pairs={{0,1},{1,0},{2,3},{3,2},{4,5},{5,4},{6,7},{7,6},{8,9},{9,8},{10,11... | collective-permute-start | bytes 1351688 | tf_op jit(solution)/shard_map/ppermute | solution.py:324
  7.7 6.7 %collective-permute-start.5 = (bf16[26,1280]{1,0:T(8,128)(2,1)S(1)}, bf16[26,1280]{1,0:T(8,128)(2,1)S(1)}, u32[]{:S(2)}, u32[]{:S(2)}) collective-permute-start(bf16[26,1280]{1,0:T(8,128)(2,1)S(1)} %get-tuple-element.29), channel_id=1, source_target_pairs={{0,4},{8,12},{16,20},{24,28},{4,0},{12,8},{20,16},{28,24},{1,5},{9... | collective-permute-start | bytes 199688 | tf_op jit(solution)/shard_map/ppermute | solution.py:328
  8.0 7.8 %collective-permute-start.6 = (bf16[26,1280]{1,0:T(8,128)(2,1)S(1)}, bf16[26,1280]{1,0:T(8,128)(2,1)S(1)}, u32[]{:S(2)}, u32[]{:S(2)}) collective-permute-start(bf16[26,1280]{1,0:T(8,128)(2,1)S(1)} %get-tuple-element.30), channel_id=1, source_target_pairs={{4,8},{12,16},{20,24},{8,4},{16,12},{24,20},{5,9},{13,17},{21,25},... | collective-permute-start | bytes 199688 | tf_op jit(solution)/shard_map/ppermute | solution.py:328
  13.4 6.2 %collective-permute-start.7 = (bf16[176,1280]{1,0:T(8,128)(2,1)S(1)}, bf16[176,1280]{1,0:T(8,128)(2,1)S(1)}, u32[]{:S(2)}, u32[]{:S(2)}) collective-permute-start(bf16[176,1280]{1,0:T(8,128)(2,1)S(1)} %side.3.refs_0_), channel_id=1, source_target_pairs={{0,1},{1,0},{2,3},{3,2},{4,5},{5,4},{6,7},{7,6},{8,9},{9,8},{10,11... | collective-permute-start | bytes 1351688 | tf_op jit(solution)/shard_map/ppermute | solution.py:324
  14.4 11.9 %collective-permute-start.3 = (bf16[176,1280]{1,0:T(8,128)(2,1)S(1)}, bf16[176,1280]{1,0:T(8,128)(2,1)S(1)}, u32[]{:S(2)}, u32[]{:S(2)}) collective-permute-start(bf16[176,1280]{1,0:T(8,128)(2,1)S(1)} %side.3.refs_0_), channel_id=1, source_target_pairs={{0,2},{1,3},{2,0},{3,1},{4,6},{5,7},{6,4},{7,5},{8,10},{9,11},{10,... | collective-permute-start | bytes 1351688 | tf_op jit(solution)/shard_map/ppermute | solution.py:319
  15.8 3.5 %collective-permute-start.10 = (bf16[128,1280]{1,0:T(8,128)(2,1)S(1)}, bf16[128,1280]{1,0:T(8,128)(2,1)S(1)}, u32[]{:S(2)}, u32[]{:S(2)}) collective-permute-start(bf16[128,1280]{1,0:T(8,128)(2,1)S(1)} %slice.24), channel_id=1, source_target_pairs={{0,1},{1,0},{2,3},{3,2},{4,5},{5,4},{6,7},{7,6},{8,9},{9,8},{10,11... | collective-permute-start | bytes 983048 | tf_op jit(solution)/shard_map/ppermute | solution.py:324
  16.3 1.4 %collective-permute-start.11 = (bf16[48,1280]{1,0:T(8,128)(2,1)S(1)}, bf16[48,1280]{1,0:T(8,128)(2,1)S(1)}, u32[]{:S(2)}, u32[]{:S(2)}) collective-permute-start(bf16[48,1280]{1,0:T(8,128)(2,1)S(1)} %slice.25), channel_id=1, source_target_pairs={{0,1},{1,0},{2,3},{3,2},{4,5},{5,4},{6,7},{7,6},{8,9},{9,8},{10,11... | collective-permute-start | bytes 368648 | tf_op jit(solution)/shard_map/ppermute | solution.py:324
  17.7 1.8 %collective-permute-start.8 = (bf16[48,1280]{1,0:T(8,128)(2,1)S(1)}, bf16[48,1280]{1,0:T(8,128)(2,1)S(1)}, u32[]{:S(2)}, u32[]{:S(2)}) collective-permute-start(bf16[48,1280]{1,0:T(8,128)(2,1)S(1)} %edges.1.refs_1_.refs_3_.refs_5_), channel_id=1, source_target_pairs={{0,1},{1,0},{2,3},{3,2},{4,5},{5,4},{6,7},{7,6},{8,9},{9,8},{10,11... | collective-permute-start | bytes 368648 | tf_op jit(solution)/shard_map/ppermute | solution.py:324
  18.1 10.9 %collective-permute-start.14 = (bf16[48,1280]{1,0:T(8,128)(2,1)S(1)}, bf16[48,1280]{1,0:T(8,128)(2,1)S(1)}, u32[]{:S(2)}, u32[]{:S(2)}) collective-permute-start(bf16[48,1280]{1,0:T(8,128)(2,1)S(1)} %edges.1.refs_1_.refs_3_.refs_5_), channel_id=1, source_target_pairs={{0,2},{1,3},{2,0},{3,1},{4,6},{5,7},{6,4},{7,5},{8,10},{9,11},{10,... | collective-permute-start | bytes 368648 | tf_op jit(solution)/shard_map/ppermute | solution.py:319
  19.4 19.2 %collective-permute-start.2 = (bf16[176,1280]{1,0:T(8,128)(2,1)S(1)}, bf16[176,1280]{1,0:T(8,128)(2,1)S(1)}, u32[]{:S(2)}, u32[]{:S(2)}) collective-permute-start(bf16[176,1280]{1,0:T(8,128)(2,1)S(1)} %side.2.refs_4_), channel_id=1, source_target_pairs={{0,2},{1,3},{2,0},{3,1},{4,6},{5,7},{6,4},{7,5},{8,10},{9,11},{10,... | collective-permute-start | bytes 1351688 | tf_op jit(solution)/shard_map/ppermute | solution.py:319
  28.9 2.3 %collective-permute-start.15 = (bf16[48,1280]{1,0:T(8,128)(2,1)S(1)}, bf16[48,1280]{1,0:T(8,128)(2,1)S(1)}, u32[]{:S(2)}, u32[]{:S(2)}) collective-permute-start(bf16[48,1280]{1,0:T(8,128)(2,1)S(1)} %collective-permute-done.14.refs_1_.refs_3_), channel_id=1, source_target_pairs={{0,1},{1,0},{2,3},{3,2},{4,5},{5,4},{6,7},{7,6},{8,9},{9,8},{10,11... | collective-permute-start | bytes 368648 | tf_op jit(solution)/shard_map/ppermute | solution.py:324
  30.3 3.6 %collective-permute-start.16 = (bf16[96,1280]{1,0:T(8,128)(2,1)S(1)}, bf16[96,1280]{1,0:T(8,128)(2,1)S(1)}, u32[]{:S(2)}, u32[]{:S(2)}) collective-permute-start(bf16[96,1280]{1,0:T(8,128)(2,1)S(1)} %slice.22), channel_id=1, source_target_pairs={{0,1},{1,0},{2,3},{3,2},{4,5},{5,4},{6,7},{7,6},{8,9},{9,8},{10,11... | collective-permute-start | bytes 737288 | tf_op jit(solution)/shard_map/ppermute | solution.py:324
  30.4 3.5 %collective-permute-start.12 = (bf16[96,1280]{1,0:T(8,128)(2,1)S(1)}, bf16[96,1280]{1,0:T(8,128)(2,1)S(1)}, u32[]{:S(2)}, u32[]{:S(2)}) collective-permute-start(bf16[96,1280]{1,0:T(8,128)(2,1)S(1)} %slice.20), channel_id=1, source_target_pairs={{0,1},{1,0},{2,3},{3,2},{4,5},{5,4},{6,7},{7,6},{8,9},{9,8},{10,11... | collective-permute-start | bytes 737288 | tf_op jit(solution)/shard_map/ppermute | solution.py:324
  30.9 3.0 %collective-permute-start.17 = (bf16[80,1280]{1,0:T(8,128)(2,1)S(1)}, bf16[80,1280]{1,0:T(8,128)(2,1)S(1)}, u32[]{:S(2)}, u32[]{:S(2)}) collective-permute-start(bf16[80,1280]{1,0:T(8,128)(2,1)S(1)} %slice.23), channel_id=1, source_target_pairs={{0,1},{1,0},{2,3},{3,2},{4,5},{5,4},{6,7},{7,6},{8,9},{9,8},{10,11... | collective-permute-start | bytes 614408 | tf_op jit(solution)/shard_map/ppermute | solution.py:324
  31.2 2.7 %collective-permute-start.13 = (bf16[80,1280]{1,0:T(8,128)(2,1)S(1)}, bf16[80,1280]{1,0:T(8,128)(2,1)S(1)}, u32[]{:S(2)}, u32[]{:S(2)}) collective-permute-start(bf16[80,1280]{1,0:T(8,128)(2,1)S(1)} %slice.21), channel_id=1, source_target_pairs={{0,1},{1,0},{2,3},{3,2},{4,5},{5,4},{6,7},{7,6},{8,9},{9,8},{10,11... | collective-permute-start | bytes 614408 | tf_op jit(solution)/shard_map/ppermute | solution.py:324
  38.6 2.6 %collective-permute-start.18 = (bf16[176,1280]{1,0:T(8,128)(2,1)S(1)}, bf16[176,1280]{1,0:T(8,128)(2,1)S(1)}, u32[]{:S(2)}, u32[]{:S(2)}) collective-permute-start(bf16[176,1280]{1,0:T(8,128)(2,1)S(1)} %collective-permute-done.2.refs_0_), channel_id=1, source_target_pairs={{0,1},{1,0},{2,3},{3,2},{4,5},{5,4},{6,7},{7,6},{8,9},{9,8},{10,11... | collective-permute-start | bytes 1351688 | tf_op jit(solution)/shard_map/ppermute | solution.py:324

commit v6 on v5

--- a/solution.py
+++ b/solution.py
@@ -12,7 +12,9 @@
 LANES = 128
 EPS = 1e-06
 VMEM_LIMIT = 32 * 1024 * 1024
-K = {'pieceF': 128, 'extra': 32, 'early': 8, 'piece': 96, 'pieceA': 96, 'bsplit': 0, 'csplit': 0, 'A2': 'edges', 'B': None, 'C1': None, 'D': None, 'swA': 'X', 'swB': 'X', 'swD': 'X', 'z': 2, 'y': 2}
+PIECE = 96
+OWN_PIECE = 128
+LAST_PIECE = 176
 BF16 = jnp.bfloat16
 F32 = jnp.float32
 
@@ -224,11 +226,16 @@
     normalize(mixed, 2 * cols, vec_ref.at[1], vec_ref.at[2], out_ref)
 
 
-def project_kernel(rows, plan, count, fresh, step, side_count, *refs):
+def project_kernel(rows, plan, count, mode, step, side_count, *refs):
     parts, (w_ref, b_ref), refs = refs[:count], refs[count : count + 2], refs[count + 2 :]
-    if not fresh:
-        refs = refs[1:]
-    out_ref, sums, blocks, sems = refs
+    if mode == "blocks":
+        blocks, sums = refs
+    else:
+        if mode == "last":
+            before, refs = refs[0], refs[1:]
+        if mode != "first":
+            refs = refs[1:]
+        out_ref, sums, blocks, sems = refs
     heads = w_ref.shape[1] // HD
     width = w_ref.shape[2]
     total = 3 * heads * HD
@@ -237,6 +244,18 @@
     bias = jnp.concatenate([b_ref[pl.ds(t, 1), :].astype(F32) for t in range(3)], axis=1)
     owner = lax.rem(lax.axis_index("cols") + 2 * step, side_count)
     side = rows * GROUP
+    copies = []
+
+    def write(source, other, group, t, sem):
+        position = owner ^ 1 if other else owner
+        lane = pl.multiple_of(position * (out_ref.shape[3] // side_count) + group * block, LANES)
+        copies.append(pltpu.make_async_copy(source.at[t], out_ref.at[t, :, :, pl.ds(lane, block)], sem))
+        copies[-1].start()
+
+    if mode == "last":
+        for g, (_, other, group) in enumerate(plan):
+            for t in range(3):
+                write(before.at[g], 1 - other, group, t, sems.at[len(plan) + g, t])
     for batch in batches_of(len(plan)):
         pieces = [parts[ref][pl.ds(at, size), :] for g in batch for ref, at, size in plan[g][0]]
         acc = (
@@ -253,10 +272,7 @@
                 sums[g, k // LANES, pl.ds(GROUP, inner), span] = piece[:inner]
                 sums[g, k // LANES, pl.ds(0, GROUP), span] = piece[inner : inner + GROUP]
                 sums[g, k // LANES, pl.ds(inner + GROUP, GROUP), span] = piece[inner + GROUP :]
-    copies = []
     for g, (_, other, group) in enumerate(plan):
-        position = owner ^ 1 if other else owner
-        lane = pl.multiple_of(position * (out_ref.shape[3] // side_count) + group * block, LANES)
         for t in range(3):
             for h in range(heads):
                 start = (t * heads + h) * HD
@@ -267,11 +283,8 @@
                     cell = tiles[0] if len(tiles) == 1 else jnp.concatenate(tiles, axis=1)
                     cells.append(cell[:, start - lo * LANES : start - lo * LANES + HD])
                 blocks[g, t, h] = jnp.concatenate(cells, axis=1).astype(BF16)
-            copy = pltpu.make_async_copy(
-                blocks.at[g, t], out_ref.at[t, :, :, pl.ds(lane, block)], sems.at[g, t]
-            )
-            copy.start()
-            copies.append(copy)
+            if mode != "blocks":
+                write(blocks.at[g], other, group, t, sems.at[g, t])
     for copy in copies:
         copy.wait()
 
@@ -281,23 +294,24 @@
     return [range(at, min(at + size, count)) for at in range(0, count, size)]
 
 
-def project(out, parts, plan, step, weight, bias, rows, side_count, shape):
+def project(out, parts, plan, step, weight, bias, rows, side_count, shape, mode, before=None):
     count = len(parts)
     heads = weight.shape[1] // HD
-    fresh = out is None
-    operands = [*parts, weight, bias] + ([] if fresh else [out])
+    operands = [*parts, weight, bias] + [v for v in (before, out) if v is not None]
+    sums = pltpu.VMEM((len(plan), pl.cdiv(3 * heads * HD, LANES), (rows + 1) * GROUP, LANES), F32)
+    blocks = (len(plan), 3, heads, rows, GROUP * HD)
+    body = functools.partial(project_kernel, rows, plan, count, mode, step, side_count)
+    specs = [VMEM] * (count + 2 + (before is not None)) + [HBM] * (out is not None)
+    if mode == "blocks":
+        return call(body, "project", jax.ShapeDtypeStruct(blocks, BF16), specs, VMEM, [sums])(*operands)
     return call(
-        functools.partial(project_kernel, rows, plan, count, fresh, step, side_count),
+        body,
         "project",
         jax.ShapeDtypeStruct(shape, BF16),
-        [VMEM] * (count + 2) + ([] if fresh else [HBM]),
+        specs,
         HBM,
-        [
-            pltpu.VMEM((len(plan), pl.cdiv(3 * heads * HD, LANES), rows * GROUP, LANES), F32),
-            pltpu.VMEM((len(plan), 3, heads, rows, GROUP * HD), BF16),
-            pltpu.SemaphoreType.DMA((len(plan), 3)),
-        ],
-        aliases={} if fresh else {len(operands) - 1: 0},
+        [sums, pltpu.VMEM(blocks, BF16), pltpu.SemaphoreType.DMA(((2 if mode == "last" else 1) * len(plan), 3))],
+        aliases={} if out is None else {len(operands) - 1: 0},
     )(*operands)
 
 
@@ -305,7 +319,6 @@
     rows, cols, width = patches.shape
     up_count, side_count = lax.axis_size("rows"), lax.axis_size("cols")
     chips = side_count // 2
-    wide = cols - 2 * GROUP
     inner = rows - 2
     half = inner * GROUP
     two = 2 * GROUP
@@ -378,6 +391,7 @@
         [VMEM] * 2,
         [],
     )(x, sides)
+
     def side(last):
         return call(
             functools.partial(side_kernel, last),
@@ -388,18 +402,9 @@
             [pltpu.VMEM((rows, width), F32), pltpu.VMEM((half, width), F32)],
         )(x, sides, taps, vectors)
 
-    near, far = [side(0)], [side(1)]
-    got_near = [across(v) for v in near]
-    got_far = [across(v) for v in far]
-    marks = {"A2": got_middle, "B": sum(got_near, []), "C1": got_far[0]}
-
-    def hold(place, values):
-        others = sum([marks[k] for k in marks if K[k] == place], [])
-        return after(values, others) if others else list(values)
-
-    pair, cross = hold("up", (pair, cross))
-    pair, cross = exchange(pair, 0), exchange(cross, 1)
-    pair, cross = hold("edges", (pair, cross))
+    near, far = side(0), side(1)
+    got_near, got_far = across(near), across(far)
+    pair, cross = after((exchange(pair, 0), exchange(cross, 1)), got_middle)
     edge = call(
         edges_kernel,
         "edges",
@@ -409,7 +414,6 @@
         [pltpu.VMEM((2 * cols, width), F32)],
     )(x, sides, pair, cross, taps, vectors)
     got_edge = across(edge)
-    marks["D"] = got_edge
 
     shape = (3, qkv_weight.shape[2] // HD, rows, side_count * cols * HD)
     weight = jnp.swapaxes(qkv_weight, 1, 2)
@@ -425,7 +429,7 @@
             (whole(far) + [(edge, 2 * two, two)], other, 2),
         ]
 
-    def step_on(out, groups, step):
+    def step_on(out, groups, step, mode="next", before=None):
         arrays, entries = [], []
         for pieces, other, group in groups:
             entry = []
@@ -433,46 +437,29 @@
                 entry.append((len(arrays), at, size))
                 arrays.append(value)
             entries.append((tuple(entry), other, group))
-        return run(out, arrays, entries, step)
-
-    (late,) = hold("eswap", (edge,))
-    (held,) = hold("X", (middle,))
-    out = step_on(
-        None,
-        groups_of(near, [held], edge, far, 0)
-        + groups_of([swap(v) for v in near], [swap(middle)], swap(late), [swap(far[0][p : p + K['pieceF']]) for p in range(0, half, K['pieceF'])], 1),
-        0,
-    )
+        return run(out, arrays, entries, step, mode=mode, before=before)
+
+    def cut(value, size):
+        return [value[at : at + size] for at in range(0, value.shape[0], size)]
+
+    def swaps(value, size=half):
+        return [swap(part) for part in cut(value, size)]
+
+    own = groups_of([near], [middle], edge, [far], 0)
+    own = own + groups_of(swaps(near), swaps(middle), swap(edge), swaps(far, OWN_PIECE), 1)
+    out = step_on(None, own, 0, "first")
     for step in steps:
-        at = step - 1
-        pick = dict(
-            swA=[got_middle[at]], swB=[v[at] for v in got_near], swD=[got_edge[at]]
-        )
-        for key in pick:
-            if K[key] == "X":
-                *pick[key], out = lax.optimization_barrier((*pick[key], out))
-        c1 = [v[at] for v in got_far]
-        if K["C1"] == "dswap":
-            pick["swD"] = after(pick["swD"], c1[:1])
-        gota, gotb, (gote,) = pick["swA"], pick["swB"], pick["swD"]
-        other_near = [swap(v[p : p + K["piece"]]) for v in gotb for p in range(0, v.shape[0], K["piece"])]
-        other_middle = [swap(v[p : p + K["pieceA"]]) for v in gota for p in range(0, v.shape[0], K["pieceA"])]
-        othere = swap(gote)
-        mine = groups_of(gotb, gota, gote, [], 0)[:2]
-        theirs = groups_of(other_near, other_middle, othere, [], 1)[:2]
-        if K["y"] == 2:
-            out = step_on(out, mine, chips - step)
-            out = step_on(out, theirs, chips - step)
-        else:
-            out = step_on(out, mine + theirs, chips - step)
-        *c1, out = lax.optimization_barrier((*c1, out))
-        last = groups_of([], [], gote, c1, 0)[2:]
-        other = groups_of([], [], othere, [swap(v) for v in c1], 1)[2:]
-        if K["z"] == 2:
-            out = step_on(out, last, chips - step)
-            out = step_on(out, other, chips - step)
-        else:
-            out = step_on(out, last + other, chips - step)
+        got = [v[step - 1] for v in (got_near, got_middle, got_edge)]
+        *got, out = lax.optimization_barrier((*got, out))
+        one, second, border = got
+        other_border = swap(border)
+        out = step_on(out, groups_of([one], [second], border, [], 0)[:2], chips - step)
+        theirs = groups_of(swaps(one, PIECE), swaps(second, PIECE), other_border, [], 1)[:2]
+        out = step_on(out, theirs, chips - step)
+        last, out = lax.optimization_barrier((got_far[step - 1], out))
+        blocks = step_on(None, groups_of([], [], border, [last], 0)[2:], chips - step, "blocks")
+        theirs = groups_of([], [], other_border, swaps(last, LAST_PIECE), 1)[2:]
+        out = step_on(out, theirs, chips - step, "last", blocks)
     return out
 
 

time: 43.4 us -> 43.4 us (level)
  Pallas kernels: 19 us -> 18.4 us
    pallas_call x5, Pallas kernels: 12.9 us -> 12.3 us  [the longest x4 11.2 us: project(): call(body, 'project', jax.ShapeDtypeStruct(shape, BF16), specs, HBM, [sum...]
  transfers between devices with their start and end apart: 19 -> 19, of which waited for: 7 -> 7; matrix products, arithmetic and copies ran while one was open for 0% -> 0% of each run, Pallas kernels for 37% -> 36%
where the time goes in v6:
time: 43.4 us; the launch traced here: 42.6 us
  Pallas kernels  18.4 us (42%)
  starting transfers between devices  15 us (35%)
  waiting for transfers between devices  8.99 us (21%)
    pallas_call x4, Pallas kernels, project(): call(body, 'project', jax.ShapeDtypeStruct(shape, BF16), specs, HBM, [sum...  11.2 us
    ppermute x12, starting transfers between devices, swap(): return lax.ppermute(value, 'cols', [(q, q ^ 1) for q in range(side_count)])  7.31 us
    ppermute x5, waiting for transfers between devices, across(): lax.ppermute(value, 'cols', [(q, (q + 2 * step) % side_count) for q in ra...  7 us
    ppermute x2, starting transfers between devices, exchange(): return lax.ppermute(value, 'rows', pairs + [(j, i) for i, j in pairs])  4.44 us
    ppermute x5, starting transfers between devices, across(): lax.ppermute(value, 'cols', [(q, (q + 2 * step) % side_count) for q in ra...  3.23 us
    pallas_call x2, Pallas kernels, side(): call(functools.partial(side_kernel, last), 'side', array(half, width), [V...  2.48 us
    ppermute x12, waiting for transfers between devices, swap(): return lax.ppermute(value, 'cols', [(q, q ^ 1) for q in range(side_count)])  1.98 us
    pallas_call x1, Pallas kernels, local(): call(first_kernel, 'first', [array(rows, width), array(rows, cols, width)...  1.45 us
  transfers between devices with their start and end apart: 19, of which 7 were waited for; matrix products, arithmetic and copies ran while one was open for 0% of the time, Pallas kernels for 36%

profile of v6, /device:TPU:15, one launch (start us, length us, event | category | flops | bytes accessed | tf_op | source)
XLA Modules:
  0.0 42.6 jit_solution(13202055428636895504)
XLA Ops:
  0.0 1.4 %first.1 = (bf16[24,1280]{1,0:T(8,128)(2,1)S(1)}, bf16[24,24,1280]{2,1,0:T(8,128)(2,1)S(1)}, f32[3,3,1280]{2,1,0:T(4,128)S(1)}, f32[3,1,1280]{2,1,0:T(1,128)S(1)}) custom-call(bf16[24,24,1280]{2,1,0:T(8,128)(2,1)} %x_hbm.1, f32[3,3,1280]{2,1,0:T(4,128)} %taps_hbm.1, f32[1280]{0:T(1024)} %cbias_hbm.1, f32[1280]{0:T(1024)} %gain_hbm.1, f32[1280]{0:T(1024)} %nbias_hbm.1), custom_call_target="tpu_custom_call" | custom-call | flops 1024 | bytes 1024 | tf_op jit(solution)/shard_map/first/pallas_call | solution.py:350
  1.5 0.3 collective-permute-start
  1.8 1.4 %middle.1 = (bf16[176,1280]{1,0:T(8,128)(2,1)S(1)}, bf16[24,1280]{1,0:T(8,128)(2,1)S(1)}) custom-call(bf16[24,24,1280]{2,1,0:T(8,128)(2,1)S(1)} %get-tuple-element.21.x_ref, f32[3,3,1280]{2,1,0:T(4,128)S(1)} %get-tuple-element.22.taps_ref, f32[3,1,1280]{2,1,0:T(1,128)S(1)} %get-tuple-element.23.vec_ref), custom_call_target="tpu_custom_call" | custom-call | flops 1024 | bytes 1024 | tf_op jit(solution)/shard_map/middle/pallas_call | solution.py:365
  3.2 1.3 %collective-permute-start.4 = (bf16[176,1280]{1,0:T(8,128)(2,1)S(1)}, bf16[176,1280]{1,0:T(8,128)(2,1)S(1)}, u32[]{:S(2)}, u32[]{:S(2)}) collective-permute-start(bf16[176,1280]{1,0:T(8,128)(2,1)S(1)} %get-tuple-element.26.refs_2_), channel_id=1, source_target_pairs={{0,2},{1,3},{2,0},{3,1},{4,6},{5,7},{6,4},{7,5},{8,10},{9,11},{10,... | collective-permute-start | bytes 1351688 | tf_op jit(solution)/shard_map/ppermute | solution.py:332
  4.5 0.1 collective-permute-done.before_ref.behind_ref
  4.6 0.0 copy-start
  4.6 0.0 copy-start.1
  4.7 2.0 %collective-permute-start.1 = (bf16[48,1280]{1,0:T(8,128)(2,1)S(1)}, bf16[48,1280]{1,0:T(8,128)(2,1)S(1)}, u32[]{:S(2)}, u32[]{:S(2)}) collective-permute-start(bf16[48,1280]{1,0:T(8,128)(2,1)S(1)} %relay.1), channel_id=1, source_target_pairs={{0,1},{1,0},{2,3},{3,2},{4,5},{5,4},{6,7},{7,6},{8,9},{9,8},{10,11... | collective-permute-start | bytes 368648 | tf_op jit(solution)/shard_map/ppermute | solution.py:337
  6.6 0.1 collective-permute-start.10
  6.7 0.9 %collective-permute-done.1.sides_ref = bf16[48,1280]{1,0:T(8,128)(2,1)S(1)} collective-permute-done((bf16[48,1280]{1,0:T(8,128)(2,1)S(1)}, bf16[48,1280]{1,0:T(8,128)(2,1)S(1)}, u32[]{:S(2)}, u32[]{:S(2)}) %collective-permute-start.1) | collective-permute-done | bytes 122912 | tf_op jit(solution)/shard_map/ppermute | solution.py:337
  7.6 0.1 ends.1
  7.7 0.3 collective-permute-start.5
  8.0 4.1 %collective-permute-start.6 = (bf16[26,1280]{1,0:T(8,128)(2,1)S(1)}, bf16[26,1280]{1,0:T(8,128)(2,1)S(1)}, u32[]{:S(2)}, u32[]{:S(2)}) collective-permute-start(bf16[26,1280]{1,0:T(8,128)(2,1)S(1)} %get-tuple-element.28), channel_id=1, source_target_pairs={{4,8},{12,16},{20,24},{8,4},{16,12},{24,20},{5,9},{13,17},{21,25},... | collective-permute-start | bytes 199688 | tf_op jit(solution)/shard_map/ppermute | solution.py:341
  12.2 1.2 %side.3.refs_0_ = bf16[176,1280]{1,0:T(8,128)(2,1)S(1)} custom-call(bf16[24,24,1280]{2,1,0:T(8,128)(2,1)S(1)} %get-tuple-element.21.x_ref, bf16[48,1280]{1,0:T(8,128)(2,1)S(1)} %collective-permute-done.1.sides_ref, f32[3,3,1280]{2,1,0:T(4,128)S(1)} %get-tuple-element.22.taps_ref, f32[3,1,1280]{2,1,0:T(1,128)S(1)} %get-tuple-element.23.vec_ref), custom_call_target="tpu_custom_call" | custom-call | flops 1024 | bytes 1024 | tf_op jit(solution)/shard_map/side/pallas_call | solution.py:396
  13.4 1.0 %collective-permute-start.8 = (bf16[176,1280]{1,0:T(8,128)(2,1)S(1)}, bf16[176,1280]{1,0:T(8,128)(2,1)S(1)}, u32[]{:S(2)}, u32[]{:S(2)}) collective-permute-start(bf16[176,1280]{1,0:T(8,128)(2,1)S(1)} %side.3.refs_0_), channel_id=1, source_target_pairs={{0,1},{1,0},{2,3},{3,2},{4,5},{5,4},{6,7},{7,6},{8,9},{9,8},{10,11... | collective-permute-start | bytes 1351688 | tf_op jit(solution)/shard_map/ppermute | solution.py:337
  14.4 0.0 collective-permute-done.5.pair_ref
  14.4 0.2 collective-permute-start.3
  14.5 1.2 %side.2.refs_4_ = bf16[176,1280]{1,0:T(8,128)(2,1)S(1)} custom-call(bf16[24,24,1280]{2,1,0:T(8,128)(2,1)S(1)} %get-tuple-element.21.x_ref, bf16[48,1280]{1,0:T(8,128)(2,1)S(1)} %collective-permute-done.1.sides_ref, f32[3,3,1280]{2,1,0:T(4,128)S(1)} %get-tuple-element.22.taps_ref, f32[3,1,1280]{2,1,0:T(1,128)S(1)} %get-tuple-element.23.vec_ref), custom_call_target="tpu_custom_call" | custom-call | flops 1024 | bytes 1024 | tf_op jit(solution)/shard_map/side/pallas_call | solution.py:396
  15.8 0.0 collective-permute-done.6.cross_ref
  15.8 0.4 collective-permute-start.11
  16.3 0.0 collective-permute-done.4.refs_2_
  16.3 0.2 collective-permute-start.12
  16.5 0.7 %edges.1.refs_1_.refs_3_.refs_5_ = bf16[48,1280]{1,0:T(8,128)(2,1)S(1)} custom-call(bf16[24,24,1280]{2,1,0:T(8,128)(2,1)S(1)} %get-tuple-element.21.x_ref, bf16[48,1280]{1,0:T(8,128)(2,1)S(1)} %collective-permute-done.1.sides_ref, bf16[26,1280]{1,0:T(8,128)(2,1)S(1)} %collective-permute-done.5.pair_ref, ...), custom_call_target="tpu_custom_call" | custom-call | flops 1024 | bytes 1024 | tf_op jit(solution)/shard_map/edges/pallas_call | solution.py:408
  17.2 0.5 %collective-permute-done.12.refs_11_ = bf16[48,1280]{1,0:T(8,128)(2,1)S(1)} collective-permute-done((bf16[48,1280]{1,0:T(8,128)(2,1)S(1)}, bf16[48,1280]{1,0:T(8,128)(2,1)S(1)}, u32[]{:S(2)}, u32[]{:S(2)}) %collective-permute-start.12) | collective-permute-done | bytes 122912 | tf_op jit(solution)/shard_map/ppermute | solution.py:337
  17.7 0.4 collective-permute-start.9
  18.1 0.0 collective-permute-done.10.refs_8_
  18.1 1.3 %collective-permute-start.7 = (bf16[48,1280]{1,0:T(8,128)(2,1)S(1)}, bf16[48,1280]{1,0:T(8,128)(2,1)S(1)}, u32[]{:S(2)}, u32[]{:S(2)}) collective-permute-start(bf16[48,1280]{1,0:T(8,128)(2,1)S(1)} %edges.1.refs_1_.refs_3_.refs_5_), channel_id=1, source_target_pairs={{0,2},{1,3},{2,0},{3,1},{4,6},{5,7},{6,4},{7,5},{8,10},{9,11},{10,... | collective-permute-start | bytes 368648 | tf_op jit(solution)/shard_map/ppermute | solution.py:332
  19.4 0.0 collective-permute-done.11.refs_10_
  19.4 0.2 collective-permute-start.2
  19.5 0.0 collective-permute-done.9.refs_7_.refs_9_.refs_12_
  19.5 0.0 collective-permute-done.8.refs_6_
  19.5 0.0 copy-done
  19.6 0.0 copy-done.1
  19.6 4.9 %project.5.refs_6_ = bf16[3,4,24,7680]{3,2,1,0:T(8,128)(2,1)} custom-call(bf16[176,1280]{1,0:T(8,128)(2,1)S(1)} %side.3.refs_0_, bf16[48,1280]{1,0:T(8,128)(2,1)S(1)} %edges.1.refs_1_.refs_3_.refs_5_, bf16[176,1280]{1,0:T(8,128)(2,1)S(1)} %get-tuple-element.26.refs_2_, bf16[48,1280]{1,0:T(8,128)(2,1)S(1)} %edges.1.refs_1_.refs_3_.refs_5_, ...), custom_call_target="tpu_custom_call" | custom-call | flops 1024 | bytes 1024 | tf_op jit(solution)/shard_map/project/pallas_call | solution.py:307
  24.4 4.5 %collective-permute-done.7.refs_1_.refs_3_ = bf16[48,1280]{1,0:T(8,128)(2,1)S(1)} collective-permute-done((bf16[48,1280]{1,0:T(8,128)(2,1)S(1)}, bf16[48,1280]{1,0:T(8,128)(2,1)S(1)}, u32[]{:S(2)}, u32[]{:S(2)}) %collective-permute-start.7) | collective-permute-done | bytes 122912 | tf_op jit(solution)/shard_map/ppermute | solution.py:332
  28.9 0.0 collective-permute-done.3.refs_0_
  28.9 1.3 %collective-permute-start.15 = (bf16[48,1280]{1,0:T(8,128)(2,1)S(1)}, bf16[48,1280]{1,0:T(8,128)(2,1)S(1)}, u32[]{:S(2)}, u32[]{:S(2)}) collective-permute-start(bf16[48,1280]{1,0:T(8,128)(2,1)S(1)} %collective-permute-done.7.refs_1_.refs_3_), channel_id=1, source_target_pairs={{0,1},{1,0},{2,3},{3,2},{4,5},{5,4},{6,7},{7,6},{8,9},{9,8},{10,11... | collective-permute-start | bytes 368648 | tf_op jit(solution)/shard_map/ppermute | solution.py:337
  30.3 0.1 collective-permute-start.16
  30.4 0.5 %collective-permute-start.13 = (bf16[96,1280]{1,0:T(8,128)(2,1)S(1)}, bf16[96,1280]{1,0:T(8,128)(2,1)S(1)}, u32[]{:S(2)}, u32[]{:S(2)}) collective-permute-start(bf16[96,1280]{1,0:T(8,128)(2,1)S(1)} %slice.20), channel_id=1, source_target_pairs={{0,1},{1,0},{2,3},{3,2},{4,5},{5,4},{6,7},{7,6},{8,9},{9,8},{10,11... | collective-permute-start | bytes 737288 | tf_op jit(solution)/shard_map/ppermute | solution.py:337
  30.9 0.1 collective-permute-start.17
  31.1 0.2 collective-permute-done.15.refs_2_.refs_5_.refs_1_
  31.2 0.4 collective-permute-start.14
  31.6 2.3 %project.6.refs_8_ = bf16[3,4,24,7680]{3,2,1,0:T(8,128)(2,1)} custom-call(bf16[176,1280]{1,0:T(8,128)(2,1)S(1)} %collective-permute-done.3.refs_0_, bf16[48,1280]{1,0:T(8,128)(2,1)S(1)} %collective-permute-done.7.refs_1_.refs_3_, bf16[176,1280]{1,0:T(8,128)(2,1)S(1)} %collective-permute-done.4.refs_2_, ...), custom_call_target="tpu_custom_call", output_to_operand_aliasing={{}: (6, {})} | custom-call | flops 1024 | bytes 1024 | tf_op jit(solution)/shard_map/project/pallas_call | solution.py:307
  33.9 0.0 collective-permute-done.17.refs_4_
  33.9 0.0 collective-permute-done.14.refs_1_
  33.9 0.0 collective-permute-done.16.refs_3_
  33.9 0.0 collective-permute-done.13.refs_0_
  33.9 2.3 %project.7.refs_5_ = bf16[3,4,24,7680]{3,2,1,0:T(8,128)(2,1)} custom-call(bf16[96,1280]{1,0:T(8,128)(2,1)S(1)} %collective-permute-done.13.refs_0_, bf16[80,1280]{1,0:T(8,128)(2,1)S(1)} %collective-permute-done.14.refs_1_, bf16[48,1280]{1,0:T(8,128)(2,1)S(1)} %collective-permute-done.15.refs_2_.refs_5_.refs_1_, ...), custom_call_target="tpu_custom_call", output_to_operand_aliasing={{}: (8, {})} | custom-call | flops 1024 | bytes 1024 | tf_op jit(solution)/shard_map/project/pallas_call | solution.py:307
  36.2 2.4 %collective-permute-done.2.refs_0_ = bf16[176,1280]{1,0:T(8,128)(2,1)S(1)} collective-permute-done((bf16[176,1280]{1,0:T(8,128)(2,1)S(1)}, bf16[176,1280]{1,0:T(8,128)(2,1)S(1)}, u32[]{:S(2)}, u32[]{:S(2)}) %collective-permute-start.2) | collective-permute-done | bytes 450592 | tf_op jit(solution)/shard_map/ppermute | solution.py:332
  38.6 0.9 %collective-permute-start.18 = (bf16[176,1280]{1,0:T(8,128)(2,1)S(1)}, bf16[176,1280]{1,0:T(8,128)(2,1)S(1)}, u32[]{:S(2)}, u32[]{:S(2)}) collective-permute-start(bf16[176,1280]{1,0:T(8,128)(2,1)S(1)} %collective-permute-done.2.refs_0_), channel_id=1, source_target_pairs={{0,1},{1,0},{2,3},{3,2},{4,5},{5,4},{6,7},{7,6},{8,9},{9,8},{10,11... | collective-permute-start | bytes 1351688 | tf_op jit(solution)/shard_map/ppermute | solution.py:337
  39.4 1.1 %project.8.refs_4_ = bf16[1,3,4,24,640]{4,3,2,1,0:T(8,128)(2,1)S(1)} custom-call(bf16[176,1280]{1,0:T(8,128)(2,1)S(1)} %collective-permute-done.2.refs_0_, bf16[48,1280]{1,0:T(8,128)(2,1)S(1)} %collective-permute-done.7.refs_1_.refs_3_, bf16[3,320,1280]{2,1,0:T(8,128)(2,1)S(1)} %bitcast.4, bf16[3,320]{1,0:T(4,128)(2,1)S(1)} %copy-done.1), custom_call_target="tpu_custom_call" | custom-call | flops 1024 | bytes 1024 | tf_op jit(solution)/shard_map/project/pallas_call | solution.py:306
  40.5 0.4 collective-permute-done.18.refs_0_
  40.9 1.8 %project.9 = bf16[3,4,24,7680]{3,2,1,0:T(8,128)(2,1)} custom-call(bf16[176,1280]{1,0:T(8,128)(2,1)S(1)} %collective-permute-done.18.refs_0_, bf16[48,1280]{1,0:T(8,128)(2,1)S(1)} %collective-permute-done.15.refs_2_.refs_5_.refs_1_, bf16[3,320,1280]{2,1,0:T(8,128)(2,1)S(1)} %bitcast.5, bf16[3,320]{1,0:T(4,128)(2,1)S(1)} %copy-done.1, ...), custom_call_target="tpu_custom_call", output_to_operand_aliasing={{}: (5, {})} | custom-call | flops 1024 | bytes 1024 | tf_op jit(solution)/shard_map/project/pallas_call | solution.py:307
  (7 shorter events, 0.1 us)
Async XLA Ops:
  1.5 3.1 %collective-permute-start = (bf16[24,1280]{1,0:T(8,128)(2,1)S(1)}, bf16[24,1280]{1,0:T(8,128)(2,1)S(1)}, u32[]{:S(2)}, u32[]{:S(2)}) collective-permute-start(bf16[24,1280]{1,0:T(8,128)(2,1)S(1)} %get-tuple-element.25), channel_id=1, source_target_pairs={{0,2},{1,3},{2,0},{3,1},{4,6},{5,7},{6,4},{7,5},{8,10},{9,11},{10,... | collective-permute-start | bytes 184328 | tf_op jit(solution)/shard_map/ppermute | solution.py:332
  3.2 13.1 %collective-permute-start.4 = (bf16[176,1280]{1,0:T(8,128)(2,1)S(1)}, bf16[176,1280]{1,0:T(8,128)(2,1)S(1)}, u32[]{:S(2)}, u32[]{:S(2)}) collective-permute-start(bf16[176,1280]{1,0:T(8,128)(2,1)S(1)} %get-tuple-element.26.refs_2_), channel_id=1, source_target_pairs={{0,2},{1,3},{2,0},{3,1},{4,6},{5,7},{6,4},{7,5},{8,10},{9,11},{10,... | collective-permute-start | bytes 1351688 | tf_op jit(solution)/shard_map/ppermute | solution.py:332
  4.6 14.9 %copy-start = (bf16[3,1280,320]{1,2,0:T(8,128)(2,1)S(1)}, bf16[3,1280,320]{1,2,0:T(8,128)(2,1)}, u32[]{:S(2)}) copy-start(bf16[3,1280,320]{1,2,0:T(8,128)(2,1)} %param.12) | copy-start | bytes 7372804
  4.6 14.9 %copy-start.1 = (bf16[3,320]{1,0:T(4,128)(2,1)S(1)}, bf16[3,320]{1,0:T(4,128)(2,1)}, u32[]{:S(2)}) copy-start(bf16[3,320]{1,0:T(4,128)(2,1)} %refs_3_.3) | copy-start | bytes 5764
  4.7 3.0 %collective-permute-start.1 = (bf16[48,1280]{1,0:T(8,128)(2,1)S(1)}, bf16[48,1280]{1,0:T(8,128)(2,1)S(1)}, u32[]{:S(2)}, u32[]{:S(2)}) collective-permute-start(bf16[48,1280]{1,0:T(8,128)(2,1)S(1)} %relay.1), channel_id=1, source_target_pairs={{0,1},{1,0},{2,3},{3,2},{4,5},{5,4},{6,7},{7,6},{8,9},{9,8},{10,11... | collective-permute-start | bytes 368648 | tf_op jit(solution)/shard_map/ppermute | solution.py:337
  6.6 11.4 %collective-permute-start.10 = (bf16[176,1280]{1,0:T(8,128)(2,1)S(1)}, bf16[176,1280]{1,0:T(8,128)(2,1)S(1)}, u32[]{:S(2)}, u32[]{:S(2)}) collective-permute-start(bf16[176,1280]{1,0:T(8,128)(2,1)S(1)} %get-tuple-element.26.refs_2_), channel_id=1, source_target_pairs={{0,1},{1,0},{2,3},{3,2},{4,5},{5,4},{6,7},{7,6},{8,9},{9,8},{10,11... | collective-permute-start | bytes 1351688 | tf_op jit(solution)/shard_map/ppermute | solution.py:337
  7.7 6.7 %collective-permute-start.5 = (bf16[26,1280]{1,0:T(8,128)(2,1)S(1)}, bf16[26,1280]{1,0:T(8,128)(2,1)S(1)}, u32[]{:S(2)}, u32[]{:S(2)}) collective-permute-start(bf16[26,1280]{1,0:T(8,128)(2,1)S(1)} %get-tuple-element.27), channel_id=1, source_target_pairs={{0,4},{8,12},{16,20},{24,28},{4,0},{12,8},{20,16},{28,24},{1,5},{9... | collective-permute-start | bytes 199688 | tf_op jit(solution)/shard_map/ppermute | solution.py:341
  8.0 7.8 %collective-permute-start.6 = (bf16[26,1280]{1,0:T(8,128)(2,1)S(1)}, bf16[26,1280]{1,0:T(8,128)(2,1)S(1)}, u32[]{:S(2)}, u32[]{:S(2)}) collective-permute-start(bf16[26,1280]{1,0:T(8,128)(2,1)S(1)} %get-tuple-element.28), channel_id=1, source_target_pairs={{4,8},{12,16},{20,24},{8,4},{16,12},{24,20},{5,9},{13,17},{21,25},... | collective-permute-start | bytes 199688 | tf_op jit(solution)/shard_map/ppermute | solution.py:341
  13.4 6.2 %collective-permute-start.8 = (bf16[176,1280]{1,0:T(8,128)(2,1)S(1)}, bf16[176,1280]{1,0:T(8,128)(2,1)S(1)}, u32[]{:S(2)}, u32[]{:S(2)}) collective-permute-start(bf16[176,1280]{1,0:T(8,128)(2,1)S(1)} %side.3.refs_0_), channel_id=1, source_target_pairs={{0,1},{1,0},{2,3},{3,2},{4,5},{5,4},{6,7},{7,6},{8,9},{9,8},{10,11... | collective-permute-start | bytes 1351688 | tf_op jit(solution)/shard_map/ppermute | solution.py:337
  14.4 14.5 %collective-permute-start.3 = (bf16[176,1280]{1,0:T(8,128)(2,1)S(1)}, bf16[176,1280]{1,0:T(8,128)(2,1)S(1)}, u32[]{:S(2)}, u32[]{:S(2)}) collective-permute-start(bf16[176,1280]{1,0:T(8,128)(2,1)S(1)} %side.3.refs_0_), channel_id=1, source_target_pairs={{0,2},{1,3},{2,0},{3,1},{4,6},{5,7},{6,4},{7,5},{8,10},{9,11},{10,... | collective-permute-start | bytes 1351688 | tf_op jit(solution)/shard_map/ppermute | solution.py:332
  15.8 3.5 %collective-permute-start.11 = (bf16[128,1280]{1,0:T(8,128)(2,1)S(1)}, bf16[128,1280]{1,0:T(8,128)(2,1)S(1)}, u32[]{:S(2)}, u32[]{:S(2)}) collective-permute-start(bf16[128,1280]{1,0:T(8,128)(2,1)S(1)} %slice.24), channel_id=1, source_target_pairs={{0,1},{1,0},{2,3},{3,2},{4,5},{5,4},{6,7},{7,6},{8,9},{9,8},{10,11... | collective-permute-start | bytes 983048 | tf_op jit(solution)/shard_map/ppermute | solution.py:337
  16.3 1.4 %collective-permute-start.12 = (bf16[48,1280]{1,0:T(8,128)(2,1)S(1)}, bf16[48,1280]{1,0:T(8,128)(2,1)S(1)}, u32[]{:S(2)}, u32[]{:S(2)}) collective-permute-start(bf16[48,1280]{1,0:T(8,128)(2,1)S(1)} %slice.25), channel_id=1, source_target_pairs={{0,1},{1,0},{2,3},{3,2},{4,5},{5,4},{6,7},{7,6},{8,9},{9,8},{10,11... | collective-permute-start | bytes 368648 | tf_op jit(solution)/shard_map/ppermute | solution.py:337
  17.7 1.8 %collective-permute-start.9 = (bf16[48,1280]{1,0:T(8,128)(2,1)S(1)}, bf16[48,1280]{1,0:T(8,128)(2,1)S(1)}, u32[]{:S(2)}, u32[]{:S(2)}) collective-permute-start(bf16[48,1280]{1,0:T(8,128)(2,1)S(1)} %edges.1.refs_1_.refs_3_.refs_5_), channel_id=1, source_target_pairs={{0,1},{1,0},{2,3},{3,2},{4,5},{5,4},{6,7},{7,6},{8,9},{9,8},{10,11... | collective-permute-start | bytes 368648 | tf_op jit(solution)/shard_map/ppermute | solution.py:337
  18.1 10.9 %collective-permute-start.7 = (bf16[48,1280]{1,0:T(8,128)(2,1)S(1)}, bf16[48,1280]{1,0:T(8,128)(2,1)S(1)}, u32[]{:S(2)}, u32[]{:S(2)}) collective-permute-start(bf16[48,1280]{1,0:T(8,128)(2,1)S(1)} %edges.1.refs_1_.refs_3_.refs_5_), channel_id=1, source_target_pairs={{0,2},{1,3},{2,0},{3,1},{4,6},{5,7},{6,4},{7,5},{8,10},{9,11},{10,... | collective-permute-start | bytes 368648 | tf_op jit(solution)/shard_map/ppermute | solution.py:332
  19.4 19.2 %collective-permute-start.2 = (bf16[176,1280]{1,0:T(8,128)(2,1)S(1)}, bf16[176,1280]{1,0:T(8,128)(2,1)S(1)}, u32[]{:S(2)}, u32[]{:S(2)}) collective-permute-start(bf16[176,1280]{1,0:T(8,128)(2,1)S(1)} %side.2.refs_4_), channel_id=1, source_target_pairs={{0,2},{1,3},{2,0},{3,1},{4,6},{5,7},{6,4},{7,5},{8,10},{9,11},{10,... | collective-permute-start | bytes 1351688 | tf_op jit(solution)/shard_map/ppermute | solution.py:332
  28.9 2.3 %collective-permute-start.15 = (bf16[48,1280]{1,0:T(8,128)(2,1)S(1)}, bf16[48,1280]{1,0:T(8,128)(2,1)S(1)}, u32[]{:S(2)}, u32[]{:S(2)}) collective-permute-start(bf16[48,1280]{1,0:T(8,128)(2,1)S(1)} %collective-permute-done.7.refs_1_.refs_3_), channel_id=1, source_target_pairs={{0,1},{1,0},{2,3},{3,2},{4,5},{5,4},{6,7},{7,6},{8,9},{9,8},{10,11... | collective-permute-start | bytes 368648 | tf_op jit(solution)/shard_map/ppermute | solution.py:337
  30.3 3.6 %collective-permute-start.16 = (bf16[96,1280]{1,0:T(8,128)(2,1)S(1)}, bf16[96,1280]{1,0:T(8,128)(2,1)S(1)}, u32[]{:S(2)}, u32[]{:S(2)}) collective-permute-start(bf16[96,1280]{1,0:T(8,128)(2,1)S(1)} %slice.22), channel_id=1, source_target_pairs={{0,1},{1,0},{2,3},{3,2},{4,5},{5,4},{6,7},{7,6},{8,9},{9,8},{10,11... | collective-permute-start | bytes 737288 | tf_op jit(solution)/shard_map/ppermute | solution.py:337
  30.4 3.5 %collective-permute-start.13 = (bf16[96,1280]{1,0:T(8,128)(2,1)S(1)}, bf16[96,1280]{1,0:T(8,128)(2,1)S(1)}, u32[]{:S(2)}, u32[]{:S(2)}) collective-permute-start(bf16[96,1280]{1,0:T(8,128)(2,1)S(1)} %slice.20), channel_id=1, source_target_pairs={{0,1},{1,0},{2,3},{3,2},{4,5},{5,4},{6,7},{7,6},{8,9},{9,8},{10,11... | collective-permute-start | bytes 737288 | tf_op jit(solution)/shard_map/ppermute | solution.py:337
  30.9 3.0 %collective-permute-start.17 = (bf16[80,1280]{1,0:T(8,128)(2,1)S(1)}, bf16[80,1280]{1,0:T(8,128)(2,1)S(1)}, u32[]{:S(2)}, u32[]{:S(2)}) collective-permute-start(bf16[80,1280]{1,0:T(8,128)(2,1)S(1)} %slice.23), channel_id=1, source_target_pairs={{0,1},{1,0},{2,3},{3,2},{4,5},{5,4},{6,7},{7,6},{8,9},{9,8},{10,11... | collective-permute-start | bytes 614408 | tf_op jit(solution)/shard_map/ppermute | solution.py:337
  31.2 2.7 %collective-permute-start.14 = (bf16[80,1280]{1,0:T(8,128)(2,1)S(1)}, bf16[80,1280]{1,0:T(8,128)(2,1)S(1)}, u32[]{:S(2)}, u32[]{:S(2)}) collective-permute-start(bf16[80,1280]{1,0:T(8,128)(2,1)S(1)} %slice.21), channel_id=1, source_target_pairs={{0,1},{1,0},{2,3},{3,2},{4,5},{5,4},{6,7},{7,6},{8,9},{9,8},{10,11... | collective-permute-start | bytes 614408 | tf_op jit(solution)/shard_map/ppermute | solution.py:337
  38.6 2.3 %collective-permute-start.18 = (bf16[176,1280]{1,0:T(8,128)(2,1)S(1)}, bf16[176,1280]{1,0:T(8,128)(2,1)S(1)}, u32[]{:S(2)}, u32[]{:S(2)}) collective-permute-start(bf16[176,1280]{1,0:T(8,128)(2,1)S(1)} %collective-permute-done.2.refs_0_), channel_id=1, source_target_pairs={{0,1},{1,0},{2,3},{3,2},{4,5},{5,4},{6,7},{7,6},{8,9},{9,8},{10,11... | collective-permute-start | bytes 1351688 | tf_op jit(solution)/shard_map/ppermute | solution.py:337

commit v7 on v6

--- a/solution.py
+++ b/solution.py
@@ -256,35 +256,46 @@
         for g, (_, other, group) in enumerate(plan):
             for t in range(3):
                 write(before.at[g], 1 - other, group, t, sems.at[len(plan) + g, t])
-    for batch in batches_of(len(plan)):
+    inner = side - 2 * GROUP
+
+    def multiply(batch, lo, hi):
         pieces = [parts[ref][pl.ds(at, size), :] for g in batch for ref, at, size in plan[g][0]]
-        acc = (
-            lax.dot_general(
-                jnp.concatenate(pieces, axis=0), weight, (((1,), (1,)), ((), ())), preferred_element_type=F32
-            )
-            + bias
+        acc = lax.dot_general(
+            jnp.concatenate(pieces, axis=0), weight[lo:hi], (((1,), (1,)), ((), ())), preferred_element_type=F32
         )
-        inner = side - 2 * GROUP
+        acc = acc + bias[:, lo:hi]
         for n, g in enumerate(batch):
-            for k in range(0, total, LANES):
-                piece = acc[n * side : (n + 1) * side, k : k + LANES]
+            for k in range(lo, hi, LANES):
+                piece = acc[n * side : (n + 1) * side, k - lo : min(k + LANES, hi) - lo]
                 span = pl.ds(0, piece.shape[1])
                 sums[g, k // LANES, pl.ds(GROUP, inner), span] = piece[:inner]
                 sums[g, k // LANES, pl.ds(0, GROUP), span] = piece[inner : inner + GROUP]
                 sums[g, k // LANES, pl.ds(inner + GROUP, GROUP), span] = piece[inner + GROUP :]
-    for g, (_, other, group) in enumerate(plan):
-        for t in range(3):
-            for h in range(heads):
-                start = (t * heads + h) * HD
-                lo, hi = start // LANES, (start + HD - 1) // LANES + 1
-                cells = []
-                for j in range(GROUP):
-                    tiles = [sums[g, k, pl.ds(j, rows, stride=GROUP), :] for k in range(lo, hi)]
-                    cell = tiles[0] if len(tiles) == 1 else jnp.concatenate(tiles, axis=1)
-                    cells.append(cell[:, start - lo * LANES : start - lo * LANES + HD])
-                blocks[g, t, h] = jnp.concatenate(cells, axis=1).astype(BF16)
-            if mode != "blocks":
-                write(blocks.at[g], other, group, t, sems.at[g, t])
+
+    def lay_out(g, t):
+        for h in range(heads):
+            start = (t * heads + h) * HD
+            lo, hi = start // LANES, (start + HD - 1) // LANES + 1
+            cells = []
+            for j in range(GROUP):
+                tiles = [sums[g, k, pl.ds(j, rows, stride=GROUP), :] for k in range(lo, hi)]
+                cell = tiles[0] if len(tiles) == 1 else jnp.concatenate(tiles, axis=1)
+                cells.append(cell[:, start - lo * LANES : start - lo * LANES + HD])
+            blocks[g, t, h] = jnp.concatenate(cells, axis=1).astype(BF16)
+        if mode != "blocks":
+            write(blocks.at[g], plan[g][1], plan[g][2], t, sems.at[g, t])
+
+    half = min(4 * LANES, total) if len(plan) == 1 else total
+    ready = 0
+    for lo, hi in ((0, half), (half, total)):
+        if lo < hi:
+            for batch in batches_of(len(plan)):
+                multiply(batch, lo, hi)
+        complete = hi // (heads * HD)
+        for g in range(len(plan)):
+            for t in range(ready, complete):
+                lay_out(g, t)
+        ready = complete
     for copy in copies:
         copy.wait()
 

time: 43.4 us -> 43.4 us (level)
  no operation moved by 1% of the time
where the time goes in v7:
time: 43.4 us; the launch traced here: 42.6 us
  Pallas kernels  18.4 us (42%)
  starting transfers between devices  15 us (35%)
  waiting for transfers between devices  8.99 us (21%)
    pallas_call x4, Pallas kernels, project(): call(body, 'project', jax.ShapeDtypeStruct(shape, BF16), specs, HBM, [sum...  11.2 us
    ppermute x12, starting transfers between devices, swap(): return lax.ppermute(value, 'cols', [(q, q ^ 1) for q in range(side_count)])  7.31 us
    ppermute x5, waiting for transfers between devices, across(): lax.ppermute(value, 'cols', [(q, (q + 2 * step) % side_count) for q in ra...  7 us
    ppermute x2, starting transfers between devices, exchange(): return lax.ppermute(value, 'rows', pairs + [(j, i) for i, j in pairs])  4.44 us
    ppermute x5, starting transfers between devices, across(): lax.ppermute(value, 'cols', [(q, (q + 2 * step) % side_count) for q in ra...  3.23 us
    pallas_call x2, Pallas kernels, side(): call(functools.partial(side_kernel, last), 'side', array(half, width), [V...  2.48 us
    ppermute x12, waiting for transfers between devices, swap(): return lax.ppermute(value, 'cols', [(q, q ^ 1) for q in range(side_count)])  1.99 us
    pallas_call x1, Pallas kernels, local(): call(first_kernel, 'first', [array(rows, width), array(rows, cols, width)...  1.45 us
  transfers between devices with their start and end apart: 19, of which 7 were waited for; matrix products, arithmetic and copies ran while one was open for 0% of the time, Pallas kernels for 36%

profile of v7, /device:TPU:15, one launch (start us, length us, event | category | flops | bytes accessed | tf_op | source)
XLA Modules:
  0.0 42.6 jit_solution(16192175809822666771)
XLA Ops:
  0.0 1.4 %first.1 = (bf16[24,1280]{1,0:T(8,128)(2,1)S(1)}, bf16[24,24,1280]{2,1,0:T(8,128)(2,1)S(1)}, f32[3,3,1280]{2,1,0:T(4,128)S(1)}, f32[3,1,1280]{2,1,0:T(1,128)S(1)}) custom-call(bf16[24,24,1280]{2,1,0:T(8,128)(2,1)} %x_hbm.1, f32[3,3,1280]{2,1,0:T(4,128)} %taps_hbm.1, f32[1280]{0:T(1024)} %cbias_hbm.1, f32[1280]{0:T(1024)} %gain_hbm.1, f32[1280]{0:T(1024)} %nbias_hbm.1), custom_call_target="tpu_custom_call" | custom-call | flops 1024 | bytes 1024 | tf_op jit(solution)/shard_map/first/pallas_call | solution.py:361
  1.5 0.3 collective-permute-start
  1.8 1.4 %middle.1 = (bf16[176,1280]{1,0:T(8,128)(2,1)S(1)}, bf16[24,1280]{1,0:T(8,128)(2,1)S(1)}) custom-call(bf16[24,24,1280]{2,1,0:T(8,128)(2,1)S(1)} %get-tuple-element.21.x_ref, f32[3,3,1280]{2,1,0:T(4,128)S(1)} %get-tuple-element.22.taps_ref, f32[3,1,1280]{2,1,0:T(1,128)S(1)} %get-tuple-element.23.vec_ref), custom_call_target="tpu_custom_call" | custom-call | flops 1024 | bytes 1024 | tf_op jit(solution)/shard_map/middle/pallas_call | solution.py:376
  3.2 1.3 %collective-permute-start.4 = (bf16[176,1280]{1,0:T(8,128)(2,1)S(1)}, bf16[176,1280]{1,0:T(8,128)(2,1)S(1)}, u32[]{:S(2)}, u32[]{:S(2)}) collective-permute-start(bf16[176,1280]{1,0:T(8,128)(2,1)S(1)} %get-tuple-element.26.refs_2_), channel_id=1, source_target_pairs={{0,2},{1,3},{2,0},{3,1},{4,6},{5,7},{6,4},{7,5},{8,10},{9,11},{10,... | collective-permute-start | bytes 1351688 | tf_op jit(solution)/shard_map/ppermute | solution.py:343
  4.5 0.1 collective-permute-done.before_ref.behind_ref
  4.6 0.0 copy-start
  4.6 0.0 copy-start.1
  4.7 2.0 %collective-permute-start.1 = (bf16[48,1280]{1,0:T(8,128)(2,1)S(1)}, bf16[48,1280]{1,0:T(8,128)(2,1)S(1)}, u32[]{:S(2)}, u32[]{:S(2)}) collective-permute-start(bf16[48,1280]{1,0:T(8,128)(2,1)S(1)} %relay.1), channel_id=1, source_target_pairs={{0,1},{1,0},{2,3},{3,2},{4,5},{5,4},{6,7},{7,6},{8,9},{9,8},{10,11... | collective-permute-start | bytes 368648 | tf_op jit(solution)/shard_map/ppermute | solution.py:348
  6.6 0.1 collective-permute-start.10
  6.7 0.9 %collective-permute-done.1.sides_ref = bf16[48,1280]{1,0:T(8,128)(2,1)S(1)} collective-permute-done((bf16[48,1280]{1,0:T(8,128)(2,1)S(1)}, bf16[48,1280]{1,0:T(8,128)(2,1)S(1)}, u32[]{:S(2)}, u32[]{:S(2)}) %collective-permute-start.1) | collective-permute-done | bytes 122912 | tf_op jit(solution)/shard_map/ppermute | solution.py:348
  7.6 0.1 ends.1
  7.7 0.3 collective-permute-start.5
  8.0 4.1 %collective-permute-start.6 = (bf16[26,1280]{1,0:T(8,128)(2,1)S(1)}, bf16[26,1280]{1,0:T(8,128)(2,1)S(1)}, u32[]{:S(2)}, u32[]{:S(2)}) collective-permute-start(bf16[26,1280]{1,0:T(8,128)(2,1)S(1)} %get-tuple-element.28), channel_id=1, source_target_pairs={{4,8},{12,16},{20,24},{8,4},{16,12},{24,20},{5,9},{13,17},{21,25},... | collective-permute-start | bytes 199688 | tf_op jit(solution)/shard_map/ppermute | solution.py:352
  12.2 1.2 %side.3.refs_0_ = bf16[176,1280]{1,0:T(8,128)(2,1)S(1)} custom-call(bf16[24,24,1280]{2,1,0:T(8,128)(2,1)S(1)} %get-tuple-element.21.x_ref, bf16[48,1280]{1,0:T(8,128)(2,1)S(1)} %collective-permute-done.1.sides_ref, f32[3,3,1280]{2,1,0:T(4,128)S(1)} %get-tuple-element.22.taps_ref, f32[3,1,1280]{2,1,0:T(1,128)S(1)} %get-tuple-element.23.vec_ref), custom_call_target="tpu_custom_call" | custom-call | flops 1024 | bytes 1024 | tf_op jit(solution)/shard_map/side/pallas_call | solution.py:407
  13.4 1.0 %collective-permute-start.8 = (bf16[176,1280]{1,0:T(8,128)(2,1)S(1)}, bf16[176,1280]{1,0:T(8,128)(2,1)S(1)}, u32[]{:S(2)}, u32[]{:S(2)}) collective-permute-start(bf16[176,1280]{1,0:T(8,128)(2,1)S(1)} %side.3.refs_0_), channel_id=1, source_target_pairs={{0,1},{1,0},{2,3},{3,2},{4,5},{5,4},{6,7},{7,6},{8,9},{9,8},{10,11... | collective-permute-start | bytes 1351688 | tf_op jit(solution)/shard_map/ppermute | solution.py:348
  14.4 0.0 collective-permute-done.5.pair_ref
  14.4 0.2 collective-permute-start.3
  14.5 1.2 %side.2.refs_4_ = bf16[176,1280]{1,0:T(8,128)(2,1)S(1)} custom-call(bf16[24,24,1280]{2,1,0:T(8,128)(2,1)S(1)} %get-tuple-element.21.x_ref, bf16[48,1280]{1,0:T(8,128)(2,1)S(1)} %collective-permute-done.1.sides_ref, f32[3,3,1280]{2,1,0:T(4,128)S(1)} %get-tuple-element.22.taps_ref, f32[3,1,1280]{2,1,0:T(1,128)S(1)} %get-tuple-element.23.vec_ref), custom_call_target="tpu_custom_call" | custom-call | flops 1024 | bytes 1024 | tf_op jit(solution)/shard_map/side/pallas_call | solution.py:407
  15.8 0.0 collective-permute-done.6.cross_ref
  15.8 0.4 collective-permute-start.11
  16.3 0.0 collective-permute-done.4.refs_2_
  16.3 0.2 collective-permute-start.12
  16.5 0.7 %edges.1.refs_1_.refs_3_.refs_5_ = bf16[48,1280]{1,0:T(8,128)(2,1)S(1)} custom-call(bf16[24,24,1280]{2,1,0:T(8,128)(2,1)S(1)} %get-tuple-element.21.x_ref, bf16[48,1280]{1,0:T(8,128)(2,1)S(1)} %collective-permute-done.1.sides_ref, bf16[26,1280]{1,0:T(8,128)(2,1)S(1)} %collective-permute-done.5.pair_ref, ...), custom_call_target="tpu_custom_call" | custom-call | flops 1024 | bytes 1024 | tf_op jit(solution)/shard_map/edges/pallas_call | solution.py:419
  17.2 0.5 %collective-permute-done.12.refs_11_ = bf16[48,1280]{1,0:T(8,128)(2,1)S(1)} collective-permute-done((bf16[48,1280]{1,0:T(8,128)(2,1)S(1)}, bf16[48,1280]{1,0:T(8,128)(2,1)S(1)}, u32[]{:S(2)}, u32[]{:S(2)}) %collective-permute-start.12) | collective-permute-done | bytes 122912 | tf_op jit(solution)/shard_map/ppermute | solution.py:348
  17.7 0.4 collective-permute-start.9
  18.1 0.0 collective-permute-done.10.refs_8_
  18.1 1.3 %collective-permute-start.7 = (bf16[48,1280]{1,0:T(8,128)(2,1)S(1)}, bf16[48,1280]{1,0:T(8,128)(2,1)S(1)}, u32[]{:S(2)}, u32[]{:S(2)}) collective-permute-start(bf16[48,1280]{1,0:T(8,128)(2,1)S(1)} %edges.1.refs_1_.refs_3_.refs_5_), channel_id=1, source_target_pairs={{0,2},{1,3},{2,0},{3,1},{4,6},{5,7},{6,4},{7,5},{8,10},{9,11},{10,... | collective-permute-start | bytes 368648 | tf_op jit(solution)/shard_map/ppermute | solution.py:343
  19.4 0.0 collective-permute-done.11.refs_10_
  19.4 0.2 collective-permute-start.2
  19.5 0.0 collective-permute-done.9.refs_7_.refs_9_.refs_12_
  19.5 0.0 collective-permute-done.8.refs_6_
  19.5 0.0 copy-done
  19.6 0.0 copy-done.1
  19.6 4.9 %project.5.refs_6_ = bf16[3,4,24,7680]{3,2,1,0:T(8,128)(2,1)} custom-call(bf16[176,1280]{1,0:T(8,128)(2,1)S(1)} %side.3.refs_0_, bf16[48,1280]{1,0:T(8,128)(2,1)S(1)} %edges.1.refs_1_.refs_3_.refs_5_, bf16[176,1280]{1,0:T(8,128)(2,1)S(1)} %get-tuple-element.26.refs_2_, bf16[48,1280]{1,0:T(8,128)(2,1)S(1)} %edges.1.refs_1_.refs_3_.refs_5_, ...), custom_call_target="tpu_custom_call" | custom-call | flops 1024 | bytes 1024 | tf_op jit(solution)/shard_map/project/pallas_call | solution.py:318
  24.4 4.5 %collective-permute-done.7.refs_1_.refs_3_ = bf16[48,1280]{1,0:T(8,128)(2,1)S(1)} collective-permute-done((bf16[48,1280]{1,0:T(8,128)(2,1)S(1)}, bf16[48,1280]{1,0:T(8,128)(2,1)S(1)}, u32[]{:S(2)}, u32[]{:S(2)}) %collective-permute-start.7) | collective-permute-done | bytes 122912 | tf_op jit(solution)/shard_map/ppermute | solution.py:343
  28.9 0.0 collective-permute-done.3.refs_0_
  28.9 1.3 %collective-permute-start.15 = (bf16[48,1280]{1,0:T(8,128)(2,1)S(1)}, bf16[48,1280]{1,0:T(8,128)(2,1)S(1)}, u32[]{:S(2)}, u32[]{:S(2)}) collective-permute-start(bf16[48,1280]{1,0:T(8,128)(2,1)S(1)} %collective-permute-done.7.refs_1_.refs_3_), channel_id=1, source_target_pairs={{0,1},{1,0},{2,3},{3,2},{4,5},{5,4},{6,7},{7,6},{8,9},{9,8},{10,11... | collective-permute-start | bytes 368648 | tf_op jit(solution)/shard_map/ppermute | solution.py:348
  30.3 0.1 collective-permute-start.16
  30.4 0.5 %collective-permute-start.13 = (bf16[96,1280]{1,0:T(8,128)(2,1)S(1)}, bf16[96,1280]{1,0:T(8,128)(2,1)S(1)}, u32[]{:S(2)}, u32[]{:S(2)}) collective-permute-start(bf16[96,1280]{1,0:T(8,128)(2,1)S(1)} %slice.20), channel_id=1, source_target_pairs={{0,1},{1,0},{2,3},{3,2},{4,5},{5,4},{6,7},{7,6},{8,9},{9,8},{10,11... | collective-permute-start | bytes 737288 | tf_op jit(solution)/shard_map/ppermute | solution.py:348
  30.9 0.1 collective-permute-start.17
  31.1 0.2 collective-permute-done.15.refs_2_.refs_5_.refs_1_
  31.2 0.4 collective-permute-start.14
  31.6 2.3 %project.6.refs_8_ = bf16[3,4,24,7680]{3,2,1,0:T(8,128)(2,1)} custom-call(bf16[176,1280]{1,0:T(8,128)(2,1)S(1)} %collective-permute-done.3.refs_0_, bf16[48,1280]{1,0:T(8,128)(2,1)S(1)} %collective-permute-done.7.refs_1_.refs_3_, bf16[176,1280]{1,0:T(8,128)(2,1)S(1)} %collective-permute-done.4.refs_2_, ...), custom_call_target="tpu_custom_call", output_to_operand_aliasing={{}: (6, {})} | custom-call | flops 1024 | bytes 1024 | tf_op jit(solution)/shard_map/project/pallas_call | solution.py:318
  33.9 0.0 collective-permute-done.17.refs_4_
  33.9 0.0 collective-permute-done.14.refs_1_
  33.9 0.0 collective-permute-done.16.refs_3_
  33.9 0.0 collective-permute-done.13.refs_0_
  33.9 2.3 %project.7.refs_5_ = bf16[3,4,24,7680]{3,2,1,0:T(8,128)(2,1)} custom-call(bf16[96,1280]{1,0:T(8,128)(2,1)S(1)} %collective-permute-done.13.refs_0_, bf16[80,1280]{1,0:T(8,128)(2,1)S(1)} %collective-permute-done.14.refs_1_, bf16[48,1280]{1,0:T(8,128)(2,1)S(1)} %collective-permute-done.15.refs_2_.refs_5_.refs_1_, ...), custom_call_target="tpu_custom_call", output_to_operand_aliasing={{}: (8, {})} | custom-call | flops 1024 | bytes 1024 | tf_op jit(solution)/shard_map/project/pallas_call | solution.py:318
  36.2 2.4 %collective-permute-done.2.refs_0_ = bf16[176,1280]{1,0:T(8,128)(2,1)S(1)} collective-permute-done((bf16[176,1280]{1,0:T(8,128)(2,1)S(1)}, bf16[176,1280]{1,0:T(8,128)(2,1)S(1)}, u32[]{:S(2)}, u32[]{:S(2)}) %collective-permute-start.2) | collective-permute-done | bytes 450592 | tf_op jit(solution)/shard_map/ppermute | solution.py:343
  38.6 0.9 %collective-permute-start.18 = (bf16[176,1280]{1,0:T(8,128)(2,1)S(1)}, bf16[176,1280]{1,0:T(8,128)(2,1)S(1)}, u32[]{:S(2)}, u32[]{:S(2)}) collective-permute-start(bf16[176,1280]{1,0:T(8,128)(2,1)S(1)} %collective-permute-done.2.refs_0_), channel_id=1, source_target_pairs={{0,1},{1,0},{2,3},{3,2},{4,5},{5,4},{6,7},{7,6},{8,9},{9,8},{10,11... | collective-permute-start | bytes 1351688 | tf_op jit(solution)/shard_map/ppermute | solution.py:348
  39.4 1.1 %project.8.refs_4_ = bf16[1,3,4,24,640]{4,3,2,1,0:T(8,128)(2,1)S(1)} custom-call(bf16[176,1280]{1,0:T(8,128)(2,1)S(1)} %collective-permute-done.2.refs_0_, bf16[48,1280]{1,0:T(8,128)(2,1)S(1)} %collective-permute-done.7.refs_1_.refs_3_, bf16[3,320,1280]{2,1,0:T(8,128)(2,1)S(1)} %bitcast.4, bf16[3,320]{1,0:T(4,128)(2,1)S(1)} %copy-done.1), custom_call_target="tpu_custom_call" | custom-call | flops 1024 | bytes 1024 | tf_op jit(solution)/shard_map/project/pallas_call | solution.py:317
  40.5 0.4 collective-permute-done.18.refs_0_
  40.9 1.8 %project.9 = bf16[3,4,24,7680]{3,2,1,0:T(8,128)(2,1)} custom-call(bf16[176,1280]{1,0:T(8,128)(2,1)S(1)} %collective-permute-done.18.refs_0_, bf16[48,1280]{1,0:T(8,128)(2,1)S(1)} %collective-permute-done.15.refs_2_.refs_5_.refs_1_, bf16[3,320,1280]{2,1,0:T(8,128)(2,1)S(1)} %bitcast.5, bf16[3,320]{1,0:T(4,128)(2,1)S(1)} %copy-done.1, ...), custom_call_target="tpu_custom_call", output_to_operand_aliasing={{}: (5, {})} | custom-call | flops 1024 | bytes 1024 | tf_op jit(solution)/shard_map/project/pallas_call | solution.py:318
  (7 shorter events, 0.1 us)
Async XLA Ops:
  1.5 3.1 %collective-permute-start = (bf16[24,1280]{1,0:T(8,128)(2,1)S(1)}, bf16[24,1280]{1,0:T(8,128)(2,1)S(1)}, u32[]{:S(2)}, u32[]{:S(2)}) collective-permute-start(bf16[24,1280]{1,0:T(8,128)(2,1)S(1)} %get-tuple-element.25), channel_id=1, source_target_pairs={{0,2},{1,3},{2,0},{3,1},{4,6},{5,7},{6,4},{7,5},{8,10},{9,11},{10,... | collective-permute-start | bytes 184328 | tf_op jit(solution)/shard_map/ppermute | solution.py:343
  3.2 13.1 %collective-permute-start.4 = (bf16[176,1280]{1,0:T(8,128)(2,1)S(1)}, bf16[176,1280]{1,0:T(8,128)(2,1)S(1)}, u32[]{:S(2)}, u32[]{:S(2)}) collective-permute-start(bf16[176,1280]{1,0:T(8,128)(2,1)S(1)} %get-tuple-element.26.refs_2_), channel_id=1, source_target_pairs={{0,2},{1,3},{2,0},{3,1},{4,6},{5,7},{6,4},{7,5},{8,10},{9,11},{10,... | collective-permute-start | bytes 1351688 | tf_op jit(solution)/shard_map/ppermute | solution.py:343
  4.6 14.9 %copy-start = (bf16[3,1280,320]{1,2,0:T(8,128)(2,1)S(1)}, bf16[3,1280,320]{1,2,0:T(8,128)(2,1)}, u32[]{:S(2)}) copy-start(bf16[3,1280,320]{1,2,0:T(8,128)(2,1)} %param.12) | copy-start | bytes 7372804
  4.6 14.9 %copy-start.1 = (bf16[3,320]{1,0:T(4,128)(2,1)S(1)}, bf16[3,320]{1,0:T(4,128)(2,1)}, u32[]{:S(2)}) copy-start(bf16[3,320]{1,0:T(4,128)(2,1)} %refs_3_.3) | copy-start | bytes 5764
  4.7 3.0 %collective-permute-start.1 = (bf16[48,1280]{1,0:T(8,128)(2,1)S(1)}, bf16[48,1280]{1,0:T(8,128)(2,1)S(1)}, u32[]{:S(2)}, u32[]{:S(2)}) collective-permute-start(bf16[48,1280]{1,0:T(8,128)(2,1)S(1)} %relay.1), channel_id=1, source_target_pairs={{0,1},{1,0},{2,3},{3,2},{4,5},{5,4},{6,7},{7,6},{8,9},{9,8},{10,11... | collective-permute-start | bytes 368648 | tf_op jit(solution)/shard_map/ppermute | solution.py:348
  6.6 11.4 %collective-permute-start.10 = (bf16[176,1280]{1,0:T(8,128)(2,1)S(1)}, bf16[176,1280]{1,0:T(8,128)(2,1)S(1)}, u32[]{:S(2)}, u32[]{:S(2)}) collective-permute-start(bf16[176,1280]{1,0:T(8,128)(2,1)S(1)} %get-tuple-element.26.refs_2_), channel_id=1, source_target_pairs={{0,1},{1,0},{2,3},{3,2},{4,5},{5,4},{6,7},{7,6},{8,9},{9,8},{10,11... | collective-permute-start | bytes 1351688 | tf_op jit(solution)/shard_map/ppermute | solution.py:348
  7.7 6.7 %collective-permute-start.5 = (bf16[26,1280]{1,0:T(8,128)(2,1)S(1)}, bf16[26,1280]{1,0:T(8,128)(2,1)S(1)}, u32[]{:S(2)}, u32[]{:S(2)}) collective-permute-start(bf16[26,1280]{1,0:T(8,128)(2,1)S(1)} %get-tuple-element.27), channel_id=1, source_target_pairs={{0,4},{8,12},{16,20},{24,28},{4,0},{12,8},{20,16},{28,24},{1,5},{9... | collective-permute-start | bytes 199688 | tf_op jit(solution)/shard_map/ppermute | solution.py:352
  8.0 7.8 %collective-permute-start.6 = (bf16[26,1280]{1,0:T(8,128)(2,1)S(1)}, bf16[26,1280]{1,0:T(8,128)(2,1)S(1)}, u32[]{:S(2)}, u32[]{:S(2)}) collective-permute-start(bf16[26,1280]{1,0:T(8,128)(2,1)S(1)} %get-tuple-element.28), channel_id=1, source_target_pairs={{4,8},{12,16},{20,24},{8,4},{16,12},{24,20},{5,9},{13,17},{21,25},... | collective-permute-start | bytes 199688 | tf_op jit(solution)/shard_map/ppermute | solution.py:352
  13.4 6.2 %collective-permute-start.8 = (bf16[176,1280]{1,0:T(8,128)(2,1)S(1)}, bf16[176,1280]{1,0:T(8,128)(2,1)S(1)}, u32[]{:S(2)}, u32[]{:S(2)}) collective-permute-start(bf16[176,1280]{1,0:T(8,128)(2,1)S(1)} %side.3.refs_0_), channel_id=1, source_target_pairs={{0,1},{1,0},{2,3},{3,2},{4,5},{5,4},{6,7},{7,6},{8,9},{9,8},{10,11... | collective-permute-start | bytes 1351688 | tf_op jit(solution)/shard_map/ppermute | solution.py:348
  14.4 14.5 %collective-permute-start.3 = (bf16[176,1280]{1,0:T(8,128)(2,1)S(1)}, bf16[176,1280]{1,0:T(8,128)(2,1)S(1)}, u32[]{:S(2)}, u32[]{:S(2)}) collective-permute-start(bf16[176,1280]{1,0:T(8,128)(2,1)S(1)} %side.3.refs_0_), channel_id=1, source_target_pairs={{0,2},{1,3},{2,0},{3,1},{4,6},{5,7},{6,4},{7,5},{8,10},{9,11},{10,... | collective-permute-start | bytes 1351688 | tf_op jit(solution)/shard_map/ppermute | solution.py:343
  15.8 3.5 %collective-permute-start.11 = (bf16[128,1280]{1,0:T(8,128)(2,1)S(1)}, bf16[128,1280]{1,0:T(8,128)(2,1)S(1)}, u32[]{:S(2)}, u32[]{:S(2)}) collective-permute-start(bf16[128,1280]{1,0:T(8,128)(2,1)S(1)} %slice.24), channel_id=1, source_target_pairs={{0,1},{1,0},{2,3},{3,2},{4,5},{5,4},{6,7},{7,6},{8,9},{9,8},{10,11... | collective-permute-start | bytes 983048 | tf_op jit(solution)/shard_map/ppermute | solution.py:348
  16.3 1.4 %collective-permute-start.12 = (bf16[48,1280]{1,0:T(8,128)(2,1)S(1)}, bf16[48,1280]{1,0:T(8,128)(2,1)S(1)}, u32[]{:S(2)}, u32[]{:S(2)}) collective-permute-start(bf16[48,1280]{1,0:T(8,128)(2,1)S(1)} %slice.25), channel_id=1, source_target_pairs={{0,1},{1,0},{2,3},{3,2},{4,5},{5,4},{6,7},{7,6},{8,9},{9,8},{10,11... | collective-permute-start | bytes 368648 | tf_op jit(solution)/shard_map/ppermute | solution.py:348
  17.7 1.8 %collective-permute-start.9 = (bf16[48,1280]{1,0:T(8,128)(2,1)S(1)}, bf16[48,1280]{1,0:T(8,128)(2,1)S(1)}, u32[]{:S(2)}, u32[]{:S(2)}) collective-permute-start(bf16[48,1280]{1,0:T(8,128)(2,1)S(1)} %edges.1.refs_1_.refs_3_.refs_5_), channel_id=1, source_target_pairs={{0,1},{1,0},{2,3},{3,2},{4,5},{5,4},{6,7},{7,6},{8,9},{9,8},{10,11... | collective-permute-start | bytes 368648 | tf_op jit(solution)/shard_map/ppermute | solution.py:348
  18.1 10.9 %collective-permute-start.7 = (bf16[48,1280]{1,0:T(8,128)(2,1)S(1)}, bf16[48,1280]{1,0:T(8,128)(2,1)S(1)}, u32[]{:S(2)}, u32[]{:S(2)}) collective-permute-start(bf16[48,1280]{1,0:T(8,128)(2,1)S(1)} %edges.1.refs_1_.refs_3_.refs_5_), channel_id=1, source_target_pairs={{0,2},{1,3},{2,0},{3,1},{4,6},{5,7},{6,4},{7,5},{8,10},{9,11},{10,... | collective-permute-start | bytes 368648 | tf_op jit(solution)/shard_map/ppermute | solution.py:343
  19.4 19.2 %collective-permute-start.2 = (bf16[176,1280]{1,0:T(8,128)(2,1)S(1)}, bf16[176,1280]{1,0:T(8,128)(2,1)S(1)}, u32[]{:S(2)}, u32[]{:S(2)}) collective-permute-start(bf16[176,1280]{1,0:T(8,128)(2,1)S(1)} %side.2.refs_4_), channel_id=1, source_target_pairs={{0,2},{1,3},{2,0},{3,1},{4,6},{5,7},{6,4},{7,5},{8,10},{9,11},{10,... | collective-permute-start | bytes 1351688 | tf_op jit(solution)/shard_map/ppermute | solution.py:343
  28.9 2.3 %collective-permute-start.15 = (bf16[48,1280]{1,0:T(8,128)(2,1)S(1)}, bf16[48,1280]{1,0:T(8,128)(2,1)S(1)}, u32[]{:S(2)}, u32[]{:S(2)}) collective-permute-start(bf16[48,1280]{1,0:T(8,128)(2,1)S(1)} %collective-permute-done.7.refs_1_.refs_3_), channel_id=1, source_target_pairs={{0,1},{1,0},{2,3},{3,2},{4,5},{5,4},{6,7},{7,6},{8,9},{9,8},{10,11... | collective-permute-start | bytes 368648 | tf_op jit(solution)/shard_map/ppermute | solution.py:348
  30.3 3.6 %collective-permute-start.16 = (bf16[96,1280]{1,0:T(8,128)(2,1)S(1)}, bf16[96,1280]{1,0:T(8,128)(2,1)S(1)}, u32[]{:S(2)}, u32[]{:S(2)}) collective-permute-start(bf16[96,1280]{1,0:T(8,128)(2,1)S(1)} %slice.22), channel_id=1, source_target_pairs={{0,1},{1,0},{2,3},{3,2},{4,5},{5,4},{6,7},{7,6},{8,9},{9,8},{10,11... | collective-permute-start | bytes 737288 | tf_op jit(solution)/shard_map/ppermute | solution.py:348
  30.4 3.5 %collective-permute-start.13 = (bf16[96,1280]{1,0:T(8,128)(2,1)S(1)}, bf16[96,1280]{1,0:T(8,128)(2,1)S(1)}, u32[]{:S(2)}, u32[]{:S(2)}) collective-permute-start(bf16[96,1280]{1,0:T(8,128)(2,1)S(1)} %slice.20), channel_id=1, source_target_pairs={{0,1},{1,0},{2,3},{3,2},{4,5},{5,4},{6,7},{7,6},{8,9},{9,8},{10,11... | collective-permute-start | bytes 737288 | tf_op jit(solution)/shard_map/ppermute | solution.py:348
  30.9 3.0 %collective-permute-start.17 = (bf16[80,1280]{1,0:T(8,128)(2,1)S(1)}, bf16[80,1280]{1,0:T(8,128)(2,1)S(1)}, u32[]{:S(2)}, u32[]{:S(2)}) collective-permute-start(bf16[80,1280]{1,0:T(8,128)(2,1)S(1)} %slice.23), channel_id=1, source_target_pairs={{0,1},{1,0},{2,3},{3,2},{4,5},{5,4},{6,7},{7,6},{8,9},{9,8},{10,11... | collective-permute-start | bytes 614408 | tf_op jit(solution)/shard_map/ppermute | solution.py:348
  31.2 2.7 %collective-permute-start.14 = (bf16[80,1280]{1,0:T(8,128)(2,1)S(1)}, bf16[80,1280]{1,0:T(8,128)(2,1)S(1)}, u32[]{:S(2)}, u32[]{:S(2)}) collective-permute-start(bf16[80,1280]{1,0:T(8,128)(2,1)S(1)} %slice.21), channel_id=1, source_target_pairs={{0,1},{1,0},{2,3},{3,2},{4,5},{5,4},{6,7},{7,6},{8,9},{9,8},{10,11... | collective-permute-start | bytes 614408 | tf_op jit(solution)/shard_map/ppermute | solution.py:348
  38.6 2.3 %collective-permute-start.18 = (bf16[176,1280]{1,0:T(8,128)(2,1)S(1)}, bf16[176,1280]{1,0:T(8,128)(2,1)S(1)}, u32[]{:S(2)}, u32[]{:S(2)}) collective-permute-start(bf16[176,1280]{1,0:T(8,128)(2,1)S(1)} %collective-permute-done.2.refs_0_), channel_id=1, source_target_pairs={{0,1},{1,0},{2,3},{3,2},{4,5},{5,4},{6,7},{7,6},{8,9},{9,8},{10,11... | collective-permute-start | bytes 1351688 | tf_op jit(solution)/shard_map/ppermute | solution.py:348
